TPU v7x, 32 devices: a whole 2x2x4 slice. The times are simulated.
32 devices in a mesh: wide: 16 (over z, y, x), narrow: 2 (over core).
Axes of the slice: x: 2, y: 2, z: 4, core: 2. Of those that a mesh axis runs over, the one named last changes fastest.
Arguments:
- inputs: bfloat16 [393216, 256], P(('wide', 'narrow')), may hold values from -6 to 6
- input_segments: int32 [393216], P(('wide', 'narrow')), may hold values from 0 to 3, as said below
- latent_segments: int32 [196608], P(('wide', 'narrow')), may hold values from 0 to 3, as said below
- cotangent: bfloat16 [196608, 512], P(('wide', 'narrow')), may hold values from -6 to 6
- latent_array: bfloat16 [1024, 512], P('wide', 'narrow'), may hold values from -6 to 6
- query_gain: bfloat16 [512], replicated, may hold values from 0.25 to 1.75
- query_shift: bfloat16 [512], replicated, may hold values from -1.796875 to 1.796875
- source_gain: bfloat16 [256], replicated, may hold values from 0.25 to 1.75
- source_shift: bfloat16 [256], replicated, may hold values from -1.796875 to 1.796875
- cross_query: bfloat16 [512, 512], P('wide', 'narrow'), may hold values from -0.25 to 0.25
- cross_qbias: bfloat16 [512], replicated, may hold values from -1.796875 to 1.796875
- cross_keyval: bfloat16 [256, 1024], P('wide', 'narrow'), may hold values from -0.375 to 0.375
- cross_vbias: bfloat16 [512], replicated, may hold values from -1.796875 to 1.796875
- cross_output: bfloat16 [512, 512], P('wide', 'narrow'), may hold values from -1.5 to 1.5
- cross_obias: bfloat16 [512], replicated, may hold values from -1.796875 to 1.796875
- self_gain: bfloat16 [512], replicated, may hold values from 0.25 to 1.75
- self_shift: bfloat16 [512], replicated, may hold values from -1.796875 to 1.796875
- self_project: bfloat16 [512, 1536], P('wide', 'narrow'), may hold values from -0.25 to 0.25
- self_qbias: bfloat16 [512], replicated, may hold values from -1.796875 to 1.796875
- self_vbias: bfloat16 [512], replicated, may hold values from -1.796875 to 1.796875
- self_output: bfloat16 [512, 512], P('wide', 'narrow'), may hold values from -1 to 1
- self_obias: bfloat16 [512], replicated, may hold values from -1.796875 to 1.796875
- feed_gain: bfloat16 [512], replicated, may hold values from 0.25 to 1.75
- feed_shift: bfloat16 [512], replicated, may hold values from -1.796875 to 1.796875
- feed_upward: bfloat16 [512, 2048], P('wide', 'narrow'), may hold values from -0.25 to 0.25
- feed_ubias: bfloat16 [2048], replicated, may hold values from -1.796875 to 1.796875
- feed_downward: bfloat16 [2048, 512], P('wide', 'narrow'), may hold values from -0.125 to 0.125
- feed_dbias: bfloat16 [512], replicated, may hold values from -1.796875 to 1.796875
Outputs:
- latents_out: bfloat16 [196608, 512], P(('wide', 'narrow'))
- inputs_grad: float32 [393216, 256], P(('wide', 'narrow'))
- latent_array_grad: float32 [1024, 512], P('wide', 'narrow')
- query_gain_grad: float32 [512], replicated
- query_shift_grad: float32 [512], replicated
- source_gain_grad: float32 [256], replicated
- source_shift_grad: float32 [256], replicated
- cross_query_grad: float32 [512, 512], P('wide', 'narrow')
- cross_qbias_grad: float32 [512], replicated
- cross_keyval_grad: float32 [256, 1024], P('wide', 'narrow')
- cross_vbias_grad: float32 [512], replicated
- cross_output_grad: float32 [512, 512], P('wide', 'narrow')
- cross_obias_grad: float32 [512], replicated
- self_gain_grad: float32 [512], replicated
- self_shift_grad: float32 [512], replicated
- self_project_grad: float32 [512, 1536], P('wide', 'narrow')
- self_qbias_grad: float32 [512], replicated
- self_vbias_grad: float32 [512], replicated
- self_output_grad: float32 [512, 512], P('wide', 'narrow')
- self_obias_grad: float32 [512], replicated
- feed_gain_grad: float32 [512], replicated
- feed_shift_grad: float32 [512], replicated
- feed_upward_grad: float32 [512, 2048], P('wide', 'narrow')
- feed_ubias_grad: float32 [2048], replicated
- feed_downward_grad: float32 [2048, 512], P('wide', 'narrow')
- feed_dbias_grad: float32 [512], replicated
Inputs may be any that keep to these rules, and one draw needn't show every extreme that they name: `input_segments`: within each aligned group of 512 input tokens the ids start at 0, never fall, and every id of 0 to 3 occurs. `latent_segments`: within each aligned group of 256 latent rows the ids start at 0, never fall, and every id of 0 to 3 occurs.
All inputs are finite; a program needn't handle non-finite values.
Results may differ from a plain program's by a relative error of at most 0.023.
Values may be sent and summed in bfloat16 or wider, within the bound.
No kernel may reach another device: no remote copies, remote signals or barrier semaphores. Data moves between devices by JAX's collectives and lax.ppermute only.
A program may use at most 448 MiB of HBM per device.

v0:
```python
import math

import jax
import jax.numpy as jnp
from jax import lax
from jax.sharding import PartitionSpec as P

D = 512
HEADS = 16
HD = 32
CIN = 256
G = 4
NL = 256
IN_G = 512
SAMP_DEV = 2
MICRO = 3


NEG_FILL = -1e30
EPSILON = 1e-05


def gelu_exact(values_in):
    return 0.5 * values_in * (1.0 + jax.scipy.special.erf(values_in * 0.5**0.5))


def dot_plain(left, right):
    return jnp.dot(left, right, preferred_element_type=jnp.float32)


def dot_first(left, right):
    return lax.dot_general(
        left, right, (((0,), (0,)), ((), ())), preferred_element_type=jnp.float32
    )


def dot_last(left, right):
    return lax.dot_general(
        left, right, (((1,), (1,)), ((), ())), preferred_element_type=jnp.float32
    )


def layer_norm(source_rows, gain_vec, shift_vec):
    centered = source_rows - jnp.mean(source_rows, -1, keepdims=True)
    rscale = lax.rsqrt(jnp.mean(centered * centered, -1, keepdims=True) + EPSILON)
    normed = centered * rscale
    return (normed * gain_vec.astype(jnp.float32) + shift_vec.astype(jnp.float32), normed, rscale)


def norm_back(grad_rows, normed, rscale, gain_vec):
    dnormed = grad_rows * gain_vec.astype(jnp.float32)
    inner_term = (
        dnormed
        - jnp.mean(dnormed, -1, keepdims=True)
        - normed * jnp.mean(dnormed * normed, -1, keepdims=True)
    )
    return (rscale * inner_term, jnp.sum(grad_rows * normed, 0), jnp.sum(grad_rows, 0))


def block_scores(queries, key_rows, query_seg, key_seg):
    groups = queries.shape[0]
    qheads = queries.reshape(groups, queries.shape[1], HEADS, HD)
    kheads = key_rows.reshape(groups, key_rows.shape[1], HEADS, HD)
    scores = jnp.einsum(
        "gqhd,gkhd->ghqk", qheads, kheads, preferred_element_type=jnp.float32
    ) * HD ** (-0.5)
    allowed = query_seg[:, None, :, None] == key_seg[:, None, None, :]
    return (jnp.where(allowed, scores, NEG_FILL), qheads, kheads)


def attend_forward(block_args):
    queries, key_rows, values, query_seg, key_seg = block_args
    groups = queries.shape[0]
    scores, qheads, kheads = block_scores(queries, key_rows, query_seg, key_seg)
    row_max = jnp.max(scores, -1, keepdims=True)
    powers = jnp.exp(scores - row_max)
    total = jnp.sum(powers, -1, keepdims=True)
    attn_probs = (powers / total).astype(jnp.bfloat16)
    vheads = values.reshape(groups, values.shape[1], HEADS, HD)
    blended = jnp.einsum("ghqk,gkhd->gqhd", attn_probs, vheads, preferred_element_type=jnp.float32)
    log_total = (row_max + jnp.log(total))[..., 0]
    return (blended.reshape(groups, queries.shape[1], D).astype(jnp.bfloat16), log_total)


def attend_backward(block_args):
    queries, key_rows, values, query_seg, key_seg, log_total, out_grad = block_args
    groups = queries.shape[0]
    scores, qheads, kheads = block_scores(queries, key_rows, query_seg, key_seg)
    attn_probs = jnp.exp(scores - log_total[..., None])
    vheads = values.reshape(groups, values.shape[1], HEADS, HD)
    gheads = out_grad.reshape(groups, out_grad.shape[1], HEADS, HD)
    dprobs = jnp.einsum("gqhd,gkhd->ghqk", gheads, vheads, preferred_element_type=jnp.float32)
    delta = jnp.sum(attn_probs * dprobs, -1, keepdims=True)
    dscores = (attn_probs * (dprobs - delta)).astype(jnp.bfloat16)
    scale = HD ** (-0.5)
    dquery = (
        jnp.einsum("ghqk,gkhd->gqhd", dscores, kheads, preferred_element_type=jnp.float32) * scale
    )
    dkey = (
        jnp.einsum("ghqk,gqhd->gkhd", dscores, qheads, preferred_element_type=jnp.float32) * scale
    )
    dvalue = jnp.einsum(
        "ghqk,gqhd->gkhd",
        attn_probs.astype(jnp.bfloat16),
        gheads,
        preferred_element_type=jnp.float32,
    )
    return (
        dquery.reshape(groups, queries.shape[1], D),
        dkey.reshape(groups, key_rows.shape[1], D),
        dvalue.reshape(groups, key_rows.shape[1], D),
    )


def blocked(function, arrays, per_block):
    block_count = arrays[0].shape[0] // per_block
    pieces = tuple((item.reshape((block_count, per_block) + item.shape[1:]) for item in arrays))
    results = lax.map(function, pieces)
    return tuple((item.reshape((block_count * per_block,) + item.shape[2:]) for item in results))


def gather_cross(mats):
    columns = (
        lax.all_gather(mats[0], "narrow", axis=1, tiled=True),
        lax.all_gather(mats[1], "narrow", axis=1, tiled=True),
        lax.all_gather(mats[2], "narrow", axis=1, tiled=True),
        lax.all_gather(mats[3], "narrow", axis=1, tiled=True),
    )
    return tuple(
        (
            lax.all_gather(columns[0], "wide", axis=0, tiled=True),
            lax.all_gather(columns[1], "wide", axis=0, tiled=True),
            lax.all_gather(columns[2], "wide", axis=0, tiled=True),
            lax.all_gather(columns[3], "wide", axis=0, tiled=True),
        )
    )


def gather_self(mats):
    columns = (
        lax.all_gather(mats[0], "narrow", axis=1, tiled=True),
        lax.all_gather(mats[1], "narrow", axis=1, tiled=True),
    )
    return tuple(
        (
            lax.all_gather(columns[0], "wide", axis=0, tiled=True),
            lax.all_gather(columns[1], "wide", axis=0, tiled=True),
        )
    )


def gather_feed(mats):
    columns = (
        lax.all_gather(mats[0], "narrow", axis=1, tiled=True),
        lax.all_gather(mats[1], "narrow", axis=1, tiled=True),
    )
    return tuple(
        (
            lax.all_gather(columns[0], "wide", axis=0, tiled=True),
            lax.all_gather(columns[1], "wide", axis=0, tiled=True),
        )
    )


def scatter_all(grads):
    cp, sp, fp = grads
    cross_rows = (
        lax.psum_scatter(
            cp[0].astype(jnp.bfloat16), "wide", scatter_dimension=0, tiled=True
        ).astype(jnp.float32),
        lax.psum_scatter(
            cp[5].astype(jnp.bfloat16), "wide", scatter_dimension=0, tiled=True
        ).astype(jnp.float32),
        lax.psum_scatter(
            cp[7].astype(jnp.bfloat16), "wide", scatter_dimension=0, tiled=True
        ).astype(jnp.float32),
        lax.psum_scatter(
            cp[9].astype(jnp.bfloat16), "wide", scatter_dimension=0, tiled=True
        ).astype(jnp.float32),
    )
    cross_mats = (
        lax.psum_scatter(
            cross_rows[0].astype(jnp.bfloat16), "narrow", scatter_dimension=1, tiled=True
        ).astype(jnp.float32),
        lax.psum_scatter(
            cross_rows[1].astype(jnp.bfloat16), "narrow", scatter_dimension=1, tiled=True
        ).astype(jnp.float32),
        lax.psum_scatter(
            cross_rows[2].astype(jnp.bfloat16), "narrow", scatter_dimension=1, tiled=True
        ).astype(jnp.float32),
        lax.psum_scatter(
            cross_rows[3].astype(jnp.bfloat16), "narrow", scatter_dimension=1, tiled=True
        ).astype(jnp.float32),
    )
    self_rows = (
        lax.psum_scatter(
            sp[2].astype(jnp.bfloat16), "wide", scatter_dimension=0, tiled=True
        ).astype(jnp.float32),
        lax.psum_scatter(
            sp[5].astype(jnp.bfloat16), "wide", scatter_dimension=0, tiled=True
        ).astype(jnp.float32),
    )
    self_mats = (
        lax.psum_scatter(
            self_rows[0].astype(jnp.bfloat16), "narrow", scatter_dimension=1, tiled=True
        ).astype(jnp.float32),
        lax.psum_scatter(
            self_rows[1].astype(jnp.bfloat16), "narrow", scatter_dimension=1, tiled=True
        ).astype(jnp.float32),
    )
    feed_rows = (
        lax.psum_scatter(
            fp[2].astype(jnp.bfloat16), "wide", scatter_dimension=0, tiled=True
        ).astype(jnp.float32),
        lax.psum_scatter(
            fp[4].astype(jnp.bfloat16), "wide", scatter_dimension=0, tiled=True
        ).astype(jnp.float32),
    )
    feed_mats = (
        lax.psum_scatter(
            feed_rows[0].astype(jnp.bfloat16), "narrow", scatter_dimension=1, tiled=True
        ).astype(jnp.float32),
        lax.psum_scatter(
            feed_rows[1].astype(jnp.bfloat16), "narrow", scatter_dimension=1, tiled=True
        ).astype(jnp.float32),
    )
    small = lax.psum(
        (
            cp[1],
            cp[2],
            cp[3],
            cp[4],
            cp[6],
            cp[8],
            cp[10],
            sp[0],
            sp[1],
            sp[3],
            sp[4],
            sp[6],
            fp[0],
            fp[1],
            fp[3],
            fp[5],
        ),
        ("wide", "narrow"),
    )
    cross_sums = (
        cross_mats[0],
        small[0],
        small[1],
        small[2],
        small[3],
        cross_mats[1],
        small[4],
        cross_mats[2],
        small[5],
        cross_mats[3],
        small[6],
    )
    self_sums = (small[7], small[8], self_mats[0], small[9], small[10], self_mats[1], small[11])
    feed_sums = (small[12], small[13], feed_mats[0], small[14], feed_mats[1], small[15])
    return (cross_sums, self_sums, feed_sums)


def forward_pass(inputs, in_segs, lat_segs, cross_full, self_full, feed_full):
    (
        latent_full,
        query_gain,
        query_shift,
        source_gain,
        source_shift,
        cross_query,
        cross_qbias,
        cross_keyval,
        cross_vbias,
        cross_output,
        cross_obias,
    ) = cross_full
    self_gain, self_shift, self_project, self_qbias, self_vbias, self_output, self_obias = self_full
    feed_gain, feed_shift, feed_upward, feed_ubias, feed_downward, feed_dbias = feed_full
    groups = SAMP_DEV * G
    per_block = math.gcd(groups, max(1, 512 // NL))
    lat_segs = lat_segs.reshape(groups, NL)
    in_segs = in_segs.reshape(groups, IN_G)
    lat_rows = latent_full.astype(jnp.float32)
    lat_norm, lat_hat, lat_scale = layer_norm(lat_rows, query_gain, query_shift)
    lat_low = lat_norm.astype(jnp.bfloat16)
    query_rows = (dot_plain(lat_low, cross_query) + cross_qbias.astype(jnp.float32)).astype(
        jnp.bfloat16
    )
    query_all = jnp.tile(query_rows.reshape(G, NL, D), (SAMP_DEV, 1, 1))
    src_norm, src_hat, src_scale = layer_norm(inputs.astype(jnp.float32), source_gain, source_shift)
    src_low = src_norm.astype(jnp.bfloat16)
    kv_bias = jnp.concatenate([jnp.zeros((D,), jnp.float32), cross_vbias.astype(jnp.float32)])
    keyval = (
        (dot_plain(src_low, cross_keyval) + kv_bias)
        .astype(jnp.bfloat16)
        .reshape(groups, IN_G, 2 * D)
    )
    key_rows = keyval[:, :, :D]
    value_rows = keyval[:, :, D:]
    cross_mix, cross_lse = blocked(
        attend_forward, (query_all, key_rows, value_rows, lat_segs, in_segs), per_block
    )
    cross_mix = cross_mix.reshape(groups * NL, D)
    after_cross = (
        jnp.tile(lat_rows, (SAMP_DEV, 1))
        + dot_plain(cross_mix, cross_output)
        + cross_obias.astype(jnp.float32)
    )
    mid_norm, mid_hat, mid_scale = layer_norm(after_cross, self_gain, self_shift)
    mid_low = mid_norm.astype(jnp.bfloat16)
    proj_bias = jnp.concatenate(
        [
            self_qbias.astype(jnp.float32),
            jnp.zeros((D,), jnp.float32),
            self_vbias.astype(jnp.float32),
        ]
    )
    triple = (
        (dot_plain(mid_low, self_project) + proj_bias)
        .astype(jnp.bfloat16)
        .reshape(groups, NL, 3 * D)
    )
    self_query = triple[:, :, :D]
    self_key = triple[:, :, D : 2 * D]
    self_value = triple[:, :, 2 * D :]
    self_mix, self_lse = blocked(
        attend_forward, (self_query, self_key, self_value, lat_segs, lat_segs), per_block
    )
    self_mix = self_mix.reshape(groups * NL, D)
    after_self = after_cross + dot_plain(self_mix, self_output) + self_obias.astype(jnp.float32)
    top_norm, top_hat, top_scale = layer_norm(after_self, feed_gain, feed_shift)
    top_low = top_norm.astype(jnp.bfloat16)
    hidden = dot_plain(top_low, feed_upward) + feed_ubias.astype(jnp.float32)
    active = gelu_exact(hidden).astype(jnp.bfloat16)
    result = (
        after_self + dot_plain(active, feed_downward) + feed_dbias.astype(jnp.float32)
    ).astype(jnp.bfloat16)
    saved = {
        "lat_low": lat_low,
        "lat_hat": lat_hat,
        "lat_scale": lat_scale,
        "query_all": query_all,
        "src_low": src_low,
        "src_hat": src_hat,
        "src_scale": src_scale,
        "key_rows": key_rows,
        "value_rows": value_rows,
        "cross_mix": cross_mix,
        "cross_lse": cross_lse,
        "mid_low": mid_low,
        "mid_hat": mid_hat,
        "mid_scale": mid_scale,
        "self_query": self_query,
        "self_key": self_key,
        "self_value": self_value,
        "self_mix": self_mix,
        "self_lse": self_lse,
        "top_low": top_low,
        "top_hat": top_hat,
        "top_scale": top_scale,
        "hidden": hidden,
        "active": active,
        "lat_segs": lat_segs,
        "in_segs": in_segs,
    }
    return (result, saved)


def backward_pass(saved, cotangent, cross_full, self_full, feed_full):
    (
        latent_full,
        query_gain,
        query_shift,
        source_gain,
        source_shift,
        cross_query,
        cross_qbias,
        cross_keyval,
        cross_vbias,
        cross_output,
        cross_obias,
    ) = cross_full
    self_gain, self_shift, self_project, self_qbias, self_vbias, self_output, self_obias = self_full
    feed_gain, feed_shift, feed_upward, feed_ubias, feed_downward, feed_dbias = feed_full
    groups = SAMP_DEV * G
    per_block = math.gcd(groups, max(1, 512 // NL))
    dfinal = cotangent.astype(jnp.float32)
    g_down = dot_first(saved["active"], cotangent)
    g_dbias = jnp.sum(dfinal, 0)
    dactive = dot_last(cotangent, feed_downward)
    dhidden = jax.vjp(gelu_exact, saved["hidden"])[1](dactive)[0].astype(jnp.bfloat16)
    g_upward = dot_first(saved["top_low"], dhidden)
    g_ubias = jnp.sum(dhidden.astype(jnp.float32), 0)
    dtop = dot_last(dhidden, feed_upward)
    dself_ln, g_fgain, g_fshift = norm_back(dtop, saved["top_hat"], saved["top_scale"], feed_gain)
    dafter_self = dfinal + dself_ln
    dself_out = dafter_self.astype(jnp.bfloat16)
    g_soutput = dot_first(saved["self_mix"], dself_out)
    g_sobias = jnp.sum(dself_out.astype(jnp.float32), 0)
    dself_mix = dot_last(dself_out, self_output).astype(jnp.bfloat16).reshape(groups, NL, D)
    self_dq, self_dk, self_dv = blocked(
        attend_backward,
        (
            saved["self_query"],
            saved["self_key"],
            saved["self_value"],
            saved["lat_segs"],
            saved["lat_segs"],
            saved["self_lse"],
            dself_mix,
        ),
        per_block,
    )
    dtriple = (
        jnp.concatenate([self_dq, self_dk, self_dv], -1)
        .reshape(groups * NL, 3 * D)
        .astype(jnp.bfloat16)
    )
    g_project = dot_first(saved["mid_low"], dtriple)
    g_sqbias = jnp.sum(dtriple[:, :D].astype(jnp.float32), 0)
    g_svbias = jnp.sum(dtriple[:, 2 * D :].astype(jnp.float32), 0)
    dmid = dot_last(dtriple, self_project)
    dcross_ln, g_sgain, g_sshift = norm_back(dmid, saved["mid_hat"], saved["mid_scale"], self_gain)
    dafter_cross = dafter_self + dcross_ln
    dcross_out = dafter_cross.astype(jnp.bfloat16)
    g_coutput = dot_first(saved["cross_mix"], dcross_out)
    g_cobias = jnp.sum(dcross_out.astype(jnp.float32), 0)
    dcross_mix = dot_last(dcross_out, cross_output).astype(jnp.bfloat16).reshape(groups, NL, D)
    cross_dq, cross_dk, cross_dv = blocked(
        attend_backward,
        (
            saved["query_all"],
            saved["key_rows"],
            saved["value_rows"],
            saved["lat_segs"],
            saved["in_segs"],
            saved["cross_lse"],
            dcross_mix,
        ),
        per_block,
    )
    dquery = jnp.sum(cross_dq.reshape(SAMP_DEV, G * NL, D), 0).astype(jnp.bfloat16)
    g_query = dot_first(saved["lat_low"], dquery)
    g_qbias = jnp.sum(dquery.astype(jnp.float32), 0)
    dlat_norm = dot_last(dquery, cross_query)
    dlat_ln, g_qgain, g_qshift = norm_back(
        dlat_norm, saved["lat_hat"], saved["lat_scale"], query_gain
    )
    g_latent = jnp.sum(dafter_cross.reshape(SAMP_DEV, G * NL, D), 0) + dlat_ln
    dkeyval = (
        jnp.concatenate([cross_dk, cross_dv], -1).reshape(groups * IN_G, 2 * D).astype(jnp.bfloat16)
    )
    g_keyval = dot_first(saved["src_low"], dkeyval)
    g_vbias = jnp.sum(dkeyval[:, D:].astype(jnp.float32), 0)
    dsource = dot_last(dkeyval, cross_keyval)
    dinput, g_srcgain, g_srcshift = norm_back(
        dsource, saved["src_hat"], saved["src_scale"], source_gain
    )
    cross_part = (
        g_latent,
        g_qgain,
        g_qshift,
        g_srcgain,
        g_srcshift,
        g_query,
        g_qbias,
        g_keyval,
        g_vbias,
        g_coutput,
        g_cobias,
    )
    self_part = (g_sgain, g_sshift, g_project, g_sqbias, g_svbias, g_soutput, g_sobias)
    feed_part = (g_fgain, g_fshift, g_upward, g_ubias, g_down, g_dbias)
    return (dinput, (cross_part, self_part, feed_part))


def assemble(cross_mats, self_mats, feed_mats, small_cross, small_self, small_feed):
    cross_full = (
        cross_mats[0],
        small_cross[0],
        small_cross[1],
        small_cross[2],
        small_cross[3],
        cross_mats[1],
        small_cross[4],
        cross_mats[2],
        small_cross[5],
        cross_mats[3],
        small_cross[6],
    )
    self_full = (
        small_self[0],
        small_self[1],
        self_mats[0],
        small_self[2],
        small_self[3],
        self_mats[1],
        small_self[4],
    )
    feed_full = (
        small_feed[0],
        small_feed[1],
        feed_mats[0],
        small_feed[2],
        feed_mats[1],
        small_feed[3],
    )
    return (cross_full, self_full, feed_full)


def local(
    inputs,
    input_segments,
    latent_segments,
    cotangent,
    latent_array,
    query_gain,
    query_shift,
    source_gain,
    source_shift,
    cross_query,
    cross_qbias,
    cross_keyval,
    cross_vbias,
    cross_output,
    cross_obias,
    self_gain,
    self_shift,
    self_project,
    self_qbias,
    self_vbias,
    self_output,
    self_obias,
    feed_gain,
    feed_shift,
    feed_upward,
    feed_ubias,
    feed_downward,
    feed_dbias,
):
    cross_local = (latent_array, cross_query, cross_keyval, cross_output)
    self_local = (self_project, self_output)
    feed_local = (feed_upward, feed_downward)
    small_cross = (
        query_gain,
        query_shift,
        source_gain,
        source_shift,
        cross_qbias,
        cross_vbias,
        cross_obias,
    )
    small_self = (self_gain, self_shift, self_qbias, self_vbias, self_obias)
    small_feed = (feed_gain, feed_shift, feed_ubias, feed_dbias)
    input_parts = inputs.reshape(MICRO, -1, CIN)
    in_seg_parts = input_segments.reshape(MICRO, -1)
    lat_seg_parts = latent_segments.reshape(MICRO, -1)
    cot_parts = cotangent.reshape(MICRO, -1, D)
    latent_outs = []
    input_grads = []
    totals = None
    for micro_index in range(MICRO):
        cross_mats = gather_cross(cross_local)
        self_mats = gather_self(self_local)
        feed_mats = gather_feed(feed_local)
        cross_full, self_full, feed_full = assemble(
            cross_mats, self_mats, feed_mats, small_cross, small_self, small_feed
        )
        latent_out, saved = forward_pass(
            input_parts[micro_index],
            in_seg_parts[micro_index],
            lat_seg_parts[micro_index],
            cross_full,
            self_full,
            feed_full,
        )
        feed_mats = gather_feed(feed_local)
        self_mats = gather_self(self_local)
        cross_mats = gather_cross(cross_local)
        cross_full, self_full, feed_full = assemble(
            cross_mats, self_mats, feed_mats, small_cross, small_self, small_feed
        )
        input_grad, micro_grads = backward_pass(
            saved, cot_parts[micro_index], cross_full, self_full, feed_full
        )
        latent_outs.append(latent_out)
        input_grads.append(input_grad)
        micro_grads = scatter_all(micro_grads)
        totals = micro_grads if totals is None else jax.tree.map(jnp.add, totals, micro_grads)
    return (
        (jnp.concatenate(latent_outs, 0), jnp.concatenate(input_grads, 0))
        + tuple(totals[0])
        + tuple(totals[1])
        + tuple(totals[2])
    )


def solution(mesh):
    placed = (
        P(("wide", "narrow"), None),
        P(("wide", "narrow")),
        P(("wide", "narrow")),
        P(("wide", "narrow"), None),
        P("wide", "narrow"),
        P(),
        P(),
        P(),
        P(),
        P("wide", "narrow"),
        P(),
        P("wide", "narrow"),
        P(),
        P("wide", "narrow"),
        P(),
        P(),
        P(),
        P("wide", "narrow"),
        P(),
        P(),
        P("wide", "narrow"),
        P(),
        P(),
        P(),
        P("wide", "narrow"),
        P(),
        P("wide", "narrow"),
        P(),
    )
    return jax.shard_map(
        local,
        mesh=mesh,
        in_specs=placed,
        out_specs=(
            P(("wide", "narrow"), None),
            P(("wide", "narrow"), None),
            P("wide", "narrow"),
            P(),
            P(),
            P(),
            P(),
            P("wide", "narrow"),
            P(),
            P("wide", "narrow"),
            P(),
            P("wide", "narrow"),
            P(),
            P(),
            P(),
            P("wide", "narrow"),
            P(),
            P(),
            P("wide", "narrow"),
            P(),
            P(),
            P(),
            P("wide", "narrow"),
            P(),
            P("wide", "narrow"),
            P(),
        ),
        check_vma=False,
    )
```

profile of v0, /device:TPU:0, one launch (start us, length us, event | category | flops | bytes accessed | tf_op | source)
XLA Modules:
  0.0 3973.6 jit_solution(3632969716460804683)
XLA Ops:
  34.7 46.3 %all_gather.37 = bf16[512,512]{1,0:T(8,128)(2,1)S(1)} all-gather(bf16[32,512]{1,0:T(8,128)(2,1)S(1)} %all_gather.36), channel_id=1, replica_groups=mesh['wide'=16,'narrow'=2] {'wide'}, dimensions={0}, use_global_device_ids=true | all-gather | bytes 557056 | tf_op jit(solution)/shard_map/all_gather | solution.py:132
  93.5 39.5 all_gather.35
  156.0 45.7 %all_gather.39 = bf16[512,512]{1,0:T(8,128)(2,1)} all-gather(bf16[32,512]{1,0:T(8,128)(2,1)S(1)} %all_gather.38), channel_id=1, replica_groups=mesh['wide'=16,'narrow'=2] {'wide'}, dimensions={0}, use_global_device_ids=true | all-gather | bytes 557056 | tf_op jit(solution)/shard_map/all_gather | solution.py:134
  205.3 42.5 %all_gather.43 = bf16[512,512]{1,0:T(8,128)(2,1)} all-gather(bf16[32,512]{1,0:T(8,128)(2,1)S(1)} %all_gather.42), channel_id=1, replica_groups=mesh['wide'=16,'narrow'=2] {'wide'}, dimensions={0}, use_global_device_ids=true | all-gather | bytes 557056 | tf_op jit(solution)/shard_map/all_gather | solution.py:147
  302.3 75.1 %while.162 = (s32[]{:T(128)}, bf16[4,2,256,512]{3,2,1,0:T(8,128)(2,1)}, f32[4,2,16,256]{3,2,1,0:T(8,128)S(1)}, bf16[4,2,512,512]{2,3,1,0:T(8,128)(2,1)}, s32[4,2...) while((s32[]{:T(128)}, ...), condition=%wide.region_7.8_spmd, body=%wide.region_4.7_spmd.sunk | while | flops 587718656 | bytes 62147184 | solution.py:118
  385.8 80.6 %while.164 = (s32[]{:T(128)}, bf16[4,2,256,512]{3,2,1,0:T(8,128)(2,1)}, f32[4,2,16,256]{3,2,1,0:T(8,128)S(1)}, bf16[4,2,512,512]{2,3,1,0:T(8,128)(2,1)}, s32[4,2...) while((s32[]{:T(128)}, ...), condition=%wide.region_21.22_spmd, body=%wide.region_18.21_spmd.sunk | while | flops 587718656 | bytes 62147184 | solution.py:118
  475.0 80.8 %while.166 = (s32[]{:T(128)}, bf16[4,2,256,512]{3,2,1,0:T(8,128)(2,1)}, f32[4,2,16,256]{3,2,1,0:T(8,128)S(1)}, bf16[4,2,512,512]{2,3,1,0:T(8,128)(2,1)}, s32[4,2...) while((s32[]{:T(128)}, ...), condition=%wide.region_35.36_spmd, body=%wide.region_32.35_spmd.sunk | while | flops 587718656 | bytes 62147184 | solution.py:118
  583.7 46.4 %while.163 = (s32[]{:T(128)}, bf16[4,2,256,512]{3,2,1,0:T(8,128)(2,1)}, f32[4,2,16,256]{3,2,1,0:T(8,128)S(1)}, bf16[4,2,256,512]{2,3,1,0:T(8,128)(2,1)}, s32[4,2...) while((s32[]{:T(128)}, ...), condition=%wide.region_13.14_spmd, body=%wide.region_10.13_spmd.sunk | while | flops 293986304 | bytes 33299044 | solution.py:118
  656.1 46.5 %while.165 = (s32[]{:T(128)}, bf16[4,2,256,512]{3,2,1,0:T(8,128)(2,1)}, f32[4,2,16,256]{3,2,1,0:T(8,128)S(1)}, bf16[4,2,256,512]{2,3,1,0:T(8,128)(2,1)}, s32[4,2...) while((s32[]{:T(128)}, ...), condition=%wide.region_27.28_spmd, body=%wide.region_24.27_spmd.sunk | while | flops 293986304 | bytes 33299044 | solution.py:118
  726.9 46.8 %while.167 = (s32[]{:T(128)}, bf16[4,2,256,512]{3,2,1,0:T(8,128)(2,1)}, f32[4,2,16,256]{3,2,1,0:T(8,128)S(1)}, bf16[4,2,256,512]{2,3,1,0:T(8,128)(2,1)}, s32[4,2...) while((s32[]{:T(128)}, ...), condition=%wide.region_41.42_spmd, body=%wide.region_38.41_spmd.sunk | while | flops 293986304 | bytes 33299044 | solution.py:118
  783.9 13.4 fusion.178
  805.6 16.9 convert_reduce_fusion.1
  822.5 18.1 convert_reduce_fusion
  840.7 19.8 multiply_convert_fusion.8
  860.5 15.8 convert_reduce_fusion.2
  892.6 15.8 multiply_reduce_fusion.8
  929.2 163.6 %while.168 = (s32[]{:T(128)}, bf16[4,2,256,512]{3,2,1,0:T(8,128)(2,1)S(1)}, bf16[4,2,256,512]{3,2,1,0:T(8,128)(2,1)}, bf16[4,2,256,512]{3,2,1,0:T(8,128)(2,1)}, ...) while((s32[]{:T(128)}, ...), condition=%wide.region_48.49_spmd, body=%wide.region_46.48_spmd.sunk | while | flops 703717376 | bytes 122395344 | solution.py:118
  1103.9 131.9 %while.170 = (s32[]{:T(128)}, bf16[4,2,256,512]{3,2,1,0:T(8,128)(2,1)}, bf16[4,2,256,512]{3,2,1,0:T(8,128)(2,1)}, bf16[4,2,256,512]{3,2,1,0:T(8,128)(2,1)}, bf16...) while((s32[]{:T(128)}, ...), condition=%wide.region_60.61_spmd, body=%wide.region_58.60_spmd.sunk | while | flops 703717376 | bytes 122395848 | solution.py:118
  1240.6 166.6 %while.172 = (s32[]{:T(128)}, bf16[4,2,256,512]{3,2,1,0:T(8,128)(2,1)}, bf16[4,2,256,512]{3,2,1,0:T(8,128)(2,1)}, bf16[4,2,256,512]{3,2,1,0:T(8,128)(2,1)}, bf16...) while((s32[]{:T(128)}, ...), condition=%wide.region_72.73_spmd, body=%wide.region_70.72_spmd.sunk | while | flops 703717376 | bytes 122395848 | solution.py:118
  1425.5 12.7 convert_reduce_fusion.23
  1476.8 261.9 %while.169 = (s32[]{:T(128)}, f32[4,2,256,512]{3,2,1,0:T(8,128)}, bf16[4,2,512,512]{3,2,1,0:T(8,128)(2,1)}, bf16[4,2,512,512]{3,2,1,0:T(8,128)(2,1)}, bf16[4,2,5...) while((s32[]{:T(128)}, f32[4,2,256,512]{3,2,1,0:T(8,128)}, ...), condition=%wide.region_53.54_spmd, body=%wide.region_51.53_spmd.sunk | while | flops 1406656512 | bytes 191089872 | solution.py:118
  1492.6 14.2 multiply_reduce_fusion.50
  1506.7 12.1 multiply_convert_fusion.16
  1558.0 14.2 multiply_reduce_fusion.50
  1572.2 12.1 multiply_convert_fusion.16
  1623.5 14.2 multiply_reduce_fusion.50
  1637.7 12.1 multiply_convert_fusion.16
  1688.9 14.2 multiply_reduce_fusion.50
  1703.1 12.1 multiply_convert_fusion.16
  1753.0 261.3 %while.171 = (s32[]{:T(128)}, f32[4,2,256,512]{3,2,1,0:T(8,128)}, bf16[4,2,512,512]{3,2,1,0:T(8,128)(2,1)}, bf16[4,2,512,512]{3,2,1,0:T(8,128)(2,1)}, bf16[4,2,5...) while((s32[]{:T(128)}, f32[4,2,256,512]{3,2,1,0:T(8,128)}, ...), condition=%wide.region_65.66_spmd, body=%wide.region_63.65_spmd.sunk | while | flops 1406656512 | bytes 191089872 | solution.py:118
  1768.9 14.2 multiply_reduce_fusion.52
  1783.1 12.1 multiply_convert_fusion.18
  1834.2 14.2 multiply_reduce_fusion.52
  1848.4 12.0 multiply_convert_fusion.18
  1899.5 14.2 multiply_reduce_fusion.52
  1913.7 12.0 multiply_convert_fusion.18
  1964.8 14.2 multiply_reduce_fusion.52
  1979.0 12.0 multiply_convert_fusion.18
  2042.4 261.5 %while.173 = (s32[]{:T(128)}, f32[4,2,256,512]{3,2,1,0:T(8,128)}, bf16[4,2,512,512]{3,2,1,0:T(8,128)(2,1)}, bf16[4,2,512,512]{3,2,1,0:T(8,128)(2,1)}, bf16[4,2,5...) while((s32[]{:T(128)}, f32[4,2,256,512]{3,2,1,0:T(8,128)}, ...), condition=%wide.region_77.78_spmd, body=%wide.region_75.77_spmd.sunk | while | flops 1406656512 | bytes 191089872 | solution.py:118
  2058.2 14.2 multiply_reduce_fusion.54
  2072.4 12.1 multiply_convert_fusion.20
  2123.6 14.2 multiply_reduce_fusion.54
  2137.8 12.1 multiply_convert_fusion.20
  2189.0 14.2 multiply_reduce_fusion.54
  2203.2 12.0 multiply_convert_fusion.20
  2254.3 14.2 multiply_reduce_fusion.54
  2462.2 13.5 fusion.107
  2492.3 45.3 %reduce-scatter.65.cloned.1.call-done = bf16[32,512]{1,0:T(8,128)(2,1)} async-done(((bf16[512,512]{1,0:T(8,128)(2,1)}), bf16[32,512]{1,0:T(8,128)(2,1)}) %reduce-scatter.65.cloned.1.call-update) | async-done | bytes 32784 | tf_op jit(solution)/shard_map/reduce_scatter | solution.py:171
  2539.5 73.1 %reduce-scatter.61.cloned.1.call-done = bf16[32,512]{1,0:T(8,128)(2,1)} async-done(((bf16[512,512]{1,0:T(8,128)(2,1)}), bf16[32,512]{1,0:T(8,128)(2,1)}) %reduce-scatter.61.cloned.1.call-update) | async-done | bytes 32784 | tf_op jit(solution)/shard_map/reduce_scatter | solution.py:171
  2614.9 74.2 %reduce-scatter.49.cloned.1.call-done = bf16[64,512]{1,0:T(8,128)(2,1)} async-done(((bf16[1024,512]{1,0:T(8,128)(2,1)}), bf16[64,512]{1,0:T(8,128)(2,1)}) %reduce-scatter.49.cloned.1.call-update) | async-done | bytes 65552 | tf_op jit(solution)/shard_map/reduce_scatter | solution.py:168
  2689.6 75.8 %reduce-scatter.53.cloned.1.call-done = bf16[64,512]{1,0:T(8,128)(2,1)} async-done(((bf16[1024,512]{1,0:T(8,128)(2,1)}), bf16[64,512]{1,0:T(8,128)(2,1)}) %reduce-scatter.53.cloned.1.call-update) | async-done | bytes 65552 | tf_op jit(solution)/shard_map/reduce_scatter | solution.py:168
  2766.9 74.9 %reduce-scatter.57.cloned.1.call-done = bf16[64,512]{1,0:T(8,128)(2,1)} async-done(((bf16[1024,512]{1,0:T(8,128)(2,1)}), bf16[64,512]{1,0:T(8,128)(2,1)}) %reduce-scatter.57.cloned.1.call-update) | async-done | bytes 65552 | tf_op jit(solution)/shard_map/reduce_scatter | solution.py:168
  2869.2 18.0 pad_maximum_fusion.4
  2894.8 12.8 pad_maximum_fusion
  2907.6 60.4 %reduce-scatter.97.cloned.1.call-done = bf16[32,1536]{1,0:T(8,128)(2,1)} async-done(((bf16[512,1536]{1,0:T(8,128)(2,1)}), bf16[32,1536]{1,0:T(8,128)(2,1)}) %reduce-scatter.97.cloned.1.call-update) | async-done | bytes 98320 | tf_op jit(solution)/shard_map/reduce_scatter | solution.py:196
  2968.1 129.0 %reduce-scatter.101.cloned.1.call-done = bf16[32,1536]{1,0:T(8,128)(2,1)} async-done(((bf16[512,1536]{1,0:T(8,128)(2,1)}), bf16[32,1536]{1,0:T(8,128)(2,1)}) %reduce-scatter.101.cloned.1.call-update) | async-done | bytes 98320 | tf_op jit(solution)/shard_map/reduce_scatter | solution.py:196
  3097.2 129.0 %reduce-scatter.105.cloned.1.call-done = bf16[32,1536]{1,0:T(8,128)(2,1)} async-done(((bf16[512,1536]{1,0:T(8,128)(2,1)}), bf16[32,1536]{1,0:T(8,128)(2,1)}) %reduce-scatter.105.cloned.1.call-update) | async-done | bytes 98320 | tf_op jit(solution)/shard_map/reduce_scatter | solution.py:196
  3226.3 81.8 %reduce-scatter.133.cloned.1.call-done = bf16[128,512]{1,0:T(8,128)(2,1)} async-done(((bf16[2048,512]{1,0:T(8,128)(2,1)}), bf16[128,512]{1,0:T(8,128)(2,1)}) %reduce-scatter.133.cloned.1.call-update) | async-done | bytes 131088 | tf_op jit(solution)/shard_map/reduce_scatter | solution.py:215
  3308.2 79.7 %reduce-scatter.137.cloned.1.call-done = bf16[128,512]{1,0:T(8,128)(2,1)} async-done(((bf16[2048,512]{1,0:T(8,128)(2,1)}), bf16[128,512]{1,0:T(8,128)(2,1)}) %reduce-scatter.137.cloned.1.call-update) | async-done | bytes 131088 | tf_op jit(solution)/shard_map/reduce_scatter | solution.py:215
  3388.0 79.9 %reduce-scatter.141.cloned.1.call-done = bf16[128,512]{1,0:T(8,128)(2,1)} async-done(((bf16[2048,512]{1,0:T(8,128)(2,1)}), bf16[128,512]{1,0:T(8,128)(2,1)}) %reduce-scatter.141.cloned.1.call-update) | async-done | bytes 131088 | tf_op jit(solution)/shard_map/reduce_scatter | solution.py:215
  3468.0 38.2 all-reduce.1
  3507.6 73.2 %reduce-scatter.121.cloned.1.call-done = bf16[32,2048]{1,0:T(8,128)(2,1)} async-done(((bf16[512,2048]{1,0:T(8,128)(2,1)}), bf16[32,2048]{1,0:T(8,128)(2,1)}) %reduce-scatter.121.cloned.1.call-update) | async-done | bytes 131088 | tf_op jit(solution)/shard_map/reduce_scatter | solution.py:212
  3643.3 82.9 %reduce-scatter.125.cloned.1.call-done = bf16[32,2048]{1,0:T(8,128)(2,1)} async-done(((bf16[512,2048]{1,0:T(8,128)(2,1)}), bf16[32,2048]{1,0:T(8,128)(2,1)}) %reduce-scatter.125.cloned.1.call-update) | async-done | bytes 131088 | tf_op jit(solution)/shard_map/reduce_scatter | solution.py:212
  3788.5 82.9 %reduce-scatter.129.cloned.1.call-done = bf16[32,2048]{1,0:T(8,128)(2,1)} async-done(((bf16[512,2048]{1,0:T(8,128)(2,1)}), bf16[32,2048]{1,0:T(8,128)(2,1)}) %reduce-scatter.129.cloned.1.call-update) | async-done | bytes 131088 | tf_op jit(solution)/shard_map/reduce_scatter | solution.py:212
  (1658 shorter events, 2135.9 us)
Async XLA Ops:
  7.2 287.7 %all-gather.5.cloned.1.call-start = ((), (), s32[]{:S(2)}) async-start(), calls=%async_computation.48 | async-start | bytes 1114112 | tf_op jit(solution)/shard_map/all_gather | solution.py:131
  11.0 552.7 %all-gather.7.cloned.1.call-start = ((), (), s32[]{:S(2)}) async-start(), calls=%async_computation.49 | async-start | bytes 1671168 | tf_op jit(solution)/shard_map/all_gather | solution.py:146
  14.5 769.3 %all-gather.9.cloned.1.call-start = ((), (), s32[]{:S(2)}) async-start(), calls=%async_computation.50 | async-start | bytes 2228224 | tf_op jit(solution)/shard_map/all_gather | solution.py:159
  18.3 787.3 %all-gather.11.cloned.1.call-start = ((), (), s32[]{:S(2)}) async-start(), calls=%async_computation.51 | async-start | bytes 2228224 | tf_op jit(solution)/shard_map/all_gather | solution.py:160
  21.9 2396.0 %reduce-scatter.109.cloned.1.call-start = ((), (), s32[]{:S(2)}) async-start(), calls=%async_computation.82 | async-start | bytes 557056 | tf_op jit(solution)/shard_map/reduce_scatter | solution.py:199
  773.7 319.1 %copy-start.106 = (f32[2048]{0:T(1024)}, f32[2048]{0:T(1024)S(1)}, u32[]{:S(2)}) copy-start(f32[2048]{0:T(1024)S(1)} %broadcast_multiply_fusion.23) | copy-start | bytes 24580
  777.5 315.3 %copy-start.133 = (f32[2048]{0:T(1024)}, f32[2048]{0:T(1024)S(1)}, u32[]{:S(2)}) copy-start(f32[2048]{0:T(1024)S(1)} %add_rsqrt_fusion.5) | copy-start | bytes 24580
  929.1 1489.3 %reduce-scatter.113.cloned.1.call-start = ((), (), s32[]{:S(2)}) async-start(), calls=%async_computation.84 | async-start | bytes 557056 | tf_op jit(solution)/shard_map/reduce_scatter | solution.py:199
  1442.1 976.9 %reduce-scatter.117.cloned.1.call-start = ((), (), s32[]{:S(2)}) async-start(), calls=%async_computation.86 | async-start | bytes 557056 | tf_op jit(solution)/shard_map/reduce_scatter | solution.py:199
  1446.5 984.2 %reduce-scatter.89.cloned.1.call-start = ((), (), s32[]{:S(2)}) async-start(), calls=%async_computation.72 | async-start | bytes 557056 | tf_op jit(solution)/shard_map/reduce_scatter | solution.py:177
  1462.3 969.0 %reduce-scatter.93.cloned.1.call-start = ((), (), s32[]{:S(2)}) async-start(), calls=%async_computation.74 | async-start | bytes 557056 | tf_op jit(solution)/shard_map/reduce_scatter | solution.py:177
  1469.6 962.5 %reduce-scatter.85.cloned.1.call-start = ((), (), s32[]{:S(2)}) async-start(), calls=%async_computation.70 | async-start | bytes 557056 | tf_op jit(solution)/shard_map/reduce_scatter | solution.py:177
  1745.9 698.2 %reduce-scatter.73.cloned.1.call-start = ((), (), s32[]{:S(2)}) async-start(), calls=%async_computation.64 | async-start | bytes 557056 | tf_op jit(solution)/shard_map/reduce_scatter | solution.py:174
  2023.1 428.9 %reduce-scatter.77.cloned.1.call-start = ((), (), s32[]{:S(2)}) async-start(), calls=%async_computation.66 | async-start | bytes 557056 | tf_op jit(solution)/shard_map/reduce_scatter | solution.py:174
  2035.2 424.7 %reduce-scatter.81.cloned.1.call-start = ((), (), s32[]{:S(2)}) async-start(), calls=%async_computation.68 | async-start | bytes 557056 | tf_op jit(solution)/shard_map/reduce_scatter | solution.py:174
  2312.4 177.8 %reduce-scatter.69.cloned.1.call-start = ((), (), s32[]{:S(2)}) async-start(), calls=%async_computation.62 | async-start | bytes 557056 | tf_op jit(solution)/shard_map/reduce_scatter | solution.py:171
  2317.3 220.2 %reduce-scatter.65.cloned.1.call-start = ((), (), s32[]{:S(2)}) async-start(), calls=%async_computation.60 | async-start | bytes 557056 | tf_op jit(solution)/shard_map/reduce_scatter | solution.py:171
  2331.5 281.1 %reduce-scatter.61.cloned.1.call-start = ((), (), s32[]{:S(2)}) async-start(), calls=%async_computation.58 | async-start | bytes 557056 | tf_op jit(solution)/shard_map/reduce_scatter | solution.py:171
  2339.6 349.4 %reduce-scatter.49.cloned.1.call-start = ((), (), s32[]{:S(2)}) async-start(), calls=%async_computation.52 | async-start | bytes 1114112 | tf_op jit(solution)/shard_map/reduce_scatter | solution.py:168
  2359.6 405.7 %reduce-scatter.53.cloned.1.call-start = ((), (), s32[]{:S(2)}) async-start(), calls=%async_computation.54 | async-start | bytes 1114112 | tf_op jit(solution)/shard_map/reduce_scatter | solution.py:168
  2360.2 481.5 %reduce-scatter.57.cloned.1.call-start = ((), (), s32[]{:S(2)}) async-start(), calls=%async_computation.56 | async-start | bytes 1114112 | tf_op jit(solution)/shard_map/reduce_scatter | solution.py:168
  2361.0 607.0 %reduce-scatter.97.cloned.1.call-start = ((), (), s32[]{:S(2)}) async-start(), calls=%async_computation.76 | async-start | bytes 1671168 | tf_op jit(solution)/shard_map/reduce_scatter | solution.py:196
  2369.4 727.7 %reduce-scatter.101.cloned.1.call-start = ((), (), s32[]{:S(2)}) async-start(), calls=%async_computation.78 | async-start | bytes 1671168 | tf_op jit(solution)/shard_map/reduce_scatter | solution.py:196
  2378.5 847.7 %reduce-scatter.105.cloned.1.call-start = ((), (), s32[]{:S(2)}) async-start(), calls=%async_computation.80 | async-start | bytes 1671168 | tf_op jit(solution)/shard_map/reduce_scatter | solution.py:196
  2387.5 920.6 %reduce-scatter.133.cloned.1.call-start = ((), (), s32[]{:S(2)}) async-start(), calls=%async_computation.94 | async-start | bytes 2228224 | tf_op jit(solution)/shard_map/reduce_scatter | solution.py:215
  2397.5 990.4 %reduce-scatter.137.cloned.1.call-start = ((), (), s32[]{:S(2)}) async-start(), calls=%async_computation.96 | async-start | bytes 2228224 | tf_op jit(solution)/shard_map/reduce_scatter | solution.py:215
  2407.5 1060.4 %reduce-scatter.141.cloned.1.call-start = ((), (), s32[]{:S(2)}) async-start(), calls=%async_computation.98 | async-start | bytes 2228224 | tf_op jit(solution)/shard_map/reduce_scatter | solution.py:215
  2417.8 1088.4 %reduce-scatter.111.cloned.1.call-start = ((), (), s32[]{:S(2)}) async-start(), calls=%async_computation.83 | async-start | bytes 49152 | tf_op jit(solution)/shard_map/reduce_scatter | solution.py:207
  2418.4 1087.8 %reduce-scatter.115.cloned.1.call-start = ((), (), s32[]{:S(2)}) async-start(), calls=%async_computation.85 | async-start | bytes 49152 | tf_op jit(solution)/shard_map/reduce_scatter | solution.py:207
  2419.0 1087.2 %reduce-scatter.119.cloned.1.call-start = ((), (), s32[]{:S(2)}) async-start(), calls=%async_computation.87 | async-start | bytes 49152 | tf_op jit(solution)/shard_map/reduce_scatter | solution.py:207
  2419.8 1161.0 %reduce-scatter.121.cloned.1.call-start = ((), (), s32[]{:S(2)}) async-start(), calls=%async_computation.88 | async-start | bytes 2228224 | tf_op jit(solution)/shard_map/reduce_scatter | solution.py:212
  2430.7 1157.0 %reduce-scatter.91.cloned.1.call-start = ((), (), s32[]{:S(2)}) async-start(), calls=%async_computation.73 | async-start | bytes 49152 | tf_op jit(solution)/shard_map/reduce_scatter | solution.py:191
  2431.3 1167.2 %reduce-scatter.95.cloned.1.call-start = ((), (), s32[]{:S(2)}) async-start(), calls=%async_computation.75 | async-start | bytes 49152 | tf_op jit(solution)/shard_map/reduce_scatter | solution.py:191
  2432.0 1177.4 %reduce-scatter.87.cloned.1.call-start = ((), (), s32[]{:S(2)}) async-start(), calls=%async_computation.71 | async-start | bytes 49152 | tf_op jit(solution)/shard_map/reduce_scatter | solution.py:191
  2432.7 1187.4 %reduce-scatter.75.cloned.1.call-start = ((), (), s32[]{:S(2)}) async-start(), calls=%async_computation.65 | async-start | bytes 49152 | tf_op jit(solution)/shard_map/reduce_scatter | solution.py:188
  2444.1 1186.9 %reduce-scatter.79.cloned.1.call-start = ((), (), s32[]{:S(2)}) async-start(), calls=%async_computation.67 | async-start | bytes 49152 | tf_op jit(solution)/shard_map/reduce_scatter | solution.py:188
  2452.0 1189.9 %reduce-scatter.83.cloned.1.call-start = ((), (), s32[]{:S(2)}) async-start(), calls=%async_computation.69 | async-start | bytes 49152 | tf_op jit(solution)/shard_map/reduce_scatter | solution.py:188
  2459.9 1266.2 %reduce-scatter.125.cloned.1.call-start = ((), (), s32[]{:S(2)}) async-start(), calls=%async_computation.90 | async-start | bytes 2228224 | tf_op jit(solution)/shard_map/reduce_scatter | solution.py:212
  2461.9 1270.8 %reduce-scatter.71.cloned.1.call-start = ((), (), s32[]{:S(2)}) async-start(), calls=%async_computation.63 | async-start | bytes 49152 | tf_op jit(solution)/shard_map/reduce_scatter | solution.py:185
  2490.3 1253.3 %reduce-scatter.67.cloned.1.call-start = ((), (), s32[]{:S(2)}) async-start(), calls=%async_computation.61 | async-start | bytes 49152 | tf_op jit(solution)/shard_map/reduce_scatter | solution.py:185
  2492.3 349.5 %copy-start.65 = (bf16[1024,512]{1,0:T(8,128)(2,1)S(1)}, bf16[1024,512]{1,0:T(8,128)(2,1)}, u32[]{:S(2)}) copy-start(bf16[1024,512]{1,0:T(8,128)(2,1)} %copy-done.64) | copy-start | bytes 3145732
  2537.5 1216.7 %reduce-scatter.63.cloned.1.call-start = ((), (), s32[]{:S(2)}) async-start(), calls=%async_computation.59 | async-start | bytes 49152 | tf_op jit(solution)/shard_map/reduce_scatter | solution.py:185
  2612.9 1152.3 %reduce-scatter.51.cloned.1.call-start = ((), (), s32[]{:S(2)}) async-start(), calls=%async_computation.53 | async-start | bytes 98304 | tf_op jit(solution)/shard_map/reduce_scatter | solution.py:182
  2689.1 1087.1 %reduce-scatter.55.cloned.1.call-start = ((), (), s32[]{:S(2)}) async-start(), calls=%async_computation.55 | async-start | bytes 98304 | tf_op jit(solution)/shard_map/reduce_scatter | solution.py:182
  2765.4 1021.7 %reduce-scatter.59.cloned.1.call-start = ((), (), s32[]{:S(2)}) async-start(), calls=%async_computation.57 | async-start | bytes 98304 | tf_op jit(solution)/shard_map/reduce_scatter | solution.py:182
  2841.7 1029.6 %reduce-scatter.129.cloned.1.call-start = ((), (), s32[]{:S(2)}) async-start(), calls=%async_computation.92 | async-start | bytes 2228224 | tf_op jit(solution)/shard_map/reduce_scatter | solution.py:212
  2842.3 1035.8 %reduce-scatter.99.cloned.1.call-start = ((), (), s32[]{:S(2)}) async-start(), calls=%async_computation.77 | async-start | bytes 147456 | tf_op jit(solution)/shard_map/reduce_scatter | solution.py:204
  2894.7 413.4 %copy-start.192 = (f32[512]{0:T(512)S(1)}, f32[512]{0:T(512)}, u32[]{:S(2)}) copy-start(f32[512]{0:T(512)} %get-tuple-element.1025) | copy-start | bytes 6148
  2894.7 413.4 %copy-start.193 = (f32[512]{0:T(512)S(1)}, f32[512]{0:T(512)}, u32[]{:S(2)}) copy-start(f32[512]{0:T(512)} %get-tuple-element.1026) | copy-start | bytes 6148
  2894.7 413.4 %copy-start.194 = (f32[512]{0:T(512)S(1)}, f32[512]{0:T(512)}, u32[]{:S(2)}) copy-start(f32[512]{0:T(512)} %get-tuple-element.1030) | copy-start | bytes 6148
  2894.8 413.4 %copy-start.189 = (f32[512]{0:T(512)S(1)}, f32[512]{0:T(512)}, u32[]{:S(2)}) copy-start(f32[512]{0:T(512)} %get-tuple-element.1018) | copy-start | bytes 6148
  2894.8 413.4 %copy-start.190 = (f32[512]{0:T(512)S(1)}, f32[512]{0:T(512)}, u32[]{:S(2)}) copy-start(f32[512]{0:T(512)} %get-tuple-element.1029) | copy-start | bytes 6148
  2894.8 413.4 %copy-start.191 = (f32[512]{0:T(512)S(1)}, f32[512]{0:T(512)}, u32[]{:S(2)}) copy-start(f32[512]{0:T(512)} %get-tuple-element.1033) | copy-start | bytes 6148
  2894.8 493.2 %copy-start.166 = (f32[2048]{0:T(1024)S(1)}, f32[2048]{0:T(1024)}, u32[]{:S(2)}) copy-start(f32[2048]{0:T(1024)} %get-tuple-element.1411) | copy-start | bytes 24580
  2894.8 493.2 %copy-start.167 = (f32[2048]{0:T(1024)S(1)}, f32[2048]{0:T(1024)}, u32[]{:S(2)}) copy-start(f32[2048]{0:T(1024)} %get-tuple-element.1407) | copy-start | bytes 24580
  2894.8 493.2 %copy-start.168 = (f32[2048]{0:T(1024)S(1)}, f32[2048]{0:T(1024)}, u32[]{:S(2)}) copy-start(f32[2048]{0:T(1024)} %get-tuple-element.1409) | copy-start | bytes 24580
  2968.0 920.9 %reduce-scatter.103.cloned.1.call-start = ((), (), s32[]{:S(2)}) async-start(), calls=%async_computation.79 | async-start | bytes 147456 | tf_op jit(solution)/shard_map/reduce_scatter | solution.py:204
  3097.2 802.6 %reduce-scatter.107.cloned.1.call-start = ((), (), s32[]{:S(2)}) async-start(), calls=%async_computation.81 | async-start | bytes 147456 | tf_op jit(solution)/shard_map/reduce_scatter | solution.py:204
  3226.2 684.4 %reduce-scatter.135.cloned.1.call-start = ((), (), s32[]{:S(2)}) async-start(), calls=%async_computation.95 | async-start | bytes 196608 | tf_op jit(solution)/shard_map/reduce_scatter | solution.py:223
  3308.1 613.3 %reduce-scatter.139.cloned.1.call-start = ((), (), s32[]{:S(2)}) async-start(), calls=%async_computation.97 | async-start | bytes 196608 | tf_op jit(solution)/shard_map/reduce_scatter | solution.py:223
  3387.9 544.3 %reduce-scatter.143.cloned.1.call-start = ((), (), s32[]{:S(2)}) async-start(), calls=%async_computation.99 | async-start | bytes 196608 | tf_op jit(solution)/shard_map/reduce_scatter | solution.py:223
  3468.0 475.3 %reduce-scatter.123.cloned.1.call-start = ((), (), s32[]{:S(2)}) async-start(), calls=%async_computation.89 | async-start | bytes 196608 | tf_op jit(solution)/shard_map/reduce_scatter | solution.py:220
  3580.8 373.3 %reduce-scatter.127.cloned.1.call-start = ((), (), s32[]{:S(2)}) async-start(), calls=%async_computation.91 | async-start | bytes 196608 | tf_op jit(solution)/shard_map/reduce_scatter | solution.py:220
  3726.2 238.9 %reduce-scatter.131.cloned.1.call-start = ((), (), s32[]{:S(2)}) async-start(), calls=%async_computation.93 | async-start | bytes 196608 | tf_op jit(solution)/shard_map/reduce_scatter | solution.py:220
  (270 other events, 11845.3 us)
Sparse Core Ops, SparseCore 0:
  11.1 59.9 all-gather.4
  73.9 59.2 all-gather.6
  136.0 62.9 all-gather.8
  201.6 61.2 all-gather.10
  929.3 74.8 reduce-scatter.108
  1442.2 74.9 reduce-scatter.112
  1519.4 73.0 reduce-scatter.116
  1594.9 73.0 reduce-scatter.88
  1670.2 72.8 reduce-scatter.92
  1746.0 74.7 reduce-scatter.84
  2023.2 74.7 reduce-scatter.72
  2100.2 72.9 reduce-scatter.76
  2312.5 74.7 reduce-scatter.80
  2389.5 72.9 reduce-scatter.68
  2464.6 72.9 reduce-scatter.64
  2539.7 72.9 reduce-scatter.60
  2614.8 74.2 reduce-scatter.48
  2691.2 74.0 reduce-scatter.52
  2767.6 74.0 reduce-scatter.56
  2847.1 120.8 reduce-scatter.96
  2973.5 123.5 reduce-scatter.100
  3102.7 123.4 reduce-scatter.104
  3228.6 79.4 reduce-scatter.132
  3310.3 77.5 reduce-scatter.136
  3390.3 77.6 reduce-scatter.140
  3470.1 4.8 reduce-scatter.110
  3477.1 8.5 reduce-scatter.114
  3487.9 8.5 reduce-scatter.118
  3498.9 81.8 reduce-scatter.120
  3582.9 4.6 reduce-scatter.90
  3589.9 8.5 reduce-scatter.94
  3600.8 8.5 reduce-scatter.86
  3611.5 8.5 reduce-scatter.74
  3622.4 8.5 reduce-scatter.78
  3633.3 8.5 reduce-scatter.82
  3644.1 81.9 reduce-scatter.124
  3728.3 4.3 reduce-scatter.70
  3734.9 8.5 reduce-scatter.66
  3745.7 8.5 reduce-scatter.62
  3756.5 8.6 reduce-scatter.50
  3767.5 8.5 reduce-scatter.54
  3778.4 8.5 reduce-scatter.58
  3789.3 82.0 reduce-scatter.128
  3873.6 4.4 reduce-scatter.98
  3880.2 8.6 reduce-scatter.102
  3891.1 8.6 reduce-scatter.106
  3901.9 8.6 reduce-scatter.134
  3912.7 8.6 reduce-scatter.138
  3923.6 8.6 reduce-scatter.142
  3934.5 8.6 reduce-scatter.122
  3945.4 8.6 reduce-scatter.126
  3956.4 8.6 reduce-scatter.130
where the time goes:
time: 4000 us; the launch traced here: 3970 us
  waiting for transfers between devices  1360 us (34%)
  matrix products  1330 us (33%)
  local copies, waits for them, and re-layouts  615 us (15%)
  other arithmetic  414 us (10%)
  blocking collectives  234 us (6%)
    reduce_scatter x3, waiting for transfers between devices, scatter_all(): lax.psum_scatter(sp[2].astype(jnp.bfloat16), 'wide', scatter_dimension=0,...  318 us
    reduce_scatter x3, waiting for transfers between devices, scatter_all(): lax.psum_scatter(fp[4].astype(jnp.bfloat16), 'wide', scatter_dimension=0,...  241 us
    reduce_scatter x3, waiting for transfers between devices, scatter_all(): lax.psum_scatter(fp[2].astype(jnp.bfloat16), 'wide', scatter_dimension=0,...  239 us
    dot_general x24, matrix products, attend_backward(): jnp.einsum('gqhd,gkhd->ghqk', gheads, vheads, preferred_element_type=jnp....  237 us
    reduce_scatter x3, waiting for transfers between devices, scatter_all(): lax.psum_scatter(cp[0].astype(jnp.bfloat16), 'wide', scatter_dimension=0,...  225 us
    dot_general x48, matrix products, block_scores(): jnp.einsum('gqhd,gkhd->ghqk', qheads, kheads, preferred_element_type=jnp....  211 us
    dynamic_slice x168, local copies, waits for them, and re-layouts, blocked(): results = lax.map(function, pieces)  184 us
    dot_general x24, matrix products, attend_backward(): jnp.einsum('ghqk,gqhd->gkhd', attn_probs.astype(jnp.bfloat16), gheads, pr...  183 us
  transfers between devices with their start and end apart: 52, of which 35 were waited for; matrix products, arithmetic and copies ran while one was open for 54% of the time, Pallas kernels for 0%

commit v1 on v0

v1 whole, which is shorter than its diff:
```python
import functools

import jax
import jax.numpy as jnp
from jax import lax
from jax.experimental import pallas as pl
from jax.experimental.pallas import tpu as pltpu
from jax.sharding import PartitionSpec as P

D = 512
HEADS = 16
HD = 32
FF = 2048
CIN = 256
G = 4
NL = 256
IN_G = 512
SEGS = 4
QT = 32
PACK = 256
TILES = NL // QT
PER_STEP = 2
LAT_STEP = PER_STEP * NL
IN_STEP = PER_STEP * IN_G
CROSS_WIDTHS = (128, 192, 256, 384, 512)
SELF_WIDTHS = (128, 192, 256)

F32 = jnp.float32
BF16 = jnp.bfloat16
NEG_FILL = -1e30
EPSILON = 1e-05
SCALE = HD**-0.5
LOG2E = 1.4426950408889634
SCALE2 = SCALE * LOG2E
VMEM_BYTES = 60 * 1024 * 1024

TAIL_RATE = 0.28
TAIL_POLY = (
    0.1165209849818009,
    0.06749547174407416,
    0.2689133347091787,
    -0.23699737809142182,
    0.38987640062523105,
    -0.10580882324798475,
)

ROW_QGAIN, ROW_QSHIFT, ROW_SOURCE, ROW_QBIAS, ROW_VBIAS, ROW_COBIAS = range(6)
ROW_SGAIN, ROW_SSHIFT, ROW_SQBIAS, ROW_SVBIAS, ROW_SOBIAS = range(6, 11)
ROW_FGAIN, ROW_FSHIFT, ROW_UBIAS, ROW_DBIAS = 11, 12, 13, 17
VEC_ROWS = 24


def dot_plain(left, right):
    return lax.dot_general(left, right, (((1,), (0,)), ((), ())), preferred_element_type=F32)


def dot_first(left, right):
    return lax.dot_general(left, right, (((0,), (0,)), ((), ())), preferred_element_type=F32)


def dot_last(left, right):
    return lax.dot_general(left, right, (((1,), (1,)), ((), ())), preferred_element_type=F32)


def over_rows(total, chunk, body):
    def step(index, carry):
        body(pl.ds(pl.multiple_of(index * chunk, chunk), chunk))
        return carry

    lax.fori_loop(0, total // chunk, step, 0)


def norm_forward(rows, gain, shift):
    centered = rows - jnp.mean(rows, -1, keepdims=True)
    rscale = lax.rsqrt(jnp.mean(centered * centered, -1, keepdims=True) + EPSILON)
    normed = centered * rscale
    return normed * gain + shift, normed, rscale


def norm_backward(grad, normed, rscale, gain):
    dnormed = grad * gain
    return rscale * (
        dnormed
        - jnp.mean(dnormed, -1, keepdims=True)
        - normed * jnp.mean(dnormed * normed, -1, keepdims=True)
    )


def column_sum(rows):
    return jnp.sum(rows, 0, keepdims=True)


def gelu_pair(hidden):
    size = jnp.abs(hidden)
    ratio = 1.0 / (1.0 + TAIL_RATE * size)
    bell = jnp.exp2(hidden * hidden * (-0.5 * LOG2E))
    poly = TAIL_POLY[-1] * ratio
    for coefficient in TAIL_POLY[-2::-1]:
        poly = (poly + coefficient) * ratio
    tail = poly * bell
    cdf = jnp.where(hidden >= 0.0, 1.0 - tail, tail)
    return hidden * cdf, cdf + hidden * bell * 0.3989422804014327


def fill_block_mask(mask_ref):
    row_head = lax.broadcasted_iota(jnp.int32, (PACK, PACK), 0) // QT
    lane_head = lax.broadcasted_iota(jnp.int32, (PACK, PACK), 1) // HD
    mask_ref[...] = jnp.where(row_head == lane_head, 1.0, 0.0).astype(BF16)


def block_diagonal(rows, mask):
    return jnp.concatenate([rows] * (PACK // QT), 0) * mask


def take_diagonal(full):
    lane = lax.broadcasted_iota(jnp.int32, (QT, 128), 1)
    columns = []
    for half in range(2):
        base = 128 * half
        picked = full[base : base + QT, base : base + 128]
        for head in range(1, 4):
            row = base + QT * head
            picked = jnp.where(
                lane >= HD * head, full[row : row + QT, base : base + 128], picked
            )
        columns.append(picked)
    return jnp.concatenate(columns, 1)


def segment_at(cuts, place):
    return sum((place >= cut).astype(jnp.int32) for cut in cuts)


def pick(index, values):
    result = values[0]
    for at in range(1, len(values)):
        result = jnp.where(index == at, values[at], result)
    return result


def tile_window(query_cuts, key_cuts, key_count, tile):
    first = segment_at(query_cuts, tile * QT)
    last = segment_at(query_cuts, tile * QT + QT - 1)
    low = pick(first, [0] + key_cuts) // 16 * 16
    return low, pick(last, key_cuts + [key_count]) - low


def in_windows(low, needed, key_count, widths, body):
    smaller = 0
    for width in widths:

        @pl.when((needed > smaller) & (needed <= width))
        def _(width=width):
            body(pl.multiple_of(jnp.minimum(low, key_count - width), 16), width)

        smaller = width


def query_segments(query_cuts, tile):
    lane = lax.broadcasted_iota(jnp.int32, (1, PACK), 1) % QT
    return segment_at(query_cuts, tile * QT + lane)


def fill_key_segments(seg_ref, key_cuts):
    seg_ref[...] = segment_at(key_cuts, lax.broadcasted_iota(jnp.int32, seg_ref.shape, 0))


def allowed_pairs(seg_ref, low, width, query_seg):
    key_seg = seg_ref[pl.ds(low, width), :]
    return jnp.concatenate([key_seg, key_seg], 1) == query_seg


def attend_tile(query, keys, values, allowed, mask):
    scores = jnp.where(allowed, dot_last(keys, block_diagonal(query, mask)), NEG_FILL)
    top = jnp.max(scores, 0, keepdims=True)
    powers = jnp.exp2((scores - top) * SCALE2)
    total = jnp.sum(powers, 0, keepdims=True)
    probs = (powers * (1.0 / total)).astype(BF16)
    mixed = take_diagonal(dot_first(probs, values)).astype(BF16)
    return mixed, probs, top * SCALE2 + jnp.log2(total)


def attend_tile_back(query, keys, values, out_grad, probs, probs_low, mask):
    grad_blocks = block_diagonal(out_grad, mask)
    dprobs = dot_last(values, grad_blocks)
    weighted = probs * dprobs
    delta = jnp.sum(weighted, 0, keepdims=True)
    dscores = (weighted - probs * delta).astype(BF16)
    dvalues = dot_plain(probs_low, grad_blocks)
    dkeys = dot_plain(dscores, block_diagonal(query, mask))
    dquery = take_diagonal(dot_first(dscores, keys))
    return dquery, dkeys, dvalues


def half(part):
    return slice(PACK * part, PACK * part + PACK)


def group_cuts(cuts_ref, group):
    key_cuts = [cuts_ref[group, at] for at in range(SEGS - 1)]
    latent_cuts = [cuts_ref[group, 4 + at] for at in range(SEGS - 1)]
    return key_cuts, latent_cuts


def cross_forward_kernel(
    cuts_ref,
    inputs_ref,
    latent_ref,
    wq_ref,
    wkv_ref,
    wo_ref,
    vec_ref,
    after_ref,
    mix_ref,
    kv_ref,
    lse_ref,
    query_ref,
    source_ref,
    mask_ref,
    seg_ref,
):
    step = pl.program_id(0)

    @pl.when(step == 0)
    def _():
        fill_block_mask(mask_ref)
        low, _, _ = norm_forward(
            latent_ref[...].astype(F32),
            vec_ref[ROW_QGAIN : ROW_QGAIN + 1, :],
            vec_ref[ROW_QSHIFT : ROW_QSHIFT + 1, :],
        )
        query = dot_plain(low.astype(BF16), wq_ref[...])
        query_ref[...] = (query + vec_ref[ROW_QBIAS : ROW_QBIAS + 1, :]).astype(BF16)

    def source_rows(rows):
        low, _, _ = norm_forward(
            inputs_ref[rows, :].astype(F32),
            vec_ref[ROW_SOURCE : ROW_SOURCE + 1, :CIN],
            vec_ref[ROW_SOURCE : ROW_SOURCE + 1, CIN:],
        )
        source_ref[rows, :] = low.astype(BF16)

    over_rows(IN_STEP, 128, source_rows)
    kv_ref[:, :D] = dot_plain(source_ref[...], wkv_ref[:, :D]).astype(BF16)
    kv_ref[:, D:] = (
        dot_plain(source_ref[...], wkv_ref[:, D:]) + vec_ref[ROW_VBIAS : ROW_VBIAS + 1, :]
    ).astype(BF16)

    base = pl.multiple_of(step % (G // PER_STEP) * LAT_STEP, LAT_STEP)
    for member in range(PER_STEP):
        key_cuts, latent_cuts = group_cuts(cuts_ref, step * PER_STEP + member)
        fill_key_segments(seg_ref, key_cuts)

        def tile_body(tile, carry, member=member, key_cuts=key_cuts, latent_cuts=latent_cuts):
            row = pl.multiple_of(member * NL + tile * QT, QT)
            query_seg = query_segments(latent_cuts, tile)
            low, needed = tile_window(latent_cuts, key_cuts, IN_G, tile)

            def window(start, width):
                keys = pl.ds(member * IN_G + start, width)
                allowed = allowed_pairs(seg_ref, start, width, query_seg)
                for part in range(2):
                    mixed, _, lse = attend_tile(
                        query_ref[pl.ds(base + row, QT), half(part)],
                        kv_ref[keys, half(part)],
                        kv_ref[keys, half(part + 2)],
                        allowed,
                        mask_ref[...],
                    )
                    mix_ref[pl.ds(row, QT), half(part)] = mixed
                    lse_ref[pl.ds((member * TILES + tile) * 2 + part, 1), :] = lse

            in_windows(low, needed, IN_G, CROSS_WIDTHS, window)
            return carry

        lax.fori_loop(0, TILES, tile_body, 0)

    after_ref[...] = (
        latent_ref[pl.ds(base, LAT_STEP), :].astype(F32)
        + dot_plain(mix_ref[...], wo_ref[...])
        + vec_ref[ROW_COBIAS : ROW_COBIAS + 1, :]
    )


def middle_kernel(
    cuts_ref,
    after_ref,
    cot_ref,
    wproj_ref,
    wso_ref,
    wup_ref,
    wdn_ref,
    vec_ref,
    out_ref,
    dcross_ref,
    glat_ref,
    small_ref,
    gproj_ref,
    gso_ref,
    gup_ref,
    gdn_ref,
    mask_ref,
    seg_ref,
    hat1_ref,
    rs1_ref,
    low1_ref,
    triple_ref,
    probs_ref,
    mix_ref,
    res_ref,
    hat2_ref,
    rs2_ref,
    low2_ref,
    dtop_ref,
    dso_ref,
    dmix_ref,
    dtriple_ref,
    dkey_ref,
    dvalue_ref,
    aproj_ref,
    aso_ref,
    aup_ref,
    adn_ref,
):
    step = pl.program_id(0)
    last = pl.num_programs(0) - 1

    def vec(row):
        return vec_ref[row : row + 1, :]

    def add_small(row, value):
        small_ref[row : row + 1, :] += value

    @pl.when(step == 0)
    def _():
        fill_block_mask(mask_ref)
        for ref in (glat_ref, small_ref, aproj_ref, aso_ref, aup_ref, adn_ref):
            ref[...] = jnp.zeros(ref.shape, ref.dtype)

    def first_norm(rows):
        low, normed, rscale = norm_forward(after_ref[rows, :], vec(ROW_SGAIN), vec(ROW_SSHIFT))
        low1_ref[rows, :] = low.astype(BF16)
        hat1_ref[rows, :] = normed
        rs1_ref[rows, :] = rscale

    over_rows(LAT_STEP, 64, first_norm)
    for block, bias in enumerate((ROW_SQBIAS, None, ROW_SVBIAS)):
        columns = slice(D * block, D * block + D)
        product = dot_plain(low1_ref[...], wproj_ref[:, columns])
        if bias is not None:
            product = product + vec(bias)
        triple_ref[:, columns] = product.astype(BF16)

    for member in range(PER_STEP):
        _, latent_cuts = group_cuts(cuts_ref, step * PER_STEP + member)
        fill_key_segments(seg_ref, latent_cuts)

        def tile_body(tile, carry, member=member, latent_cuts=latent_cuts):
            row = pl.multiple_of(member * NL + tile * QT, QT)
            query_seg = query_segments(latent_cuts, tile)
            low, needed = tile_window(latent_cuts, latent_cuts, NL, tile)

            def window(start, width):
                keys = pl.ds(member * NL + start, width)
                allowed = allowed_pairs(seg_ref, start, width, query_seg)
                for part in range(2):
                    mixed, probs, _ = attend_tile(
                        triple_ref[pl.ds(row, QT), half(part)],
                        triple_ref[keys, half(part + 2)],
                        triple_ref[keys, half(part + 4)],
                        allowed,
                        mask_ref[...],
                    )
                    mix_ref[pl.ds(row, QT), half(part)] = mixed
                    probs_ref[(member * TILES + tile) * 2 + part, :width, :] = probs

            in_windows(low, needed, NL, SELF_WIDTHS, window)
            return carry

        lax.fori_loop(0, TILES, tile_body, 0)

    res_ref[...] = after_ref[...] + dot_plain(mix_ref[...], wso_ref[...]) + vec(ROW_SOBIAS)

    def second_norm(rows):
        low, normed, rscale = norm_forward(res_ref[rows, :], vec(ROW_FGAIN), vec(ROW_FSHIFT))
        low2_ref[rows, :] = low.astype(BF16)
        hat2_ref[rows, :] = normed
        rs2_ref[rows, :] = rscale

    over_rows(LAT_STEP, 64, second_norm)
    dtop_ref[...] = jnp.zeros(dtop_ref.shape, F32)

    def feed_block(block, carry):
        columns = pl.ds(pl.multiple_of(block * D, D), D)
        hidden = dot_plain(low2_ref[...], wup_ref[:, columns]) + vec_ref[
            pl.ds(ROW_UBIAS + block, 1), :
        ]
        active, slope = gelu_pair(hidden)
        active = active.astype(BF16)
        dhidden = (slope * dot_last(cot_ref[...], wdn_ref[columns, :])).astype(BF16)
        small_ref[pl.ds(ROW_UBIAS + block, 1), :] += column_sum(dhidden.astype(F32))
        res_ref[...] += dot_plain(active, wdn_ref[columns, :])
        adn_ref[columns, :] += dot_first(active, cot_ref[...])
        aup_ref[:, columns] += dot_first(low2_ref[...], dhidden)
        dtop_ref[...] += dot_last(dhidden, wup_ref[:, columns])
        return carry

    lax.fori_loop(0, FF // D, feed_block, 0)

    def after_feed(rows):
        out_ref[rows, :] = (res_ref[rows, :] + vec(ROW_DBIAS)).astype(BF16)
        dtop = dtop_ref[rows, :]
        normed = hat2_ref[rows, :]
        cot = cot_ref[rows, :].astype(F32)
        dafter = cot + norm_backward(dtop, normed, rs2_ref[rows, :], vec(ROW_FGAIN))
        dlow = dafter.astype(BF16)
        res_ref[rows, :] = dafter
        dso_ref[rows, :] = dlow
        add_small(ROW_FGAIN, column_sum(dtop * normed))
        add_small(ROW_FSHIFT, column_sum(dtop))
        add_small(ROW_DBIAS, column_sum(cot))
        add_small(ROW_SOBIAS, column_sum(dlow.astype(F32)))

    over_rows(LAT_STEP, 64, after_feed)
    aso_ref[...] += dot_first(mix_ref[...], dso_ref[...])
    dmix_ref[...] = dot_last(dso_ref[...], wso_ref[...]).astype(BF16)

    for member in range(PER_STEP):
        _, latent_cuts = group_cuts(cuts_ref, step * PER_STEP + member)
        dkey_ref[...] = jnp.zeros(dkey_ref.shape, F32)
        dvalue_ref[...] = jnp.zeros(dvalue_ref.shape, F32)

        def tile_back(tile, carry, member=member, latent_cuts=latent_cuts):
            row = pl.multiple_of(member * NL + tile * QT, QT)
            low, needed = tile_window(latent_cuts, latent_cuts, NL, tile)

            def window(start, width):
                keys = pl.ds(member * NL + start, width)
                for part in range(2):
                    probs_low = probs_ref[(member * TILES + tile) * 2 + part, :width, :]
                    dquery, dkeys, dvalues = attend_tile_back(
                        triple_ref[pl.ds(row, QT), half(part)],
                        triple_ref[keys, half(part + 2)],
                        triple_ref[keys, half(part + 4)],
                        dmix_ref[pl.ds(row, QT), half(part)],
                        probs_low.astype(F32),
                        probs_low,
                        mask_ref[...],
                    )
                    dtriple_ref[pl.ds(row, QT), half(part)] = (dquery * SCALE).astype(BF16)
                    dkey_ref[pl.ds(start, width), half(part)] += dkeys
                    dvalue_ref[pl.ds(start, width), half(part)] += dvalues

            in_windows(low, needed, NL, SELF_WIDTHS, window)
            return carry

        lax.fori_loop(0, TILES, tile_back, 0)
        rows = slice(member * NL, member * NL + NL)
        dtriple_ref[rows, D : 2 * D] = (dkey_ref[...] * SCALE).astype(BF16)
        dtriple_ref[rows, 2 * D :] = dvalue_ref[...].astype(BF16)

    for block in range(3):
        columns = slice(D * block, D * block + D)
        aproj_ref[:, columns] += dot_first(low1_ref[...], dtriple_ref[:, columns])
    add_small(ROW_SQBIAS, column_sum(dtriple_ref[:, :D].astype(F32)))
    add_small(ROW_SVBIAS, column_sum(dtriple_ref[:, 2 * D :].astype(F32)))
    dtop_ref[...] = dot_last(dtriple_ref[...], wproj_ref[...])
    base = step % (G // PER_STEP) * LAT_STEP

    def after_self(rows):
        dmid = dtop_ref[rows, :]
        normed = hat1_ref[rows, :]
        dafter = res_ref[rows, :] + norm_backward(dmid, normed, rs1_ref[rows, :], vec(ROW_SGAIN))
        dcross_ref[rows, :] = dafter.astype(BF16)
        glat_ref[pl.ds(pl.multiple_of(base + rows.start, 64), rows.size), :] += dafter
        add_small(ROW_SGAIN, column_sum(dmid * normed))
        add_small(ROW_SSHIFT, column_sum(dmid))

    over_rows(LAT_STEP, 64, after_self)

    @pl.when(step == last)
    def _():
        gproj_ref[...] = aproj_ref[...].astype(BF16)
        gso_ref[...] = aso_ref[...].astype(BF16)
        gup_ref[...] = aup_ref[...].astype(BF16)
        gdn_ref[...] = adn_ref[...].astype(BF16)


def cross_backward_kernel(
    cuts_ref,
    inputs_ref,
    kv_ref,
    mix_ref,
    lse_ref,
    dcross_ref,
    query_ref,
    latent_ref,
    glat_ref,
    wq_ref,
    wkv_ref,
    wo_ref,
    vec_ref,
    dinput_ref,
    glatout_ref,
    gq_ref,
    gkv_ref,
    go_ref,
    small_ref,
    mask_ref,
    seg_ref,
    source_ref,
    hat_ref,
    rs_ref,
    dmix_ref,
    dkey_ref,
    dvalue_ref,
    dkv_ref,
    dquery_ref,
    akv_ref,
    ao_ref,
):
    step = pl.program_id(0)
    last = pl.num_programs(0) - 1

    def vec(row):
        return vec_ref[row : row + 1, :]

    def add_small(row, value):
        small_ref[row : row + 1, :] += value

    @pl.when(step == 0)
    def _():
        fill_block_mask(mask_ref)
        for ref in (small_ref, dquery_ref, akv_ref, ao_ref):
            ref[...] = jnp.zeros(ref.shape, ref.dtype)

    source_gain = vec_ref[ROW_SOURCE : ROW_SOURCE + 1, :CIN]
    source_shift = vec_ref[ROW_SOURCE : ROW_SOURCE + 1, CIN:]

    def source_rows(rows):
        low, normed, rscale = norm_forward(
            inputs_ref[rows, :].astype(F32), source_gain, source_shift
        )
        source_ref[rows, :] = low.astype(BF16)
        hat_ref[rows, :] = normed
        rs_ref[rows, :] = rscale

    over_rows(IN_STEP, 128, source_rows)
    ao_ref[...] += dot_first(mix_ref[...], dcross_ref[...])
    add_small(ROW_COBIAS, column_sum(dcross_ref[...].astype(F32)))
    dmix_ref[...] = dot_last(dcross_ref[...], wo_ref[...]).astype(BF16)

    base = pl.multiple_of(step % (G // PER_STEP) * LAT_STEP, LAT_STEP)
    for member in range(PER_STEP):
        key_cuts, latent_cuts = group_cuts(cuts_ref, step * PER_STEP + member)
        fill_key_segments(seg_ref, key_cuts)
        dkey_ref[...] = jnp.zeros(dkey_ref.shape, F32)
        dvalue_ref[...] = jnp.zeros(dvalue_ref.shape, F32)

        def tile_back(tile, carry, member=member, key_cuts=key_cuts, latent_cuts=latent_cuts):
            row = pl.multiple_of(member * NL + tile * QT, QT)
            query_seg = query_segments(latent_cuts, tile)
            low, needed = tile_window(latent_cuts, key_cuts, IN_G, tile)

            def window(start, width):
                keys = pl.ds(member * IN_G + start, width)
                allowed = allowed_pairs(seg_ref, start, width, query_seg)
                for part in range(2):
                    query = query_ref[pl.ds(base + row, QT), half(part)]
                    key_rows = kv_ref[keys, half(part)]
                    lse = lse_ref[pl.ds((member * TILES + tile) * 2 + part, 1), :]
                    scores = dot_last(key_rows, block_diagonal(query, mask_ref[...]))
                    probs = jnp.exp2(jnp.where(allowed, scores * SCALE2 - lse, NEG_FILL))
                    dquery, dkeys, dvalues = attend_tile_back(
                        query,
                        key_rows,
                        kv_ref[keys, half(part + 2)],
                        dmix_ref[pl.ds(row, QT), half(part)],
                        probs,
                        probs.astype(BF16),
                        mask_ref[...],
                    )
                    dquery_ref[pl.ds(base + row, QT), half(part)] += dquery
                    dkey_ref[pl.ds(start, width), half(part)] += dkeys
                    dvalue_ref[pl.ds(start, width), half(part)] += dvalues

            in_windows(low, needed, IN_G, CROSS_WIDTHS, window)
            return carry

        lax.fori_loop(0, TILES, tile_back, 0)
        rows = slice(member * IN_G, member * IN_G + IN_G)
        dkv_ref[rows, :D] = (dkey_ref[...] * SCALE).astype(BF16)
        dkv_ref[rows, D:] = dvalue_ref[...].astype(BF16)

    for part in range(2):
        columns = slice(D * part, D * part + D)
        akv_ref[:, columns] += dot_first(source_ref[...], dkv_ref[:, columns])
    add_small(ROW_VBIAS, column_sum(dkv_ref[:, D:].astype(F32)))
    dinput_ref[...] = dot_last(dkv_ref[...], wkv_ref[...])

    def source_back(rows):
        dsource = dinput_ref[rows, :]
        normed = hat_ref[rows, :]
        small_ref[ROW_SOURCE : ROW_SOURCE + 1, :CIN] += column_sum(dsource * normed)
        small_ref[ROW_SOURCE : ROW_SOURCE + 1, CIN:] += column_sum(dsource)
        dinput_ref[rows, :] = norm_backward(dsource, normed, rs_ref[rows, :], source_gain)

    over_rows(IN_STEP, 128, source_back)

    @pl.when(step == last)
    def _():
        gkv_ref[...] = akv_ref[...].astype(BF16)
        go_ref[...] = ao_ref[...].astype(BF16)
        low, normed, rscale = norm_forward(
            latent_ref[...].astype(F32), vec(ROW_QGAIN), vec(ROW_QSHIFT)
        )
        dquery = (dquery_ref[...] * SCALE).astype(BF16)
        gq_ref[...] = dot_first(low.astype(BF16), dquery).astype(BF16)
        add_small(ROW_QBIAS, column_sum(dquery.astype(F32)))
        dnorm = dot_last(dquery, wq_ref[...])
        add_small(ROW_QGAIN, column_sum(dnorm * normed))
        add_small(ROW_QSHIFT, column_sum(dnorm))
        glatout_ref[...] = (
            glat_ref[...] + norm_backward(dnorm, normed, rscale, vec(ROW_QGAIN))
        ).astype(BF16)


def rows_spec(rows, columns):
    return pl.BlockSpec((rows, columns), lambda step, cuts: (step, 0))


def whole_spec(rows, columns):
    return pl.BlockSpec(
        (rows, columns), lambda step, cuts: (0, 0), pipeline_mode=pl.Buffered(1)
    )


def kernel_call(kernel, steps, in_specs, out_specs, out_shape, scratch, flops):
    return pl.pallas_call(
        kernel,
        grid_spec=pltpu.PrefetchScalarGridSpec(
            num_scalar_prefetch=1,
            grid=(steps,),
            in_specs=in_specs,
            out_specs=out_specs,
            scratch_shapes=scratch,
        ),
        out_shape=out_shape,
        compiler_params=pltpu.CompilerParams(
            vmem_limit_bytes=VMEM_BYTES, dimension_semantics=("arbitrary",)
        ),
        cost_estimate=pl.CostEstimate(
            flops=flops, bytes_accessed=100 * 2**20, transcendentals=0
        ),
    )


def gather(shard):
    return lax.all_gather(
        lax.all_gather(shard, "narrow", axis=1, tiled=True), "wide", axis=0, tiled=True
    )


def scatter(total):
    rows = lax.psum_scatter(total, "wide", scatter_dimension=0, tiled=True)
    return lax.psum_scatter(rows, "narrow", scatter_dimension=1, tiled=True).astype(F32)


def shape(rows, columns, dtype):
    return jax.ShapeDtypeStruct((rows, columns), dtype)


def local(
    inputs,
    input_segments,
    latent_segments,
    cotangent,
    latent_array,
    query_gain,
    query_shift,
    source_gain,
    source_shift,
    cross_query,
    cross_qbias,
    cross_keyval,
    cross_vbias,
    cross_output,
    cross_obias,
    self_gain,
    self_shift,
    self_project,
    self_qbias,
    self_vbias,
    self_output,
    self_obias,
    feed_gain,
    feed_shift,
    feed_upward,
    feed_ubias,
    feed_downward,
    feed_dbias,
):
    lat_rows = cotangent.shape[0]
    in_rows = inputs.shape[0]
    groups = lat_rows // NL
    steps = groups // PER_STEP

    vectors = jnp.concatenate(
        [
            query_gain,
            query_shift,
            source_gain,
            source_shift,
            cross_qbias,
            cross_vbias,
            cross_obias,
            self_gain,
            self_shift,
            self_qbias,
            self_vbias,
            self_obias,
            feed_gain,
            feed_shift,
            feed_ubias,
            feed_dbias,
            jnp.zeros(((VEC_ROWS - ROW_DBIAS - 1) * D,), BF16),
        ]
    )
    vectors = vectors.astype(F32).reshape(VEC_ROWS, D)
    marks = jnp.arange(1, SEGS, dtype=jnp.int32)
    in_cuts = jnp.sum(input_segments.reshape(groups, IN_G, 1) < marks, 1, dtype=jnp.int32)
    lat_cuts = jnp.sum(latent_segments.reshape(groups, NL, 1) < marks, 1, dtype=jnp.int32)
    blank = jnp.zeros((groups, 1), jnp.int32)
    cuts = jnp.concatenate([in_cuts, blank, lat_cuts, blank], 1)

    latent_full = gather(latent_array)
    wq = gather(cross_query)
    wkv = gather(cross_keyval)
    wo = gather(cross_output)
    wproj = gather(self_project)
    wso = gather(self_output)
    wup = gather(feed_upward)
    wdn = gather(feed_downward)

    vec_spec = whole_spec(VEC_ROWS, D)
    lse_rows = PER_STEP * TILES * 2
    after, cross_mix, keyval, lse, query = kernel_call(
        cross_forward_kernel,
        steps,
        [
            rows_spec(IN_STEP, CIN),
            whole_spec(G * NL, D),
            whole_spec(D, D),
            whole_spec(CIN, 2 * D),
            whole_spec(D, D),
            vec_spec,
        ],
        [
            rows_spec(LAT_STEP, D),
            rows_spec(LAT_STEP, D),
            rows_spec(IN_STEP, 2 * D),
            rows_spec(lse_rows, PACK),
            whole_spec(G * NL, D),
        ],
        [
            shape(lat_rows, D, F32),
            shape(lat_rows, D, BF16),
            shape(in_rows, 2 * D, BF16),
            shape(steps * lse_rows, PACK, F32),
            shape(G * NL, D, BF16),
        ],
        [
            pltpu.VMEM((IN_STEP, CIN), BF16),
            pltpu.VMEM((PACK, PACK), BF16),
            pltpu.VMEM((IN_G, 128), jnp.int32),
        ],
        60 * 10**9,
    )(cuts, inputs, latent_full, wq, wkv, wo, vectors)

    latents_out, dcross, glat, middle_small, gproj, gso, gup, gdn = kernel_call(
        middle_kernel,
        steps,
        [
            rows_spec(LAT_STEP, D),
            rows_spec(LAT_STEP, D),
            whole_spec(D, 3 * D),
            whole_spec(D, D),
            whole_spec(D, FF),
            whole_spec(FF, D),
            vec_spec,
        ],
        [
            rows_spec(LAT_STEP, D),
            rows_spec(LAT_STEP, D),
            whole_spec(G * NL, D),
            vec_spec,
            whole_spec(D, 3 * D),
            whole_spec(D, D),
            whole_spec(D, FF),
            whole_spec(FF, D),
        ],
        [
            shape(lat_rows, D, BF16),
            shape(lat_rows, D, BF16),
            shape(G * NL, D, F32),
            shape(VEC_ROWS, D, F32),
            shape(D, 3 * D, BF16),
            shape(D, D, BF16),
            shape(D, FF, BF16),
            shape(FF, D, BF16),
        ],
        [
            pltpu.VMEM((PACK, PACK), BF16),
            pltpu.VMEM((NL, 128), jnp.int32),
            pltpu.VMEM((LAT_STEP, D), F32),
            pltpu.VMEM((LAT_STEP, 1), F32),
            pltpu.VMEM((LAT_STEP, D), BF16),
            pltpu.VMEM((LAT_STEP, 3 * D), BF16),
            pltpu.VMEM((PER_STEP * TILES * 2, NL, PACK), BF16),
            pltpu.VMEM((LAT_STEP, D), BF16),
            pltpu.VMEM((LAT_STEP, D), F32),
            pltpu.VMEM((LAT_STEP, D), F32),
            pltpu.VMEM((LAT_STEP, 1), F32),
            pltpu.VMEM((LAT_STEP, D), BF16),
            pltpu.VMEM((LAT_STEP, D), F32),
            pltpu.VMEM((LAT_STEP, D), BF16),
            pltpu.VMEM((LAT_STEP, D), BF16),
            pltpu.VMEM((LAT_STEP, 3 * D), BF16),
            pltpu.VMEM((NL, D), F32),
            pltpu.VMEM((NL, D), F32),
            pltpu.VMEM((D, 3 * D), F32),
            pltpu.VMEM((D, D), F32),
            pltpu.VMEM((D, FF), F32),
            pltpu.VMEM((FF, D), F32),
        ],
        250 * 10**9,
    )(cuts, after, cotangent, wproj, wso, wup, wdn, vectors)

    dinput, glat, gq, gkv, go, cross_small = kernel_call(
        cross_backward_kernel,
        steps,
        [
            rows_spec(IN_STEP, CIN),
            rows_spec(IN_STEP, 2 * D),
            rows_spec(LAT_STEP, D),
            rows_spec(lse_rows, PACK),
            rows_spec(LAT_STEP, D),
            whole_spec(G * NL, D),
            whole_spec(G * NL, D),
            whole_spec(G * NL, D),
            whole_spec(D, D),
            whole_spec(CIN, 2 * D),
            whole_spec(D, D),
            vec_spec,
        ],
        [
            rows_spec(IN_STEP, CIN),
            whole_spec(G * NL, D),
            whole_spec(D, D),
            whole_spec(CIN, 2 * D),
            whole_spec(D, D),
            vec_spec,
        ],
        [
            shape(in_rows, CIN, F32),
            shape(G * NL, D, BF16),
            shape(D, D, BF16),
            shape(CIN, 2 * D, BF16),
            shape(D, D, BF16),
            shape(VEC_ROWS, D, F32),
        ],
        [
            pltpu.VMEM((PACK, PACK), BF16),
            pltpu.VMEM((IN_G, 128), jnp.int32),
            pltpu.VMEM((IN_STEP, CIN), BF16),
            pltpu.VMEM((IN_STEP, CIN), F32),
            pltpu.VMEM((IN_STEP, 1), F32),
            pltpu.VMEM((LAT_STEP, D), BF16),
            pltpu.VMEM((IN_G, D), F32),
            pltpu.VMEM((IN_G, D), F32),
            pltpu.VMEM((IN_STEP, 2 * D), BF16),
            pltpu.VMEM((G * NL, D), F32),
            pltpu.VMEM((CIN, 2 * D), F32),
            pltpu.VMEM((D, D), F32),
        ],
        120 * 10**9,
    )(
        cuts,
        inputs,
        keyval,
        cross_mix,
        lse,
        dcross,
        query,
        latent_full,
        glat,
        wq,
        wkv,
        wo,
        vectors,
    )

    small = lax.psum(middle_small + cross_small, ("wide", "narrow"))
    flat = small.reshape(-1)

    def part(row, size, offset=0):
        return flat[row * D + offset : row * D + offset + size]

    return (
        latents_out,
        dinput,
        scatter(glat),
        part(ROW_QGAIN, D),
        part(ROW_QSHIFT, D),
        part(ROW_SOURCE, CIN),
        part(ROW_SOURCE, CIN, CIN),
        scatter(gq),
        part(ROW_QBIAS, D),
        scatter(gkv),
        part(ROW_VBIAS, D),
        scatter(go),
        part(ROW_COBIAS, D),
        part(ROW_SGAIN, D),
        part(ROW_SSHIFT, D),
        scatter(gproj),
        part(ROW_SQBIAS, D),
        part(ROW_SVBIAS, D),
        scatter(gso),
        part(ROW_SOBIAS, D),
        part(ROW_FGAIN, D),
        part(ROW_FSHIFT, D),
        scatter(gup),
        part(ROW_UBIAS, FF),
        scatter(gdn),
        part(ROW_DBIAS, D),
    )


def solution(mesh):
    rows = P(("wide", "narrow"), None)
    flat = P(("wide", "narrow"))
    block = P("wide", "narrow")
    copied = P()
    return jax.shard_map(
        local,
        mesh=mesh,
        in_specs=(
            rows,
            flat,
            flat,
            rows,
            block,
            copied,
            copied,
            copied,
            copied,
            block,
            copied,
            block,
            copied,
            block,
            copied,
            copied,
            copied,
            block,
            copied,
            copied,
            block,
            copied,
            copied,
            copied,
            block,
            copied,
            block,
            copied,
        ),
        out_specs=(
            rows,
            rows,
            block,
            copied,
            copied,
            copied,
            copied,
            block,
            copied,
            block,
            copied,
            block,
            copied,
            copied,
            copied,
            block,
            copied,
            copied,
            block,
            copied,
            copied,
            copied,
            block,
            copied,
            block,
            copied,
        ),
        check_vma=False,
    )
```

time: 4000 us -> 1950 us (0.49)
  matrix products: 1330 us -> 0 us
  Pallas kernels: 0 us -> 1040 us
  waiting for transfers between devices: 1360 us -> 621 us
  local copies, waits for them, and re-layouts: 615 us -> 18.4 us
  other arithmetic: 414 us -> 11.6 us
    dot_general x229 -> x0, matrix products: 1330 us -> none  [the longest x24 237 us: attend_backward(): jnp.einsum('gqhd,gkhd->ghqk', gheads, vheads, preferred_element_type=jnp....]
    pallas_call x0 -> x3, Pallas kernels: none -> 1040 us  [the longest x1 564 us: local(): kernel_call(middle_kernel, steps, [rows_spec(LAT_STEP, D), rows_spec(LAT_...]
    reduce_scatter x48 -> x16, waiting for transfers between devices: 1350 us -> 616 us  [the longest x8 545 us: scatter(): rows = lax.psum_scatter(total, 'wide', scatter_dimension=0, tiled=True)]
    dynamic_slice x168 -> x0, local copies, waits for them, and re-layouts: 184 us -> none  [blocked(): results = lax.map(function, pieces)]
    convert_element_type x41 -> x8, other arithmetic: 187 us -> 11.2 us  [scatter(): lax.psum_scatter(rows, 'narrow', scatter_dimension=1, tiled=True)]
    dynamic_update_slice x168 -> x0, local copies, waits for them, and re-layouts: 168 us -> none  [blocked(): results = lax.map(function, pieces)]
    reduce_sum x55 -> x2, other arithmetic: 165 us -> 0.44 us  [the longest x1 0.23 us: local(): jnp.sum(input_segments.reshape(groups, IN_G, 1) < marks, 1, dtype=jnp.int32)]
    slice x29 -> x2, local copies, waits for them, and re-layouts: 88.8 us -> 1.2 us  [part(): return flat[row * D + offset:row * D + offset + size]]
  transfers between devices with their start and end apart: 52 -> 20, of which waited for: 35 -> 15; matrix products, arithmetic and copies ran while one was open for 54% -> 1% of each run, Pallas kernels for 0% -> 24%
where the time goes in v1:
time: 1950 us; the launch traced here: 1940 us
  Pallas kernels  1040 us (53%)
  waiting for transfers between devices  621 us (32%)
  blocking collectives  241 us (12%)
    pallas_call x1, Pallas kernels, local(): kernel_call(middle_kernel, steps, [rows_spec(LAT_STEP, D), rows_spec(LAT_...  564 us
    reduce_scatter x8, waiting for transfers between devices, scatter(): rows = lax.psum_scatter(total, 'wide', scatter_dimension=0, tiled=True)  545 us
    pallas_call x1, Pallas kernels, local(): kernel_call(cross_backward_kernel, steps, [rows_spec(IN_STEP, CIN), rows_...  255 us
    pallas_call x1, Pallas kernels, local(): kernel_call(cross_forward_kernel, steps, [rows_spec(IN_STEP, CIN), whole_...  218 us
    all_gather x4, blocking collectives, gather(): lax.all_gather(lax.all_gather(shard, 'narrow', axis=1, tiled=True), 'wide...  178 us
    reduce_scatter x8, waiting for transfers between devices, scatter(): lax.psum_scatter(rows, 'narrow', scatter_dimension=1, tiled=True)  71.1 us
  transfers between devices with their start and end apart: 20, of which 15 were waited for; matrix products, arithmetic and copies ran while one was open for 1% of the time, Pallas kernels for 24%

profile of v1, /device:TPU:0, one launch (start us, length us, event | category | flops | bytes accessed | tf_op | source)
XLA Modules:
  0.0 1944.1 jit_solution(11587808633568499332)
XLA Ops:
  7.2 3.7 all_gather.48
  11.1 3.5 all_gather.56
  14.6 3.7 all_gather.60
  18.3 3.6 all_gather.62
  22.0 0.7 lt.34
  22.8 0.9 dynamic-update-slice
  23.6 0.9 dynamic-update-slice.1
  24.5 0.8 dynamic-update-slice.2
  25.3 0.8 dynamic-update-slice.3
  26.2 0.9 dynamic-update-slice.4
  27.0 0.9 dynamic-update-slice.5
  27.9 0.9 dynamic-update-slice.6
  28.7 0.9 dynamic-update-slice.7
  29.6 0.9 dynamic-update-slice.8
  30.4 0.9 dynamic-update-slice.9
  31.3 0.9 dynamic-update-slice.10
  32.2 0.9 dynamic-update-slice.11
  33.0 0.9 dynamic-update-slice.12
  33.9 0.9 dynamic-update-slice.13
  34.7 0.9 dynamic-update-slice.14
  35.6 0.9 dynamic-update-slice.15
  36.5 0.6 reshape.82.vec_ref
  37.1 2.2 all_gather.50
  39.3 2.2 all_gather.52
  41.6 2.2 all_gather.54
  43.8 2.2 all_gather.58
  46.0 0.8 lt.30
  47.3 0.7 copy.58.cuts_ref
  48.0 48.7 %all_gather.55.wo_ref = bf16[512,512]{1,0:T(8,128)(2,1)} all-gather(bf16[32,512]{1,0:T(8,128)(2,1)S(1)} %all_gather.54), channel_id=1, replica_groups=mesh['wide'=16,'narrow'=2] {'wide'}, dimensions={0}, use_global_device_ids=true | all-gather | bytes 557056 | tf_op jit(solution)/shard_map/all_gather | solution.py:659
  96.6 42.9 %all_gather.53.wkv_ref = bf16[256,1024]{1,0:T(8,128)(2,1)} all-gather(bf16[16,1024]{1,0:T(8,128)(2,1)S(1)} %all_gather.52), channel_id=1, replica_groups=mesh['wide'=16,'narrow'=2] {'wide'}, dimensions={0}, use_global_device_ids=true | all-gather | bytes 557056 | tf_op jit(solution)/shard_map/all_gather | solution.py:659
  139.5 45.2 %all_gather.51.wq_ref = bf16[512,512]{1,0:T(8,128)(2,1)} all-gather(bf16[32,512]{1,0:T(8,128)(2,1)S(1)} %all_gather.50), channel_id=1, replica_groups=mesh['wide'=16,'narrow'=2] {'wide'}, dimensions={0}, use_global_device_ids=true | all-gather | bytes 557056 | tf_op jit(solution)/shard_map/all_gather | solution.py:659
  184.7 41.7 %all_gather.59.wso_ref = bf16[512,512]{1,0:T(8,128)(2,1)} all-gather(bf16[32,512]{1,0:T(8,128)(2,1)S(1)} %all_gather.58), channel_id=1, replica_groups=mesh['wide'=16,'narrow'=2] {'wide'}, dimensions={0}, use_global_device_ids=true | all-gather | bytes 557056 | tf_op jit(solution)/shard_map/all_gather | solution.py:659
  226.4 218.1 %shard_map.467 = (f32[6144,512]{1,0:T(8,128)}, bf16[6144,512]{1,0:T(8,128)(2,1)}, bf16[12288,1024]{1,0:T(8,128)(2,1)}, f32[384,256]{1,0:T(8,128)}, bf16[1024,512]{1,0:T(8,128)(2,1)}) custom-call(s32[24,8]{1,0:T(8,128)} %copy.58.cuts_ref, bf16[12288,256]{1,0:T(8,128)(2,1)} %inputs_ref.3, bf16[1024,512]{1,0:T(8,128)(2,1)} %all-gather.5.cloned.1.call-done.latent_ref, ...), custom_call_target="tpu_custom_call" | custom-call | flops 60000002048 | bytes 104857600 | tf_op jit(solution)/shard_map/pallas_call | solution.py:747
  444.6 563.9 %shard_map.468 = (bf16[6144,512]{1,0:T(8,128)(2,1)}, bf16[6144,512]{1,0:T(8,128)(2,1)}, f32[1024,512]{1,0:T(8,128)}, f32[24,512]{1,0:T(8,128)}, bf16[512,1536]{1...) custom-call(s32[24,8]{1,0:T(8,128)} %copy.58.cuts_ref, ...), custom_call_target="tpu_custom_call" | custom-call | flops 249999998976 | bytes 104857600 | tf_op jit(solution)/shard_map/pallas_call | solution.py:780
  1008.6 255.2 %shard_map.469 = (f32[12288,256]{1,0:T(8,128)}, bf16[1024,512]{1,0:T(8,128)(2,1)}, bf16[512,512]{1,0:T(8,128)(2,1)}, bf16[256,1024]{1,0:T(8,128)(2,1)}, bf16[512,512]{1,0:T(8,128)(2,1)}, /*index=5*/f32[24,512]{1,0:T(8,128)}) custom-call(s32[24,8]{1,0:T(8,128)} %copy.58.cuts_ref, bf16[12288,256]{1,0:T(8,128)(2,1)} %inputs_ref.3, ...), custom_call_target="tpu_custom_call" | custom-call | flops 120000004096 | bytes 104857600 | tf_op jit(solution)/shard_map/pallas_call | solution.py:839
  1263.9 0.7 reduce-scatter.25.cloned.1.call-update
  1264.6 0.7 reduce-scatter.21.cloned.1.call-update
  1265.4 0.7 reduce-scatter.17.cloned.1.call-update
  1266.7 0.7 reduce-scatter.45.cloned.1.call-update
  1268.1 0.7 reduce-scatter.39.cloned.1.call-update
  1268.8 68.8 %reduce-scatter.29.cloned.1.call-done = bf16[32,512]{1,0:T(8,128)(2,1)} async-done(((bf16[512,512]{1,0:T(8,128)(2,1)}), bf16[32,512]{1,0:T(8,128)(2,1)}) %reduce-scatter.29.cloned.1.call-update) | async-done | bytes 32784 | tf_op jit(solution)/shard_map/reduce_scatter | solution.py:665
  1337.6 75.1 %reduce-scatter.25.cloned.1.call-done = bf16[16,1024]{1,0:T(8,128)(2,1)} async-done(((bf16[256,1024]{1,0:T(8,128)(2,1)}), bf16[16,1024]{1,0:T(8,128)(2,1)}) %reduce-scatter.25.cloned.1.call-update) | async-done | bytes 32784 | tf_op jit(solution)/shard_map/reduce_scatter | solution.py:665
  1412.8 75.2 %reduce-scatter.21.cloned.1.call-done = bf16[32,512]{1,0:T(8,128)(2,1)} async-done(((bf16[512,512]{1,0:T(8,128)(2,1)}), bf16[32,512]{1,0:T(8,128)(2,1)}) %reduce-scatter.21.cloned.1.call-update) | async-done | bytes 32784 | tf_op jit(solution)/shard_map/reduce_scatter | solution.py:665
  1488.0 76.2 %reduce-scatter.17.cloned.1.call-done = bf16[64,512]{1,0:T(8,128)(2,1)} async-done(((bf16[1024,512]{1,0:T(8,128)(2,1)}), bf16[64,512]{1,0:T(8,128)(2,1)}) %reduce-scatter.17.cloned.1.call-update) | async-done | bytes 65552 | tf_op jit(solution)/shard_map/reduce_scatter | solution.py:665
  1564.3 126.4 %reduce-scatter.33.cloned.1.call-done = bf16[32,1536]{1,0:T(8,128)(2,1)} async-done(((bf16[512,1536]{1,0:T(8,128)(2,1)}), bf16[32,1536]{1,0:T(8,128)(2,1)}) %reduce-scatter.33.cloned.1.call-update) | async-done | bytes 98320 | tf_op jit(solution)/shard_map/reduce_scatter | solution.py:665
  1690.8 81.7 %reduce-scatter.45.cloned.1.call-done = bf16[128,512]{1,0:T(8,128)(2,1)} async-done(((bf16[2048,512]{1,0:T(8,128)(2,1)}), bf16[128,512]{1,0:T(8,128)(2,1)}) %reduce-scatter.45.cloned.1.call-update) | async-done | bytes 131088 | tf_op jit(solution)/shard_map/reduce_scatter | solution.py:665
  1772.7 38.8 %psum.7 = f32[24,512]{1,0:T(8,128)S(1)} all-reduce(f32[24,512]{1,0:T(8,128)S(1)} %add.47), channel_id=1, replica_groups=mesh['wide'=16,'narrow'=2] {'wide','narrow'}, use_global_device_ids=true, to_apply=%region_4.0 | all-reduce | flops 12288 | bytes 98304 | tf_op jit(solution)/shard_map/psum | solution.py:903
  1811.5 41.4 %reduce-scatter.41.cloned.1.call-done = bf16[32,2048]{1,0:T(8,128)(2,1)} async-done(((bf16[512,2048]{1,0:T(8,128)(2,1)}), bf16[32,2048]{1,0:T(8,128)(2,1)}) %reduce-scatter.41.cloned.1.call-update) | async-done | bytes 131088 | tf_op jit(solution)/shard_map/reduce_scatter | solution.py:665
  1854.8 5.2 reduce-scatter.39.cloned.1.call-done
  1860.0 1.3 convert_element_type.46
  1861.3 9.4 reduce-scatter.31.cloned.1.call-done
  1870.7 1.3 convert_element_type.44
  1872.0 9.4 reduce-scatter.27.cloned.1.call-done
  1881.4 1.3 convert_element_type.43
  1882.8 9.4 reduce-scatter.23.cloned.1.call-done
  1892.2 1.3 convert_element_type.42
  1893.5 9.4 reduce-scatter.19.cloned.1.call-done
  1902.9 1.4 convert_element_type.41
  1904.3 9.4 reduce-scatter.35.cloned.1.call-done
  1913.7 1.4 convert_element_type.45
  1915.2 9.5 reduce-scatter.47.cloned.1.call-done
  1924.7 1.5 convert_element_type.48
  1926.2 9.3 reduce-scatter.43.cloned.1.call-done
  1935.6 1.5 convert_element_type.47
  (57 shorter events, 4.4 us)
Async XLA Ops:
  7.2 219.2 %all-gather.5.cloned.1.call-start = ((), (), s32[]{:S(2)}) async-start(), calls=%async_computation.16 | async-start | bytes 1114112 | tf_op jit(solution)/shard_map/all_gather | solution.py:659
  11.0 433.6 %all-gather.7.cloned.1.call-start = ((), (), s32[]{:S(2)}) async-start(), calls=%async_computation.17 | async-start | bytes 1671168 | tf_op jit(solution)/shard_map/all_gather | solution.py:659
  14.5 430.1 %all-gather.9.cloned.1.call-start = ((), (), s32[]{:S(2)}) async-start(), calls=%async_computation.18 | async-start | bytes 2228224 | tf_op jit(solution)/shard_map/all_gather | solution.py:659
  18.3 426.3 %all-gather.11.cloned.1.call-start = ((), (), s32[]{:S(2)}) async-start(), calls=%async_computation.19 | async-start | bytes 2228224 | tf_op jit(solution)/shard_map/all_gather | solution.py:659
  21.9 1246.1 %reduce-scatter.37.cloned.1.call-start = ((), (), s32[]{:S(2)}) async-start(), calls=%async_computation.30 | async-start | bytes 557056 | tf_op jit(solution)/shard_map/reduce_scatter | solution.py:665
  1008.6 329.0 %reduce-scatter.29.cloned.1.call-start = ((), (), s32[]{:S(2)}) async-start(), calls=%async_computation.26 | async-start | bytes 557056 | tf_op jit(solution)/shard_map/reduce_scatter | solution.py:665
  1263.8 508.8 %copy-start = (f32[24,512]{1,0:T(8,128)S(1)}, f32[24,512]{1,0:T(8,128)}, u32[]{:S(2)}) copy-start(f32[24,512]{1,0:T(8,128)} %get-tuple-element.55) | copy-start | bytes 147460
  1263.8 508.8 %copy-start.1 = (f32[24,512]{1,0:T(8,128)S(1)}, f32[24,512]{1,0:T(8,128)}, u32[]{:S(2)}) copy-start(f32[24,512]{1,0:T(8,128)} %get-tuple-element.56) | copy-start | bytes 147460
  1263.9 148.9 %reduce-scatter.25.cloned.1.call-start = ((), (), s32[]{:S(2)}) async-start(), calls=%async_computation.24 | async-start | bytes 557056 | tf_op jit(solution)/shard_map/reduce_scatter | solution.py:665
  1264.6 223.3 %reduce-scatter.21.cloned.1.call-start = ((), (), s32[]{:S(2)}) async-start(), calls=%async_computation.22 | async-start | bytes 557056 | tf_op jit(solution)/shard_map/reduce_scatter | solution.py:665
  1265.4 298.9 %reduce-scatter.17.cloned.1.call-start = ((), (), s32[]{:S(2)}) async-start(), calls=%async_computation.20 | async-start | bytes 1114112 | tf_op jit(solution)/shard_map/reduce_scatter | solution.py:665
  1266.1 424.7 %reduce-scatter.33.cloned.1.call-start = ((), (), s32[]{:S(2)}) async-start(), calls=%async_computation.28 | async-start | bytes 1671168 | tf_op jit(solution)/shard_map/reduce_scatter | solution.py:665
  1266.7 505.9 %reduce-scatter.45.cloned.1.call-start = ((), (), s32[]{:S(2)}) async-start(), calls=%async_computation.34 | async-start | bytes 2228224 | tf_op jit(solution)/shard_map/reduce_scatter | solution.py:665
  1267.4 585.5 %reduce-scatter.41.cloned.1.call-start = ((), (), s32[]{:S(2)}) async-start(), calls=%async_computation.32 | async-start | bytes 2228224 | tf_op jit(solution)/shard_map/reduce_scatter | solution.py:665
  1268.0 592.0 %reduce-scatter.39.cloned.1.call-start = ((), (), s32[]{:S(2)}) async-start(), calls=%async_computation.31 | async-start | bytes 49152 | tf_op jit(solution)/shard_map/reduce_scatter | solution.py:666
  1268.7 602.0 %reduce-scatter.31.cloned.1.call-start = ((), (), s32[]{:S(2)}) async-start(), calls=%async_computation.27 | async-start | bytes 49152 | tf_op jit(solution)/shard_map/reduce_scatter | solution.py:666
  1337.6 543.8 %reduce-scatter.27.cloned.1.call-start = ((), (), s32[]{:S(2)}) async-start(), calls=%async_computation.25 | async-start | bytes 49152 | tf_op jit(solution)/shard_map/reduce_scatter | solution.py:666
  1412.7 479.4 %reduce-scatter.23.cloned.1.call-start = ((), (), s32[]{:S(2)}) async-start(), calls=%async_computation.23 | async-start | bytes 49152 | tf_op jit(solution)/shard_map/reduce_scatter | solution.py:666
  1488.0 414.9 %reduce-scatter.19.cloned.1.call-start = ((), (), s32[]{:S(2)}) async-start(), calls=%async_computation.21 | async-start | bytes 98304 | tf_op jit(solution)/shard_map/reduce_scatter | solution.py:666
  1564.3 349.5 %reduce-scatter.35.cloned.1.call-start = ((), (), s32[]{:S(2)}) async-start(), calls=%async_computation.29 | async-start | bytes 147456 | tf_op jit(solution)/shard_map/reduce_scatter | solution.py:666
  1690.8 233.9 %reduce-scatter.47.cloned.1.call-start = ((), (), s32[]{:S(2)}) async-start(), calls=%async_computation.35 | async-start | bytes 196608 | tf_op jit(solution)/shard_map/reduce_scatter | solution.py:666
  1772.6 163.0 %reduce-scatter.43.cloned.1.call-start = ((), (), s32[]{:S(2)}) async-start(), calls=%async_computation.33 | async-start | bytes 196608 | tf_op jit(solution)/shard_map/reduce_scatter | solution.py:666
Sparse Core Ops, SparseCore 0:
  11.1 59.2 all-gather.4
  73.2 59.1 all-gather.6
  135.2 63.7 all-gather.8
  201.6 59.8 all-gather.10
  1008.7 72.9 reduce-scatter.36
  1264.0 73.5 reduce-scatter.28
  1339.8 72.8 reduce-scatter.24
  1415.0 72.8 reduce-scatter.20
  1490.2 73.9 reduce-scatter.16
  1569.6 121.0 reduce-scatter.32
  1693.1 79.3 reduce-scatter.44
  1774.8 78.1 reduce-scatter.40
  1855.2 4.7 reduce-scatter.38
  1862.1 8.5 reduce-scatter.30
  1872.8 8.5 reduce-scatter.26
  1883.6 8.5 reduce-scatter.22
  1894.3 8.5 reduce-scatter.18
  1905.0 8.6 reduce-scatter.34
  1916.0 8.6 reduce-scatter.46
  1926.9 8.6 reduce-scatter.42

commit v2 on v1

v2 whole, which is shorter than its diff:
```python
import functools

import jax
import jax.numpy as jnp
from jax import lax
from jax.experimental import pallas as pl
from jax.experimental.pallas import tpu as pltpu
from jax.sharding import PartitionSpec as P

D = 512
HEADS = 16
HD = 32
FF = 2048
CIN = 256
G = 4
NL = 256
IN_G = 512
SEGS = 4
QT = 32
PACK = 256
TILES = NL // QT
SELF_GROUPS = 2
SELF_ROWS = SELF_GROUPS * NL
CROSS_GROUPS = 4
LAT_STEP = CROSS_GROUPS * NL
IN_STEP = CROSS_GROUPS * IN_G
UNITS = 4
WIDTHS = (128, 192, 256, 384, 512)

F32 = jnp.float32
BF16 = jnp.bfloat16
NEG_FILL = -1e30
EPSILON = 1e-05
SCALE = HD**-0.5
LOG2E = 1.4426950408889634
SCALE2 = SCALE * LOG2E
VMEM_BYTES = 60 * 1024 * 1024

TAIL_RATE = 0.28
TAIL_POLY = (
    0.1165209849818009,
    0.06749547174407416,
    0.2689133347091787,
    -0.23699737809142182,
    0.38987640062523105,
    -0.10580882324798475,
)

ROW_QGAIN, ROW_QSHIFT, ROW_SOURCE, ROW_QBIAS, ROW_VBIAS, ROW_COBIAS = range(6)
ROW_SGAIN, ROW_SSHIFT, ROW_SQBIAS, ROW_SVBIAS, ROW_SOBIAS = range(6, 11)
ROW_FGAIN, ROW_FSHIFT, ROW_UBIAS, ROW_DBIAS = 11, 12, 13, 17
VEC_ROWS = 24

CHUNKS = 16
HALVES = 2
CROSS_MATS = ((G * NL, D), (D, D), (CIN, 2 * D), (D, D))
MIDDLE_MATS = ((D, 3 * D), (D, D), (D, FF), (FF, D))


def slab_place(mats, at):
    sizes = [rows // CHUNKS * (columns // (HALVES * PACK)) for rows, columns in mats]
    return sum(sizes[:at]), mats[at][0] // CHUNKS, sum(sizes)


LATENT, WQ, WKV, WO = (slab_place(CROSS_MATS, at)[:2] for at in range(4))
WPROJ, WSO, WUP, WDN = (slab_place(MIDDLE_MATS, at)[:2] for at in range(4))
CROSS_SLAB = slab_place(CROSS_MATS, 0)[2]
MIDDLE_SLAB = slab_place(MIDDLE_MATS, 0)[2]


def dot_plain(left, right):
    return lax.dot_general(left, right, (((1,), (0,)), ((), ())), preferred_element_type=F32)


def dot_first(left, right):
    return lax.dot_general(left, right, (((0,), (0,)), ((), ())), preferred_element_type=F32)


def dot_last(left, right):
    return lax.dot_general(left, right, (((1,), (1,)), ((), ())), preferred_element_type=F32)


def over_rows(total, chunk, body):
    def step(index, carry):
        body(pl.ds(pl.multiple_of(index * chunk, chunk), chunk))
        return carry

    lax.fori_loop(0, total // chunk, step, 0, unroll=8)


def norm_forward(rows, gain, shift):
    centered = rows - jnp.mean(rows, -1, keepdims=True)
    rscale = lax.rsqrt(jnp.mean(centered * centered, -1, keepdims=True) + EPSILON)
    normed = centered * rscale
    return normed * gain + shift, normed, rscale


def norm_backward(grad, normed, rscale, gain):
    dnormed = grad * gain
    return rscale * (
        dnormed
        - jnp.mean(dnormed, -1, keepdims=True)
        - normed * jnp.mean(dnormed * normed, -1, keepdims=True)
    )


def column_sum(rows):
    return jnp.sum(rows, 0, keepdims=True)


def gelu_pair(hidden):
    size = jnp.abs(hidden)
    ratio = 1.0 / (1.0 + TAIL_RATE * size)
    bell = jnp.exp2(hidden * hidden * (-0.5 * LOG2E))
    poly = TAIL_POLY[-1] * ratio
    for coefficient in TAIL_POLY[-2::-1]:
        poly = (poly + coefficient) * ratio
    tail = poly * bell
    cdf = jnp.where(hidden >= 0.0, 1.0 - tail, tail)
    return hidden * cdf, cdf + hidden * bell * 0.3989422804014327


def fill_block_mask(mask_ref):
    row_head = lax.broadcasted_iota(jnp.int32, (PACK, PACK), 0) // QT
    lane_head = lax.broadcasted_iota(jnp.int32, (PACK, PACK), 1) // HD
    mask_ref[...] = jnp.where(row_head == lane_head, 1.0, 0.0).astype(BF16)


def block_diagonal(rows, mask):
    return jnp.concatenate([rows] * (PACK // QT), 0) * mask


def take_diagonal(full):
    lane = lax.broadcasted_iota(jnp.int32, (QT, 128), 1)
    columns = []
    for half in range(2):
        base = 128 * half
        picked = full[base : base + QT, base : base + 128]
        for head in range(1, 4):
            row = base + QT * head
            picked = jnp.where(
                lane >= HD * head, full[row : row + QT, base : base + 128], picked
            )
        columns.append(picked)
    return jnp.concatenate(columns, 1)


def segment_at(cuts, place):
    return sum((place >= cut).astype(jnp.int32) for cut in cuts)


def pick(index, values):
    result = values[0]
    for at in range(1, len(values)):
        result = jnp.where(index == at, values[at], result)
    return result


def in_widths(needed, body):
    smaller = 0
    for width in WIDTHS:

        @pl.when((needed > smaller) & (needed <= width))
        def _(width=width):
            body(width)

        smaller = width


def query_segments(query_cuts, tile):
    lane = lax.broadcasted_iota(jnp.int32, (1, PACK), 1) % QT
    return segment_at(query_cuts, tile * QT + lane)


def allowed_pairs(key_seg, query_seg):
    return jnp.concatenate([key_seg, key_seg], 1) == query_seg


def softmax_rows(scores, allowed):
    scores = jnp.where(allowed, scores, NEG_FILL)
    top = jnp.max(scores, 0, keepdims=True)
    powers = jnp.exp2((scores - top) * SCALE2)
    total = jnp.sum(powers, 0, keepdims=True)
    return (powers * (1.0 / total)).astype(BF16), top * SCALE2 + jnp.log2(total)


def score_grads(probs, dprobs):
    weighted = probs * dprobs
    delta = jnp.sum(weighted, 0, keepdims=True)
    return (weighted - probs * delta).astype(BF16)


def half(part):
    return slice(PACK * part, PACK * part + PACK)


def slab_part(slab_ref, place, side, piece):
    offset, rows = place
    part = slab_ref[:, side, offset + piece * rows : offset + piece * rows + rows, :]
    return part.reshape(CHUNKS * rows, PACK)


def slab_matrix(slab_ref, place, pieces):
    return jnp.concatenate(
        [
            slab_part(slab_ref, place, piece // (pieces // HALVES), piece % (pieces // HALVES))
            for piece in range(pieces)
        ],
        1,
    )


def store_slab(slab_ref, place, matrix):
    offset, rows = place
    pieces = matrix.shape[1] // PACK
    for piece in range(pieces):
        side, inner = piece // (pieces // HALVES), piece % (pieces // HALVES)
        start = offset + inner * rows
        part = matrix[:, piece * PACK : piece * PACK + PACK].astype(BF16)
        slab_ref[:, side, start : start + rows, :] = part.reshape(CHUNKS, rows, PACK)


def latent_cuts(cuts_ref, group):
    return [cuts_ref[group, 4 + at] for at in range(SEGS - 1)]


def fill_cross_segments(seg_ref, cuts_ref, step):
    place = lax.broadcasted_iota(jnp.int32, (IN_G, 128), 0)
    for member in range(CROSS_GROUPS):
        key_cuts = [cuts_ref[step * CROSS_GROUPS + member, at] for at in range(SEGS - 1)]
        seg_ref[member * IN_G : member * IN_G + IN_G, :] = segment_at(key_cuts, place)


def cross_units(plan_ref, cuts_ref, seg_ref, step, batch, width):
    units = []
    for at in range(UNITS):
        packed = plan_ref[step, batch * UNITS + at]
        slot = packed // 1024
        start = pl.multiple_of(jnp.minimum(packed % 1024, IN_G - width), 16)
        member = slot // TILES
        tile = slot % TILES
        keys = pl.ds(pl.multiple_of(member * IN_G + start, 16), width)
        cuts = latent_cuts(cuts_ref, step * CROSS_GROUPS + member)
        allowed = allowed_pairs(seg_ref[keys, :], query_segments(cuts, tile))
        units.append((slot, pl.ds(pl.multiple_of(slot * QT, QT), QT), keys, allowed))
    return units


def batch_needed(plan_ref, step, batch):
    return plan_ref[step, CROSS_GROUPS * TILES + batch]


def plan_tiles(in_cuts, lat_cuts):
    groups = in_cuts.shape[0]
    tile = jnp.arange(TILES, dtype=jnp.int32) * QT
    first = jnp.sum(tile[None, :, None] >= lat_cuts[:, None, :], -1, dtype=jnp.int32)
    last = jnp.sum(tile[None, :, None] + (QT - 1) >= lat_cuts[:, None, :], -1, dtype=jnp.int32)
    starts = jnp.concatenate([jnp.zeros((groups, 1), jnp.int32), in_cuts], 1)
    ends = jnp.concatenate([in_cuts, jnp.full((groups, 1), IN_G, jnp.int32)], 1)
    segment = jnp.arange(SEGS, dtype=jnp.int32)
    low = jnp.sum(jnp.where(first[..., None] == segment, starts[:, None, :], 0), -1) // 16 * 16
    high = jnp.sum(jnp.where(last[..., None] == segment, ends[:, None, :], 0), -1)
    count = CROSS_GROUPS * TILES
    low = low.reshape(-1, count)
    needed = high.reshape(-1, count) - low
    slot = jnp.arange(count, dtype=jnp.int32)
    earlier = slot[:, None] < slot[None, :]
    mine, other = needed[:, None, :], needed[:, :, None]
    rank = jnp.sum((other < mine) | ((other == mine) & earlier), 1, dtype=jnp.int32)
    place = rank[:, None, :] == slot[:, None]
    packed = jnp.sum(jnp.where(place, (slot * 1024 + low)[:, None, :], 0), -1)
    batches = jnp.arange(count // UNITS, dtype=jnp.int32)[:, None]
    inside = rank[:, None, :] // UNITS == batches
    widest = jnp.max(jnp.where(inside, needed[:, None, :], 0), -1)
    return jnp.concatenate([packed, widest], 1).astype(jnp.int32)


def cross_forward_kernel(
    cuts_ref,
    plan_ref,
    source_ref,
    slab_ref,
    vec_ref,
    after_ref,
    mix_ref,
    kv_ref,
    lse_ref,
    query_ref,
    mask_ref,
    seg_ref,
):
    step = pl.program_id(0)

    @pl.when(step == 0)
    def _():
        fill_block_mask(mask_ref)
        low, _, _ = norm_forward(
            slab_matrix(slab_ref, LATENT, 2).astype(F32),
            vec_ref[ROW_QGAIN : ROW_QGAIN + 1, :],
            vec_ref[ROW_QSHIFT : ROW_QSHIFT + 1, :],
        )
        query = dot_plain(low.astype(BF16), slab_matrix(slab_ref, WQ, 2))
        query_ref[...] = (query + vec_ref[ROW_QBIAS : ROW_QBIAS + 1, :]).astype(BF16)

    wkv = slab_matrix(slab_ref, WKV, 4)
    kv_ref[:, :D] = dot_plain(source_ref[...], wkv[:, :D]).astype(BF16)
    kv_ref[:, D:] = (
        dot_plain(source_ref[...], wkv[:, D:]) + vec_ref[ROW_VBIAS : ROW_VBIAS + 1, :]
    ).astype(BF16)

    fill_cross_segments(seg_ref, cuts_ref, step)

    def batch_body(batch, carry):
        def window(width):
            units = cross_units(plan_ref, cuts_ref, seg_ref, step, batch, width)
            scores = [
                dot_last(
                    kv_ref[keys, half(part)],
                    block_diagonal(query_ref[rows, half(part)], mask_ref[...]),
                )
                for _, rows, keys, _ in units
                for part in range(2)
            ]
            probs = []
            for at, (slot, _, _, allowed) in enumerate(units):
                for part in range(2):
                    low, lse = softmax_rows(scores[2 * at + part], allowed)
                    probs.append(low)
                    lse_ref[pl.ds(slot * 2 + part, 1), :] = lse
            for at, (_, rows, keys, _) in enumerate(units):
                for part in range(2):
                    full = dot_first(probs[2 * at + part], kv_ref[keys, half(part + 2)])
                    mix_ref[rows, half(part)] = take_diagonal(full).astype(BF16)

        in_widths(batch_needed(plan_ref, step, batch), window)
        return carry

    lax.fori_loop(0, CROSS_GROUPS * TILES // UNITS, batch_body, 0)
    after_ref[...] = (
        slab_matrix(slab_ref, LATENT, 2).astype(F32)
        + dot_plain(mix_ref[...], slab_matrix(slab_ref, WO, 2))
        + vec_ref[ROW_COBIAS : ROW_COBIAS + 1, :]
    )


def middle_kernel(
    cuts_ref,
    after_ref,
    cot_ref,
    slab_ref,
    vec_ref,
    out_ref,
    dcross_ref,
    glat_ref,
    small_ref,
    gslab_ref,
    mask_ref,
    hat1_ref,
    rs1_ref,
    low1_ref,
    triple_ref,
    probs_ref,
    mix_ref,
    res_ref,
    hat2_ref,
    rs2_ref,
    low2_ref,
    dtop_ref,
    dso_ref,
    dmix_ref,
    dtriple_ref,
    aproj_ref,
    aso_ref,
    aup_ref,
    adn_ref,
):
    step = pl.program_id(0)
    last = pl.num_programs(0) - 1

    def vec(row):
        return vec_ref[row : row + 1, :]

    def add_small(row, value):
        small_ref[row : row + 1, :] += value

    @pl.when(step == 0)
    def _():
        fill_block_mask(mask_ref)
        for ref in (glat_ref, small_ref, aproj_ref, aso_ref, aup_ref, adn_ref):
            ref[...] = jnp.zeros(ref.shape, ref.dtype)

    def first_norm(rows):
        low, normed, rscale = norm_forward(after_ref[rows, :], vec(ROW_SGAIN), vec(ROW_SSHIFT))
        low1_ref[rows, :] = low.astype(BF16)
        hat1_ref[rows, :] = normed
        rs1_ref[rows, :] = rscale

    over_rows(SELF_ROWS, 64, first_norm)
    wproj = slab_matrix(slab_ref, WPROJ, 6)
    for block, bias in enumerate((ROW_SQBIAS, None, ROW_SVBIAS)):
        columns = slice(D * block, D * block + D)
        product = dot_plain(low1_ref[...], wproj[:, columns])
        if bias is not None:
            product = product + vec(bias)
        triple_ref[:, columns] = product.astype(BF16)

    def attend_group(member, carry):
        start = pl.multiple_of(member * NL, NL)
        group = pl.ds(start, NL)
        cuts = latent_cuts(cuts_ref, step * SELF_GROUPS + member)
        key_seg = segment_at(cuts, lax.broadcasted_iota(jnp.int32, (NL, 128), 0))
        tiles = [pl.ds(pl.multiple_of(start + tile * QT, QT), QT) for tile in range(TILES)]
        scores = [
            dot_last(
                triple_ref[group, half(part + 2)],
                block_diagonal(triple_ref[rows, half(part)], mask_ref[...]),
            )
            for rows in tiles
            for part in range(2)
        ]
        probs = []
        for tile in range(TILES):
            allowed = allowed_pairs(key_seg, query_segments(cuts, tile))
            for part in range(2):
                low, _ = softmax_rows(scores[2 * tile + part], allowed)
                probs.append(low)
                probs_ref[(member * TILES + tile) * 2 + part] = low
        for tile, rows in enumerate(tiles):
            for part in range(2):
                full = dot_first(probs[2 * tile + part], triple_ref[group, half(part + 4)])
                mix_ref[rows, half(part)] = take_diagonal(full).astype(BF16)
        return carry

    lax.fori_loop(0, SELF_GROUPS, attend_group, 0)

    res_ref[...] = after_ref[...] + dot_plain(mix_ref[...], slab_matrix(slab_ref, WSO, 2)) + vec(ROW_SOBIAS)

    def second_norm(rows):
        low, normed, rscale = norm_forward(res_ref[rows, :], vec(ROW_FGAIN), vec(ROW_FSHIFT))
        low2_ref[rows, :] = low.astype(BF16)
        hat2_ref[rows, :] = normed
        rs2_ref[rows, :] = rscale

    over_rows(SELF_ROWS, 64, second_norm)
    dtop_ref[...] = jnp.zeros(dtop_ref.shape, F32)

    def feed_block(block, carry):
        columns = pl.ds(pl.multiple_of(block * D, D), D)
        offset, height = WUP
        side = block // 2
        wup = jnp.concatenate(
            [
                slab_ref[
                    :,
                    side,
                    pl.ds(pl.multiple_of(offset + (block % 2 * 2 + piece) * height, height), height),
                    :,
                ].reshape(D, PACK)
                for piece in range(2)
            ],
            1,
        )
        offset, height = WDN
        chunks = pl.ds(block * (D // height), D // height)
        wdn = jnp.concatenate(
            [
                slab_ref[chunks, piece, offset : offset + height, :].reshape(D, PACK)
                for piece in range(2)
            ],
            1,
        )
        hidden = dot_plain(low2_ref[...], wup) + vec_ref[pl.ds(ROW_UBIAS + block, 1), :]
        active, slope = gelu_pair(hidden)
        active = active.astype(BF16)
        dhidden = (slope * dot_last(cot_ref[...], wdn)).astype(BF16)
        small_ref[pl.ds(ROW_UBIAS + block, 1), :] += column_sum(dhidden.astype(F32))
        res_ref[...] += dot_plain(active, wdn)
        adn_ref[columns, :] += dot_first(active, cot_ref[...])
        aup_ref[:, columns] += dot_first(low2_ref[...], dhidden)
        dtop_ref[...] += dot_last(dhidden, wup)
        return carry

    lax.fori_loop(0, FF // D, feed_block, 0)

    def after_feed(rows):
        out_ref[rows, :] = (res_ref[rows, :] + vec(ROW_DBIAS)).astype(BF16)
        dtop = dtop_ref[rows, :]
        normed = hat2_ref[rows, :]
        cot = cot_ref[rows, :].astype(F32)
        dafter = cot + norm_backward(dtop, normed, rs2_ref[rows, :], vec(ROW_FGAIN))
        dlow = dafter.astype(BF16)
        res_ref[rows, :] = dafter
        dso_ref[rows, :] = dlow
        add_small(ROW_FGAIN, column_sum(dtop * normed))
        add_small(ROW_FSHIFT, column_sum(dtop))
        add_small(ROW_DBIAS, column_sum(cot))
        add_small(ROW_SOBIAS, column_sum(dlow.astype(F32)))

    over_rows(SELF_ROWS, 64, after_feed)
    aso_ref[...] += dot_first(mix_ref[...], dso_ref[...])
    dmix_ref[...] = dot_last(dso_ref[...], slab_matrix(slab_ref, WSO, 2)).astype(BF16)

    def attend_group_back(member, carry):
        start = pl.multiple_of(member * NL, NL)
        group = pl.ds(start, NL)
        tiles = [pl.ds(pl.multiple_of(start + tile * QT, QT), QT) for tile in range(TILES)]
        for part in range(2):
            keys = triple_ref[group, half(part + 2)]
            values = triple_ref[group, half(part + 4)]
            queries = [block_diagonal(triple_ref[rows, half(part)], mask_ref[...]) for rows in tiles]
            grads = [block_diagonal(dmix_ref[rows, half(part)], mask_ref[...]) for rows in tiles]
            dprobs = [dot_last(values, grad) for grad in grads]
            probs = [probs_ref[(member * TILES + tile) * 2 + part] for tile in range(TILES)]
            dscores = [score_grads(low.astype(F32), dp) for low, dp in zip(probs, dprobs)]
            dvalues = dot_plain(jnp.concatenate(probs, 1), jnp.concatenate(grads, 0))
            dtriple_ref[group, half(part + 4)] = dvalues.astype(BF16)
            dkeys = dot_plain(jnp.concatenate(dscores, 1), jnp.concatenate(queries, 0))
            dtriple_ref[group, half(part + 2)] = (dkeys * SCALE).astype(BF16)
            for rows, dscore in zip(tiles, dscores):
                dquery = take_diagonal(dot_first(dscore, keys))
                dtriple_ref[rows, half(part)] = (dquery * SCALE).astype(BF16)
        return carry

    lax.fori_loop(0, SELF_GROUPS, attend_group_back, 0)
    for block in range(3):
        columns = slice(D * block, D * block + D)
        aproj_ref[:, columns] += dot_first(low1_ref[...], dtriple_ref[:, columns])
    add_small(ROW_SQBIAS, column_sum(dtriple_ref[:, :D].astype(F32)))
    add_small(ROW_SVBIAS, column_sum(dtriple_ref[:, 2 * D :].astype(F32)))
    dtop_ref[...] = dot_last(dtriple_ref[...], slab_matrix(slab_ref, WPROJ, 6))
    base = step % (G // SELF_GROUPS) * SELF_ROWS

    def after_self(rows):
        dmid = dtop_ref[rows, :]
        normed = hat1_ref[rows, :]
        dafter = res_ref[rows, :] + norm_backward(dmid, normed, rs1_ref[rows, :], vec(ROW_SGAIN))
        dcross_ref[rows, :] = dafter.astype(BF16)
        glat_ref[pl.ds(pl.multiple_of(base + rows.start, 64), rows.size), :] += dafter
        add_small(ROW_SGAIN, column_sum(dmid * normed))
        add_small(ROW_SSHIFT, column_sum(dmid))

    over_rows(SELF_ROWS, 64, after_self)

    @pl.when(step == last)
    def _():
        store_slab(gslab_ref, WPROJ, aproj_ref[...])
        store_slab(gslab_ref, WSO, aso_ref[...])
        store_slab(gslab_ref, WUP, aup_ref[...])
        store_slab(gslab_ref, WDN, adn_ref[...])


def cross_backward_kernel(
    cuts_ref,
    plan_ref,
    inputs_ref,
    kv_ref,
    mix_ref,
    lse_ref,
    dcross_ref,
    query_ref,
    glat_ref,
    slab_ref,
    vec_ref,
    dinput_ref,
    gslab_ref,
    small_ref,
    mask_ref,
    seg_ref,
    source_ref,
    rs_ref,
    dmix_ref,
    dkey_ref,
    dvalue_ref,
    dkv_ref,
    dquery_ref,
    akv_ref,
    ao_ref,
):
    step = pl.program_id(0)
    last = pl.num_programs(0) - 1

    def vec(row):
        return vec_ref[row : row + 1, :]

    def add_small(row, value):
        small_ref[row : row + 1, :] += value

    @pl.when(step == 0)
    def _():
        fill_block_mask(mask_ref)
        for ref in (small_ref, dquery_ref, akv_ref, ao_ref):
            ref[...] = jnp.zeros(ref.shape, ref.dtype)

    source_gain = vec_ref[ROW_SOURCE : ROW_SOURCE + 1, :CIN]
    source_shift = vec_ref[ROW_SOURCE : ROW_SOURCE + 1, CIN:]

    def source_rows(rows):
        low, normed, rscale = norm_forward(
            inputs_ref[rows, :].astype(F32), source_gain, source_shift
        )
        source_ref[rows, :] = low.astype(BF16)
        dinput_ref[rows, :] = normed
        rs_ref[rows, :] = rscale

    over_rows(IN_STEP, 128, source_rows)
    ao_ref[...] += dot_first(mix_ref[...], dcross_ref[...])
    add_small(ROW_COBIAS, column_sum(dcross_ref[...].astype(F32)))
    dmix_ref[...] = dot_last(dcross_ref[...], slab_matrix(slab_ref, WO, 2)).astype(BF16)

    fill_cross_segments(seg_ref, cuts_ref, step)
    dkey_ref[...] = jnp.zeros(dkey_ref.shape, F32)
    dvalue_ref[...] = jnp.zeros(dvalue_ref.shape, F32)

    def batch_body(batch, carry):
        def window(width):
            units = cross_units(plan_ref, cuts_ref, seg_ref, step, batch, width)
            work = []
            for slot, rows, keys, allowed in units:
                for part in range(2):
                    queries = block_diagonal(query_ref[rows, half(part)], mask_ref[...])
                    grads = block_diagonal(dmix_ref[rows, half(part)], mask_ref[...])
                    scores = dot_last(kv_ref[keys, half(part)], queries)
                    dprobs = dot_last(kv_ref[keys, half(part + 2)], grads)
                    work.append((slot, rows, keys, allowed, part, queries, grads, scores, dprobs))
            ready = []
            for slot, rows, keys, allowed, part, queries, grads, scores, dprobs in work:
                lse = lse_ref[pl.ds(slot * 2 + part, 1), :]
                probs = jnp.exp2(jnp.where(allowed, scores * SCALE2 - lse, NEG_FILL))
                dscores = score_grads(probs, dprobs)
                ready.append((rows, keys, part, queries, grads, probs.astype(BF16), dscores))
            for rows, keys, part, queries, grads, probs, dscores in ready:
                dvalue_ref[keys, half(part)] += dot_plain(probs, grads)
                dkey_ref[keys, half(part)] += dot_plain(dscores, queries)
                dquery_ref[rows, half(part)] += take_diagonal(
                    dot_first(dscores, kv_ref[keys, half(part)])
                )

        in_widths(batch_needed(plan_ref, step, batch), window)
        return carry

    lax.fori_loop(0, CROSS_GROUPS * TILES // UNITS, batch_body, 0)
    dkv_ref[:, :D] = (dkey_ref[...] * SCALE).astype(BF16)
    dkv_ref[:, D:] = dvalue_ref[...].astype(BF16)

    for part in range(2):
        columns = slice(D * part, D * part + D)
        akv_ref[:, columns] += dot_first(source_ref[...], dkv_ref[:, columns])
    add_small(ROW_VBIAS, column_sum(dkv_ref[:, D:].astype(F32)))

    def source_back(rows):
        dsource = dot_last(dkv_ref[rows, :], slab_matrix(slab_ref, WKV, 4))
        normed = dinput_ref[rows, :]
        small_ref[ROW_SOURCE : ROW_SOURCE + 1, :CIN] += column_sum(dsource * normed)
        small_ref[ROW_SOURCE : ROW_SOURCE + 1, CIN:] += column_sum(dsource)
        dinput_ref[rows, :] = norm_backward(dsource, normed, rs_ref[rows, :], source_gain)

    over_rows(IN_STEP, 256, source_back)

    @pl.when(step == last)
    def _():
        store_slab(gslab_ref, WKV, akv_ref[...])
        store_slab(gslab_ref, WO, ao_ref[...])
        low, normed, rscale = norm_forward(
            slab_matrix(slab_ref, LATENT, 2).astype(F32), vec(ROW_QGAIN), vec(ROW_QSHIFT)
        )
        dquery = (dquery_ref[...] * SCALE).astype(BF16)
        store_slab(gslab_ref, WQ, dot_first(low.astype(BF16), dquery))
        add_small(ROW_QBIAS, column_sum(dquery.astype(F32)))
        dnorm = dot_last(dquery, slab_matrix(slab_ref, WQ, 2))
        add_small(ROW_QGAIN, column_sum(dnorm * normed))
        add_small(ROW_QSHIFT, column_sum(dnorm))
        total = glat_ref[...] + norm_backward(dnorm, normed, rscale, vec(ROW_QGAIN))
        store_slab(gslab_ref, LATENT, total)


def rows_spec(rows, columns):
    return pl.BlockSpec((rows, columns), lambda step, *scalars: (step, 0))


def whole_spec(rows, columns):
    return pl.BlockSpec(
        (rows, columns), lambda step, *scalars: (0, 0), pipeline_mode=pl.Buffered(1)
    )


def kernel_call(kernel, scalars, steps, in_specs, out_specs, out_shape, scratch, flops):
    return pl.pallas_call(
        kernel,
        grid_spec=pltpu.PrefetchScalarGridSpec(
            num_scalar_prefetch=scalars,
            grid=(steps,),
            in_specs=in_specs,
            out_specs=out_specs,
            scratch_shapes=scratch,
        ),
        out_shape=out_shape,
        compiler_params=pltpu.CompilerParams(
            vmem_limit_bytes=VMEM_BYTES, dimension_semantics=("arbitrary",)
        ),
        cost_estimate=pl.CostEstimate(
            flops=flops, bytes_accessed=100 * 2**20, transcendentals=0
        ),
    )


def slab_spec(rows):
    return pl.BlockSpec(
        (CHUNKS, HALVES, rows, PACK),
        lambda step, *scalars: (0, 0, 0, 0),
        pipeline_mode=pl.Buffered(1),
    )


def slab_shape(rows):
    return jax.ShapeDtypeStruct((CHUNKS, HALVES, rows, PACK), BF16)


def pack_shards(shards):
    return jnp.concatenate(
        [
            shard[:, start : start + PACK]
            for shard in shards
            for start in range(0, shard.shape[1], PACK)
        ],
        0,
    )


def unpack_shards(packed, mats):
    shards = []
    start = 0
    for rows, columns in mats:
        height = rows // CHUNKS
        pieces = []
        for _ in range(columns // (HALVES * PACK)):
            pieces.append(packed[start : start + height])
            start += height
        shards.append(jnp.concatenate(pieces, 1))
    return shards


def gather_whole(shards):
    parts = []
    for shard in shards:
        full = lax.all_gather(
            lax.all_gather(shard, "narrow", axis=1, tiled=True), "wide", axis=0, tiled=True
        )
        rows, columns = full.shape
        split = full.reshape(CHUNKS, rows // CHUNKS, HALVES, columns // (HALVES * PACK), PACK)
        parts.append(split.transpose(0, 2, 3, 1, 4).reshape(CHUNKS, HALVES, -1, PACK))
    return jnp.concatenate(parts, 2)


def scatter_whole(slab, mats):
    shards = []
    start = 0
    for rows, columns in mats:
        height = rows // CHUNKS
        pieces = columns // (HALVES * PACK)
        part = slab[:, :, start : start + height * pieces]
        start += height * pieces
        part = part.reshape(CHUNKS, HALVES, pieces, height, PACK).transpose(0, 3, 1, 2, 4)
        total = lax.psum_scatter(
            part.reshape(rows, columns), "wide", scatter_dimension=0, tiled=True
        )
        total = lax.psum_scatter(total, "narrow", scatter_dimension=1, tiled=True)
        shards.append(total.astype(F32))
    return shards


SWAP = ((0, 1), (1, 0))


def gather_soon(shards):
    packed = pack_shards(shards)
    copies = jnp.broadcast_to(packed, (CHUNKS,) + packed.shape)
    mine = lax.all_to_all(copies, "wide", 0, 0)
    other = lax.ppermute(mine, "narrow", SWAP)
    first = lax.axis_index("narrow") == 0
    return jnp.stack([jnp.where(first, mine, other), jnp.where(first, other, mine)], 1)


def gather_later(shards):
    packed = pack_shards(shards)
    full = lax.all_gather(packed, ("wide", "narrow"), axis=0)
    return full.reshape((CHUNKS, HALVES) + packed.shape)


def sum_halves(slab):
    first = lax.axis_index("narrow") == 0
    sent = lax.ppermute(jnp.where(first, slab[:, 1], slab[:, 0]), "narrow", SWAP)
    kept = jnp.where(first, slab[:, 0], slab[:, 1])
    return (sent.astype(F32) + kept.astype(F32)).astype(BF16)


def scatter_soon(slab, mats):
    parts = lax.all_to_all(sum_halves(slab), "wide", 0, 0)
    return unpack_shards(jnp.sum(parts.astype(F32), 0), mats)


def sum_small_soon(rows):
    pair = rows + lax.ppermute(rows, "narrow", SWAP)
    copies = jnp.broadcast_to(pair, (CHUNKS,) + pair.shape)
    return jnp.sum(lax.all_to_all(copies, "wide", 0, 0), 0)


def scatter_later(slab, mats):
    total = lax.psum_scatter(sum_halves(slab), "wide", scatter_dimension=0)
    return unpack_shards(total.astype(F32), mats)


def shape(rows, columns, dtype):
    return jax.ShapeDtypeStruct((rows, columns), dtype)


def local(
    wide,
    narrow,
    inputs,
    input_segments,
    latent_segments,
    cotangent,
    latent_array,
    query_gain,
    query_shift,
    source_gain,
    source_shift,
    cross_query,
    cross_qbias,
    cross_keyval,
    cross_vbias,
    cross_output,
    cross_obias,
    self_gain,
    self_shift,
    self_project,
    self_qbias,
    self_vbias,
    self_output,
    self_obias,
    feed_gain,
    feed_shift,
    feed_upward,
    feed_ubias,
    feed_downward,
    feed_dbias,
):
    lat_rows = cotangent.shape[0]
    in_rows = inputs.shape[0]
    groups = lat_rows // NL
    steps = groups // CROSS_GROUPS
    self_steps = groups // SELF_GROUPS

    vectors = jnp.concatenate(
        [
            query_gain,
            query_shift,
            source_gain,
            source_shift,
            cross_qbias,
            cross_vbias,
            cross_obias,
            self_gain,
            self_shift,
            self_qbias,
            self_vbias,
            self_obias,
            feed_gain,
            feed_shift,
            feed_ubias,
            feed_dbias,
            jnp.zeros(((VEC_ROWS - ROW_DBIAS - 1) * D,), BF16),
        ]
    )
    vectors = vectors.astype(F32).reshape(VEC_ROWS, D)
    marks = jnp.arange(1, SEGS, dtype=jnp.int32)
    in_cuts = jnp.sum(input_segments.reshape(groups, IN_G, 1) < marks, 1, dtype=jnp.int32)
    lat_cuts = jnp.sum(latent_segments.reshape(groups, NL, 1) < marks, 1, dtype=jnp.int32)
    blank = jnp.zeros((groups, 1), jnp.int32)
    cuts = jnp.concatenate([in_cuts, blank, lat_cuts, blank], 1)
    plan = plan_tiles(in_cuts, lat_cuts)

    source_low, _, _ = norm_forward(
        inputs.astype(F32), source_gain.astype(F32), source_shift.astype(F32)
    )
    source_low = source_low.astype(BF16)

    cross_shards = (latent_array, cross_query, cross_keyval, cross_output)
    middle_shards = (self_project, self_output, feed_upward, feed_downward)
    packed = (wide, narrow) == (CHUNKS, HALVES)
    if packed:
        cross_slab = gather_soon(cross_shards)
        middle_slab = gather_later(middle_shards)
    else:
        cross_slab = gather_whole(cross_shards)
        middle_slab = gather_whole(middle_shards)

    vec_spec = whole_spec(VEC_ROWS, D)
    lse_rows = CROSS_GROUPS * TILES * 2
    after, cross_mix, keyval, lse, query = kernel_call(
        cross_forward_kernel,
        2,
        steps,
        [
            rows_spec(IN_STEP, CIN),
            slab_spec(CROSS_SLAB),
            vec_spec,
        ],
        [
            rows_spec(LAT_STEP, D),
            rows_spec(LAT_STEP, D),
            rows_spec(IN_STEP, 2 * D),
            rows_spec(lse_rows, PACK),
            whole_spec(G * NL, D),
        ],
        [
            shape(lat_rows, D, F32),
            shape(lat_rows, D, BF16),
            shape(in_rows, 2 * D, BF16),
            shape(steps * lse_rows, PACK, F32),
            shape(G * NL, D, BF16),
        ],
        [
            pltpu.VMEM((PACK, PACK), BF16),
            pltpu.VMEM((IN_STEP, 128), jnp.int32),
        ],
        60 * 10**9,
    )(cuts, plan, source_low, cross_slab, vectors)

    latents_out, dcross, glat, middle_small, middle_grads = kernel_call(
        middle_kernel,
        1,
        self_steps,
        [
            rows_spec(SELF_ROWS, D),
            rows_spec(SELF_ROWS, D),
            slab_spec(MIDDLE_SLAB),
            vec_spec,
        ],
        [
            rows_spec(SELF_ROWS, D),
            rows_spec(SELF_ROWS, D),
            whole_spec(G * NL, D),
            vec_spec,
            slab_spec(MIDDLE_SLAB),
        ],
        [
            shape(lat_rows, D, BF16),
            shape(lat_rows, D, BF16),
            shape(G * NL, D, F32),
            shape(VEC_ROWS, D, F32),
            slab_shape(MIDDLE_SLAB),
        ],
        [
            pltpu.VMEM((PACK, PACK), BF16),
            pltpu.VMEM((SELF_ROWS, D), F32),
            pltpu.VMEM((SELF_ROWS, 1), F32),
            pltpu.VMEM((SELF_ROWS, D), BF16),
            pltpu.VMEM((SELF_ROWS, 3 * D), BF16),
            pltpu.VMEM((SELF_GROUPS * TILES * 2, NL, PACK), BF16),
            pltpu.VMEM((SELF_ROWS, D), BF16),
            pltpu.VMEM((SELF_ROWS, D), F32),
            pltpu.VMEM((SELF_ROWS, D), F32),
            pltpu.VMEM((SELF_ROWS, 1), F32),
            pltpu.VMEM((SELF_ROWS, D), BF16),
            pltpu.VMEM((SELF_ROWS, D), F32),
            pltpu.VMEM((SELF_ROWS, D), BF16),
            pltpu.VMEM((SELF_ROWS, D), BF16),
            pltpu.VMEM((SELF_ROWS, 3 * D), BF16),
            pltpu.VMEM((D, 3 * D), F32),
            pltpu.VMEM((D, D), F32),
            pltpu.VMEM((D, FF), F32),
            pltpu.VMEM((FF, D), F32),
        ],
        250 * 10**9,
    )(cuts, after, cotangent, middle_slab, vectors)

    dinput, cross_grads, cross_small = kernel_call(
        cross_backward_kernel,
        2,
        steps,
        [
            rows_spec(IN_STEP, CIN),
            rows_spec(IN_STEP, 2 * D),
            rows_spec(LAT_STEP, D),
            rows_spec(lse_rows, PACK),
            rows_spec(LAT_STEP, D),
            whole_spec(G * NL, D),
            whole_spec(G * NL, D),
            slab_spec(CROSS_SLAB),
            vec_spec,
        ],
        [
            rows_spec(IN_STEP, CIN),
            slab_spec(CROSS_SLAB),
            vec_spec,
        ],
        [
            shape(in_rows, CIN, F32),
            slab_shape(CROSS_SLAB),
            shape(VEC_ROWS, D, F32),
        ],
        [
            pltpu.VMEM((PACK, PACK), BF16),
            pltpu.VMEM((IN_STEP, 128), jnp.int32),
            pltpu.VMEM((IN_STEP, CIN), BF16),
            pltpu.VMEM((IN_STEP, 1), F32),
            pltpu.VMEM((LAT_STEP, D), BF16),
            pltpu.VMEM((IN_STEP, D), F32),
            pltpu.VMEM((IN_STEP, D), F32),
            pltpu.VMEM((IN_STEP, 2 * D), BF16),
            pltpu.VMEM((G * NL, D), F32),
            pltpu.VMEM((CIN, 2 * D), F32),
            pltpu.VMEM((D, D), F32),
        ],
        120 * 10**9,
    )(
        cuts,
        plan,
        inputs,
        keyval,
        cross_mix,
        lse,
        dcross,
        query,
        glat,
        cross_slab,
        vectors,
    )

    axes = ("wide", "narrow")
    middle_sum = lax.psum(middle_small, axes)[ROW_SGAIN:]
    if packed:
        gproj, gso, gup, gdn = scatter_later(middle_grads, MIDDLE_MATS)
        cross_sum = sum_small_soon(cross_small[:8])
        glatent, gq, gkv, go = scatter_soon(cross_grads, CROSS_MATS)
    else:
        gproj, gso, gup, gdn = scatter_whole(middle_grads, MIDDLE_MATS)
        cross_sum = lax.psum(cross_small, axes)
        glatent, gq, gkv, go = scatter_whole(cross_grads, CROSS_MATS)
    flat = jnp.concatenate([cross_sum[:ROW_SGAIN].reshape(-1), middle_sum.reshape(-1)])

    def part(row, size, offset=0):
        return flat[row * D + offset : row * D + offset + size]

    return (
        latents_out,
        dinput,
        glatent,
        part(ROW_QGAIN, D),
        part(ROW_QSHIFT, D),
        part(ROW_SOURCE, CIN),
        part(ROW_SOURCE, CIN, CIN),
        gq,
        part(ROW_QBIAS, D),
        gkv,
        part(ROW_VBIAS, D),
        go,
        part(ROW_COBIAS, D),
        part(ROW_SGAIN, D),
        part(ROW_SSHIFT, D),
        gproj,
        part(ROW_SQBIAS, D),
        part(ROW_SVBIAS, D),
        gso,
        part(ROW_SOBIAS, D),
        part(ROW_FGAIN, D),
        part(ROW_FSHIFT, D),
        gup,
        part(ROW_UBIAS, FF),
        gdn,
        part(ROW_DBIAS, D),
    )


def solution(mesh):
    rows = P(("wide", "narrow"), None)
    flat = P(("wide", "narrow"))
    block = P("wide", "narrow")
    copied = P()
    return jax.shard_map(
        functools.partial(local, mesh.shape["wide"], mesh.shape["narrow"]),
        mesh=mesh,
        in_specs=(
            rows,
            flat,
            flat,
            rows,
            block,
            copied,
            copied,
            copied,
            copied,
            block,
            copied,
            block,
            copied,
            block,
            copied,
            copied,
            copied,
            block,
            copied,
            copied,
            block,
            copied,
            copied,
            copied,
            block,
            copied,
            block,
            copied,
        ),
        out_specs=(
            rows,
            rows,
            block,
            copied,
            copied,
            copied,
            copied,
            block,
            copied,
            block,
            copied,
            block,
            copied,
            copied,
            copied,
            block,
            copied,
            copied,
            block,
            copied,
            copied,
            copied,
            block,
            copied,
            block,
            copied,
        ),
        check_vma=False,
    )
```

time: 1950 us -> 775 us (0.40)
  waiting for transfers between devices: 621 us -> 33 us
  Pallas kernels: 1040 us -> 574 us
  blocking collectives: 241 us -> 51.7 us
  starting transfers between devices: 0.78 us -> 35.4 us
  other arithmetic: 11.6 us -> 35.8 us
    reduce_scatter x16 -> x1, waiting for transfers between devices: 616 us -> 0.01 us  [scatter_later(): total = lax.psum_scatter(sum_halves(slab), 'wide', scatter_dimension=0)]
    pallas_call x3, Pallas kernels: 1040 us -> 574 us  [the longest x1 328 us: local(): kernel_call(middle_kernel, 1, self_steps, [rows_spec(SELF_ROWS, D), rows_...]
    all_gather x12 -> x0, blocking collectives: 202 us -> none  [the longest x4 178 us: gather(): lax.all_gather(lax.all_gather(shard, 'narrow', axis=1, tiled=True), 'wide...]
    all_to_all x0 -> x3, starting transfers between devices: none -> 33 us  [the longest x1 21 us: sum_small_soon(): return jnp.sum(lax.all_to_all(copies, 'wide', 0, 0), 0)]
    all_to_all x0 -> x3, waiting for transfers between devices: none -> 23.7 us  [the longest x1 16.3 us: gather_soon(): mine = lax.all_to_all(copies, 'wide', 0, 0)]
  transfers between devices with their start and end apart: 20 -> 9, of which waited for: 15 -> 5; matrix products, arithmetic and copies ran while one was open for 1% -> 5% of each run, Pallas kernels for 24% -> 32%
where the time goes in v2:
time: 775 us; the launch traced here: 768 us
  Pallas kernels  574 us (74%)
  blocking collectives  51.7 us (7%)
  other arithmetic  35.8 us (5%)
  starting transfers between devices  35.4 us (5%)
  waiting for transfers between devices  33 us (4%)
  local copies, waits for them, and re-layouts  23.1 us (3%)
  between operations  14.8 us (2%)
    pallas_call x1, Pallas kernels, local(): kernel_call(middle_kernel, 1, self_steps, [rows_spec(SELF_ROWS, D), rows_...  328 us
    pallas_call x1, Pallas kernels, local(): kernel_call(cross_backward_kernel, 2, steps, [rows_spec(IN_STEP, CIN), ro...  158 us
    pallas_call x1, Pallas kernels, local(): kernel_call(cross_forward_kernel, 2, steps, [rows_spec(IN_STEP, CIN), sla...  88.2 us
    psum x1, blocking collectives, local(): middle_sum = lax.psum(middle_small, axes)[ROW_SGAIN:]  51.7 us
    all_to_all x1, starting transfers between devices, sum_small_soon(): return jnp.sum(lax.all_to_all(copies, 'wide', 0, 0), 0)  21 us
    all_to_all x1, waiting for transfers between devices, gather_soon(): mine = lax.all_to_all(copies, 'wide', 0, 0)  16.3 us
  transfers between devices with their start and end apart: 9, of which 5 were waited for; matrix products, arithmetic and copies ran while one was open for 5% of the time, Pallas kernels for 32%

profile of v2, /device:TPU:0, one launch (start us, length us, event | category | flops | bytes accessed | tf_op | source)
XLA Modules:
  0.0 767.5 jit_solution(3668639844084468147)
XLA Ops:
  7.4 0.8 constant_dynamic-update-slice_fusion.13
  8.2 0.7 constant_dynamic-update-slice_fusion.12
  8.9 0.7 constant_dynamic-update-slice_fusion.11
  9.7 0.7 constant_dynamic-update-slice_fusion.10
  10.4 0.7 constant_dynamic-update-slice_fusion.9
  11.1 0.7 constant_dynamic-update-slice_fusion.8
  11.8 0.7 constant_dynamic-update-slice_fusion.7
  12.5 0.7 constant_dynamic-update-slice_fusion.6
  13.3 0.8 constant_dynamic-update-slice_fusion.5
  14.1 0.7 copy-done.3
  14.8 0.8 constant_dynamic-update-slice_fusion.4
  15.6 0.7 constant_dynamic-update-slice_fusion.3
  16.3 0.7 constant_dynamic-update-slice_fusion.2
  17.0 0.7 constant_dynamic-update-slice_fusion.1
  17.7 0.7 constant_dynamic-update-slice_fusion
  18.4 1.2 broadcast_in_dim.84
  19.6 8.3 %all-to-all-start = ((bf16[16,160,256]{2,1,0:T(8,128)(2,1)}), bf16[16,160,256]{2,1,0:T(8,128)(2,1)S(1)}, u32[]{:S(2)}, u32[]{:S(2)}) async-start(bf16[16,160,256]{2,1,0:T(8,128)(2,1)} %broadcast_in_dim.84), calls=%async_computation | async-start | bytes 2621440 | tf_op jit(solution)/shard_map/all_to_all | solution.py:777
  28.1 0.3 dynamic-update-slice.9
  28.3 0.2 dynamic-update-slice.10
  28.9 0.2 dynamic-update-slice.13
  29.2 0.2 dynamic-update-slice.14
  29.4 0.2 dynamic-update-slice.15
  29.6 0.2 dynamic-update-slice.16
  29.8 0.2 dynamic-update-slice.17
  31.2 0.3 dynamic-update-slice.23
  31.4 0.2 dynamic-update-slice.24
  31.7 0.6 reshape.283.vec_ref
  32.5 0.2 convert_reduce_fusion.2
  32.8 0.7 copy.91.cuts_ref
  33.5 4.9 convert_reduce_fusion
  38.5 3.8 fusion.2
  42.3 7.6 fusion.5.source_ref
  49.9 16.3 %all-to-all-done = bf16[16,160,256]{2,1,0:T(8,128)(2,1)S(1)} async-done(((bf16[16,160,256]{2,1,0:T(8,128)(2,1)}), bf16[16,160,256]{2,1,0:T(8,128)(2,1)S(1)}, u32[]{:S(2)}, u32[]{:S(2)}) %all-to-all-start) | async-done | bytes 1310752 | tf_op jit(solution)/shard_map/all_to_all | solution.py:777
  67.1 0.7 pad_add_fusion.1.plan_ref
  67.7 1.5 collective-permute-done
  69.4 1.7 pad_maximum_fusion.slab_ref
  71.1 88.2 %shard_map.467 = (f32[6144,512]{1,0:T(8,128)}, bf16[6144,512]{1,0:T(8,128)(2,1)}, bf16[12288,1024]{1,0:T(8,128)(2,1)}, f32[384,256]{1,0:T(8,128)}, bf16[1024,512]{1,0:T(8,128)(2,1)}) custom-call(s32[24,8]{1,0:T(8,128)} %copy.91.cuts_ref, s32[6,40]{1,0:T(8,128)} %pad_add_fusion.1.plan_ref, bf16[12288,256]{1,0:T(8,128)(2,1)} %fusion.5.source_ref, ...), custom_call_target="tpu_custom_call" | custom-call | flops 60000002048 | bytes 104857600 | tf_op jit(solution)/shard_map/pallas_call | solution.py:900
  159.4 327.6 %shard_map.468 = (bf16[6144,512]{1,0:T(8,128)(2,1)}, bf16[6144,512]{1,0:T(8,128)(2,1)}, f32[1024,512]{1,0:T(8,128)}, f32[24,512]{1,0:T(8,128)}, bf16[16,2,384,256]{3,2,1,0:T(8,128)(2,1)}) custom-call(s32[24,8]{1,0:T(8,128)} %copy.91.cuts_ref, f32[6144,512]{1,0:T(8,128)} %get-tuple-element.39.after_ref, bf16[6144,512]{1,0:T(8,128)(2,1)} %cot_ref.1, ...), custom_call_target="tpu_custom_call" | custom-call | flops 249999998976 | bytes 104857600 | tf_op jit(solution)/shard_map/pallas_call | solution.py:930
  487.0 4.0 fusion.8
  490.9 1.0 collective-permute-start.3
  491.9 5.3 collective-permute-done.3
  497.2 2.6 fusion.6
  499.8 157.9 %shard_map.469 = (f32[12288,256]{1,0:T(8,128)}, bf16[16,2,160,256]{3,2,1,0:T(8,128)(2,1)}, f32[24,512]{1,0:T(8,128)}) custom-call(s32[24,8]{1,0:T(8,128)} %copy.91.cuts_ref, s32[6,40]{1,0:T(8,128)} %pad_add_fusion.1.plan_ref, bf16[12288,256]{1,0:T(8,128)(2,1)} %inputs_ref.1, bf16[12288,1024]{1,0:T(8,128)(2,1)} %get-tuple-element.41.kv_ref, ...), custom_call_target="tpu_custom_call" | custom-call | flops 120000004096 | bytes 104857600 | tf_op jit(solution)/shard_map/pallas_call | solution.py:978
  657.7 3.3 fusion.11
  661.0 1.2 collective-permute-start.1
  662.3 2.5 collective-permute-done.2
  664.8 0.7 broadcast_in_dim.86
  665.5 21.0 %all-to-all-start.2 = ((f32[16,8,512]{2,1,0:T(8,128)}), f32[16,8,512]{2,1,0:T(8,128)S(1)}, u32[]{:S(2)}, u32[]{:S(2)}) async-start(f32[16,8,512]{2,1,0:T(8,128)} %broadcast_in_dim.86), calls=%async_computation.2 | async-start | bytes 524288 | tf_op jit(solution)/shard_map/all_to_all | solution.py:804
  686.6 3.0 fusion.9
  689.5 7.4 all-to-all-done.2
  696.9 3.7 all-to-all-start.1
  700.7 51.7 %psum.7 = f32[24,512]{1,0:T(8,128)S(1)} all-reduce(f32[24,512]{1,0:T(8,128)S(1)} %copy-done.5), channel_id=1, replica_groups=mesh['wide'=16,'narrow'=2] {'wide','narrow'}, use_global_device_ids=true, to_apply=%region_13.14 | all-reduce | flops 12288 | bytes 98304 | tf_op jit(solution)/shard_map/psum | solution.py:1032
  752.4 0.6 copy.101
  753.0 0.6 fusion.20
  753.7 0.6 fusion.22
  754.2 0.6 fusion.21
  755.0 0.6 slice.292
  755.6 0.6 pad_maximum_fusion.3
  756.3 0.6 fusion.18
  756.9 1.0 convert_element_type.85
  757.9 0.7 slice_bitcast_fusion
  758.5 0.6 slice_bitcast_fusion.4
  759.2 0.6 pad_maximum_fusion.2
  759.8 0.7 pad_maximum_fusion.1
  (100 shorter events, 3.4 us)
Async XLA Ops:
  7.2 20.8 %copy-start.22 = (bf16[256]{0:T(256)(128)(2,1)S(1)}, bf16[256]{0:T(256)(128)(2,1)}, u32[]{:S(2)}) copy-start(bf16[256]{0:T(256)(128)(2,1)} %param.35) | copy-start | bytes 1540
  7.2 20.8 %copy-start.23 = (bf16[256]{0:T(256)(128)(2,1)S(1)}, bf16[256]{0:T(256)(128)(2,1)}, u32[]{:S(2)}) copy-start(bf16[256]{0:T(256)(128)(2,1)} %param.36) | copy-start | bytes 1540
  7.2 20.8 %copy-start.6 = (s32[6144]{0:T(1024)S(1)}, s32[6144]{0:T(1024)}, u32[]{:S(2)}) copy-start(s32[6144]{0:T(1024)} %param.30) | copy-start | bytes 73732
  7.2 20.8 %copy-start.9 = (bf16[512]{0:T(512)(128)(2,1)S(1)}, bf16[512]{0:T(512)(128)(2,1)}, u32[]{:S(2)}) copy-start(bf16[512]{0:T(512)(128)(2,1)} %param.33) | copy-start | bytes 3076
  7.2 21.1 %copy-start.10 = (bf16[512]{0:T(512)(128)(2,1)S(1)}, bf16[512]{0:T(512)(128)(2,1)}, u32[]{:S(2)}) copy-start(bf16[512]{0:T(512)(128)(2,1)} %param.34) | copy-start | bytes 3076
  7.3 21.7 %copy-start.11 = (bf16[512]{0:T(512)(128)(2,1)S(1)}, bf16[512]{0:T(512)(128)(2,1)}, u32[]{:S(2)}) copy-start(bf16[512]{0:T(512)(128)(2,1)} %param.38) | copy-start | bytes 3076
  7.3 21.9 %copy-start.12 = (bf16[512]{0:T(512)(128)(2,1)S(1)}, bf16[512]{0:T(512)(128)(2,1)}, u32[]{:S(2)}) copy-start(bf16[512]{0:T(512)(128)(2,1)} %param.40) | copy-start | bytes 3076
  7.3 22.1 %copy-start.13 = (bf16[512]{0:T(512)(128)(2,1)S(1)}, bf16[512]{0:T(512)(128)(2,1)}, u32[]{:S(2)}) copy-start(bf16[512]{0:T(512)(128)(2,1)} %param.42) | copy-start | bytes 3076
  7.3 22.3 %copy-start.14 = (bf16[512]{0:T(512)(128)(2,1)S(1)}, bf16[512]{0:T(512)(128)(2,1)}, u32[]{:S(2)}) copy-start(bf16[512]{0:T(512)(128)(2,1)} %param.43) | copy-start | bytes 3076
  7.3 22.5 %copy-start.15 = (bf16[512]{0:T(512)(128)(2,1)S(1)}, bf16[512]{0:T(512)(128)(2,1)}, u32[]{:S(2)}) copy-start(bf16[512]{0:T(512)(128)(2,1)} %param.44) | copy-start | bytes 3076
  7.3 22.7 %copy-start.16 = (bf16[512]{0:T(512)(128)(2,1)S(1)}, bf16[512]{0:T(512)(128)(2,1)}, u32[]{:S(2)}) copy-start(bf16[512]{0:T(512)(128)(2,1)} %param.46) | copy-start | bytes 3076
  7.3 23.0 %copy-start.17 = (bf16[512]{0:T(512)(128)(2,1)S(1)}, bf16[512]{0:T(512)(128)(2,1)}, u32[]{:S(2)}) copy-start(bf16[512]{0:T(512)(128)(2,1)} %param.47) | copy-start | bytes 3076
  7.3 23.2 %copy-start.18 = (bf16[512]{0:T(512)(128)(2,1)S(1)}, bf16[512]{0:T(512)(128)(2,1)}, u32[]{:S(2)}) copy-start(bf16[512]{0:T(512)(128)(2,1)} %param.49) | copy-start | bytes 3076
  7.3 23.4 %copy-start.19 = (bf16[512]{0:T(512)(128)(2,1)S(1)}, bf16[512]{0:T(512)(128)(2,1)}, u32[]{:S(2)}) copy-start(bf16[512]{0:T(512)(128)(2,1)} %param.50) | copy-start | bytes 3076
  7.3 23.6 %copy-start.20 = (bf16[512]{0:T(512)(128)(2,1)S(1)}, bf16[512]{0:T(512)(128)(2,1)}, u32[]{:S(2)}) copy-start(bf16[512]{0:T(512)(128)(2,1)} %param.51) | copy-start | bytes 3076
  7.4 23.8 %copy-start.8 = (bf16[2048]{0:T(1024)(128)(2,1)S(1)}, bf16[2048]{0:T(1024)(128)(2,1)}, u32[]{:S(2)}) copy-start(bf16[2048]{0:T(1024)(128)(2,1)} %param.53) | copy-start | bytes 12292
  7.4 24.1 %copy-start.21 = (bf16[512]{0:T(512)(128)(2,1)S(1)}, bf16[512]{0:T(512)(128)(2,1)}, u32[]{:S(2)}) copy-start(bf16[512]{0:T(512)(128)(2,1)} %param.55) | copy-start | bytes 3076
  7.4 24.9 %copy-start.4 = (s32[12288]{0:T(1024)S(1)}, s32[12288]{0:T(1024)}, u32[]{:S(2)}) copy-start(s32[12288]{0:T(1024)} %param.29) | copy-start | bytes 147460
  7.4 152.0 %all-gather.3.cloned.1.call-start = ((), (), s32[]{:S(2)}) async-start(), calls=%async_computation.5 | async-start | bytes 6488064 | tf_op jit(solution)/shard_map/all_gather | solution.py:785
  14.1 0.7 copy-start.3
  19.6 46.6 %all-to-all-start = ((bf16[16,160,256]{2,1,0:T(8,128)(2,1)}), bf16[16,160,256]{2,1,0:T(8,128)(2,1)S(1)}, u32[]{:S(2)}, u32[]{:S(2)}) async-start(bf16[16,160,256]{2,1,0:T(8,128)(2,1)} %broadcast_in_dim.84), calls=%async_computation | async-start | bytes 2621440 | tf_op jit(solution)/shard_map/all_to_all | solution.py:777
  27.9 729.0 %reduce-scatter.2.cloned.1.call-start = ((), (), s32[]{:S(2)}) async-start(), calls=%async_computation.4 | async-start | bytes 3342336 | tf_op jit(solution)/shard_map/reduce_scatter | solution.py:808
  33.5 5.0 copy-start
  66.2 3.0 collective-permute-start
  486.9 10.2 %copy-start.1 = (bf16[16,2,384,256]{3,2,1,0:T(8,128)(2,1)S(1)}, bf16[16,2,384,256]{3,2,1,0:T(8,128)(2,1)}, u32[]{:S(2)}) copy-start(bf16[16,2,384,256]{3,2,1,0:T(8,128)(2,1)} %get-tuple-element.51) | copy-start | bytes 18874372
  490.9 6.3 collective-permute-start.3
  657.7 4.6 copy-start.7
  657.7 28.9 %copy-start.2 = (bf16[16,2,160,256]{3,2,1,0:T(8,128)(2,1)S(1)}, bf16[16,2,160,256]{3,2,1,0:T(8,128)(2,1)}, u32[]{:S(2)}) copy-start(bf16[16,2,160,256]{3,2,1,0:T(8,128)(2,1)} %get-tuple-element.48) | copy-start | bytes 7864324
  661.0 25.5 %collective-permute-start.1 = (bf16[16,160,256]{2,1,0:T(8,128)(2,1)}, bf16[16,160,256]{2,1,0:T(8,128)(2,1)}, u32[]{:S(2)}, u32[]{:S(2)}) collective-permute-start(bf16[16,160,256]{2,1,0:T(8,128)(2,1)} %fusion.11), channel_id=1, source_target_pairs={{0,1},{1,0},{2,3},{3,2},{4,5},{5,4},{6,7},{7,6},{8,9},{9,8},{10,11... | collective-permute-start | bytes 3932168 | tf_op jit(solution)/shard_map/ppermute | solution.py:791
  662.3 2.5 collective-permute-start.2
  665.5 31.4 %all-to-all-start.2 = ((f32[16,8,512]{2,1,0:T(8,128)}), f32[16,8,512]{2,1,0:T(8,128)S(1)}, u32[]{:S(2)}, u32[]{:S(2)}) async-start(f32[16,8,512]{2,1,0:T(8,128)} %broadcast_in_dim.86), calls=%async_computation.2 | async-start | bytes 524288 | tf_op jit(solution)/shard_map/all_to_all | solution.py:804
  686.5 14.1 %copy-start.5 = (f32[24,512]{1,0:T(8,128)S(1)}, f32[24,512]{1,0:T(8,128)}, u32[]{:S(2)}) copy-start(f32[24,512]{1,0:T(8,128)} %get-tuple-element.50) | copy-start | bytes 147460
  696.9 57.9 %all-to-all-start.1 = ((bf16[16,160,256]{2,1,0:T(8,128)(2,1)}), bf16[16,160,256]{2,1,0:T(8,128)(2,1)S(1)}, u32[]{:S(2)}, u32[]{:S(2)}) async-start(bf16[16,160,256]{2,1,0:T(8,128)(2,1)} %fusion.9), calls=%async_computation.1 | async-start | bytes 2621440 | tf_op jit(solution)/shard_map/all_to_all | solution.py:797
Sparse Core Ops, SparseCore 0:
  14.9 84.0 all-gather.2
  499.9 137.2 reduce-scatter.1

commit v3 on v2

--- a/solution.py
+++ b/solution.py
@@ -46,15 +46,17 @@
     -0.10580882324798475,
 )
 
-ROW_QGAIN, ROW_QSHIFT, ROW_SOURCE, ROW_QBIAS, ROW_VBIAS, ROW_COBIAS = range(6)
-ROW_SGAIN, ROW_SSHIFT, ROW_SQBIAS, ROW_SVBIAS, ROW_SOBIAS = range(6, 11)
-ROW_FGAIN, ROW_FSHIFT, ROW_UBIAS, ROW_DBIAS = 11, 12, 13, 17
+ROW_QGAIN, ROW_QSHIFT, ROW_SOURCE, ROW_QBIAS, ROW_VBIAS = range(5)
+ROW_UBIAS, ROW_COBIAS, ROW_SGAIN, ROW_SSHIFT, ROW_SQBIAS = 8, 12, 13, 14, 15
+ROW_SVBIAS, ROW_SOBIAS, ROW_FGAIN, ROW_FSHIFT, ROW_DBIAS = 16, 17, 18, 19, 20
 VEC_ROWS = 24
+CROSS_VECS = 8
+MIDDLE_VECS = VEC_ROWS - CROSS_VECS
 
 CHUNKS = 16
 HALVES = 2
-CROSS_MATS = ((G * NL, D), (D, D), (CIN, 2 * D), (D, D))
-MIDDLE_MATS = ((D, 3 * D), (D, D), (D, FF), (FF, D))
+CROSS_MATS = ((G * NL, D), (D, D), (CIN, 2 * D))
+MIDDLE_MATS = ((D, 3 * D), (D, D), (D, FF), (FF, D), (D, D))
 
 
 def slab_place(mats, at):
@@ -62,8 +64,8 @@
     return sum(sizes[:at]), mats[at][0] // CHUNKS, sum(sizes)
 
 
-LATENT, WQ, WKV, WO = (slab_place(CROSS_MATS, at)[:2] for at in range(4))
-WPROJ, WSO, WUP, WDN = (slab_place(MIDDLE_MATS, at)[:2] for at in range(4))
+LATENT, WQ, WKV = (slab_place(CROSS_MATS, at)[:2] for at in range(3))
+WPROJ, WSO, WUP, WDN, WO = (slab_place(MIDDLE_MATS, at)[:2] for at in range(5))
 CROSS_SLAB = slab_place(CROSS_MATS, 0)[2]
 MIDDLE_SLAB = slab_place(MIDDLE_MATS, 0)[2]
 
@@ -210,14 +212,24 @@
     )
 
 
-def store_slab(slab_ref, place, matrix):
+def store_halves(side, keep_ref, send_ref, place, matrix):
     offset, rows = place
     pieces = matrix.shape[1] // PACK
-    for piece in range(pieces):
-        side, inner = piece // (pieces // HALVES), piece % (pieces // HALVES)
-        start = offset + inner * rows
-        part = matrix[:, piece * PACK : piece * PACK + PACK].astype(BF16)
-        slab_ref[:, side, start : start + rows, :] = part.reshape(CHUNKS, rows, PACK)
+    inner = pieces // HALVES
+
+    def store(refs):
+        for piece in range(pieces):
+            start = offset + piece % inner * rows
+            part = matrix[:, piece * PACK : piece * PACK + PACK].astype(BF16)
+            refs[piece // inner][:, start : start + rows, :] = part.reshape(CHUNKS, rows, PACK)
+
+    @pl.when(side == 0)
+    def _():
+        store((keep_ref, send_ref))
+
+    @pl.when(side != 0)
+    def _():
+        store((send_ref, keep_ref))
 
 
 def latent_cuts(cuts_ref, group):
@@ -281,11 +293,11 @@
     source_ref,
     slab_ref,
     vec_ref,
-    after_ref,
     mix_ref,
     kv_ref,
     lse_ref,
     query_ref,
+    latent_ref,
     mask_ref,
     seg_ref,
 ):
@@ -294,8 +306,10 @@
     @pl.when(step == 0)
     def _():
         fill_block_mask(mask_ref)
+        latent = slab_matrix(slab_ref, LATENT, 2)
+        latent_ref[...] = latent
         low, _, _ = norm_forward(
-            slab_matrix(slab_ref, LATENT, 2).astype(F32),
+            latent.astype(F32),
             vec_ref[ROW_QGAIN : ROW_QGAIN + 1, :],
             vec_ref[ROW_QSHIFT : ROW_QSHIFT + 1, :],
         )
@@ -336,25 +350,25 @@
         return carry
 
     lax.fori_loop(0, CROSS_GROUPS * TILES // UNITS, batch_body, 0)
-    after_ref[...] = (
-        slab_matrix(slab_ref, LATENT, 2).astype(F32)
-        + dot_plain(mix_ref[...], slab_matrix(slab_ref, WO, 2))
-        + vec_ref[ROW_COBIAS : ROW_COBIAS + 1, :]
-    )
 
 
 def middle_kernel(
     cuts_ref,
-    after_ref,
+    side_ref,
+    cross_mix_ref,
     cot_ref,
+    latent_ref,
     slab_ref,
     vec_ref,
-    out_ref,
-    dcross_ref,
+    active_ref,
+    after_self_ref,
+    dcross_mix_ref,
     glat_ref,
     small_ref,
-    gslab_ref,
+    keep_ref,
+    send_ref,
     mask_ref,
+    after_ref,
     hat1_ref,
     rs1_ref,
     low1_ref,
@@ -373,6 +387,7 @@
     aso_ref,
     aup_ref,
     adn_ref,
+    ao_ref,
 ):
     step = pl.program_id(0)
     last = pl.num_programs(0) - 1
@@ -381,13 +396,20 @@
         return vec_ref[row : row + 1, :]
 
     def add_small(row, value):
-        small_ref[row : row + 1, :] += value
+        small_ref[row - CROSS_VECS : row - CROSS_VECS + 1, :] += value
 
     @pl.when(step == 0)
     def _():
         fill_block_mask(mask_ref)
-        for ref in (glat_ref, small_ref, aproj_ref, aso_ref, aup_ref, adn_ref):
+        for ref in (glat_ref, small_ref, aproj_ref, aso_ref, aup_ref, adn_ref, ao_ref):
             ref[...] = jnp.zeros(ref.shape, ref.dtype)
+
+    base = pl.multiple_of(step % (G // SELF_GROUPS) * SELF_ROWS, SELF_ROWS)
+    after_ref[...] = (
+        latent_ref[pl.ds(base, SELF_ROWS), :].astype(F32)
+        + dot_plain(cross_mix_ref[...], slab_matrix(slab_ref, WO, 2))
+        + vec(ROW_COBIAS)
+    )
 
     def first_norm(rows):
         low, normed, rscale = norm_forward(after_ref[rows, :], vec(ROW_SGAIN), vec(ROW_SSHIFT))
@@ -404,39 +426,50 @@
             product = product + vec(bias)
         triple_ref[:, columns] = product.astype(BF16)
 
-    def attend_group(member, carry):
-        start = pl.multiple_of(member * NL, NL)
-        group = pl.ds(start, NL)
+    units = [(member, part) for member in range(SELF_GROUPS) for part in range(2)]
+
+    def group_rows(member):
+        return slice(member * NL, member * NL + NL)
+
+    def block_rows(ref, member, part):
+        starts = range(member * NL, member * NL + NL, QT)
+        return jnp.concatenate(
+            [block_diagonal(ref[at : at + QT, half(part)], mask_ref[...]) for at in starts], 0
+        )
+
+    def unit_scores(member, part):
+        keys = triple_ref[group_rows(member), half(part + 2)]
+        return dot_last(block_rows(triple_ref, member, part), keys)
+
+    ahead = unit_scores(*units[0])
+    for at, (member, part) in enumerate(units):
+        scores = ahead
+        if at + 1 < len(units):
+            ahead = unit_scores(*units[at + 1])
         cuts = latent_cuts(cuts_ref, step * SELF_GROUPS + member)
-        key_seg = segment_at(cuts, lax.broadcasted_iota(jnp.int32, (NL, 128), 0))
-        tiles = [pl.ds(pl.multiple_of(start + tile * QT, QT), QT) for tile in range(TILES)]
-        scores = [
-            dot_last(
-                triple_ref[group, half(part + 2)],
-                block_diagonal(triple_ref[rows, half(part)], mask_ref[...]),
-            )
-            for rows in tiles
-            for part in range(2)
-        ]
+        key_seg = segment_at(cuts, lax.broadcasted_iota(jnp.int32, (QT, NL), 1))
+        place = lax.broadcasted_iota(jnp.int32, (QT, NL), 0)
         probs = []
         for tile in range(TILES):
-            allowed = allowed_pairs(key_seg, query_segments(cuts, tile))
-            for part in range(2):
-                low, _ = softmax_rows(scores[2 * tile + part], allowed)
-                probs.append(low)
-                probs_ref[(member * TILES + tile) * 2 + part] = low
-        for tile, rows in enumerate(tiles):
-            for part in range(2):
-                full = dot_first(probs[2 * tile + part], triple_ref[group, half(part + 4)])
-                mix_ref[rows, half(part)] = take_diagonal(full).astype(BF16)
-        return carry
-
-    lax.fori_loop(0, SELF_GROUPS, attend_group, 0)
-
-    res_ref[...] = after_ref[...] + dot_plain(mix_ref[...], slab_matrix(slab_ref, WSO, 2)) + vec(ROW_SOBIAS)
+            allowed = segment_at(cuts, tile * QT + place) == key_seg
+            block = scores[tile * PACK : tile * PACK + PACK].reshape(PACK // QT, QT, NL)
+            block = jnp.where(allowed[None], block, NEG_FILL)
+            top = jnp.max(block, 2, keepdims=True)
+            powers = jnp.exp2((block - top) * SCALE2)
+            total = jnp.sum(powers, 2, keepdims=True)
+            probs.append((powers * (1.0 / total)).reshape(PACK, NL).astype(BF16))
+        probs = jnp.concatenate(probs, 0)
+        probs_ref[member * 2 + part] = probs
+        full = dot_plain(probs, triple_ref[group_rows(member), half(part + 4)])
+        for tile in range(TILES):
+            rows = slice(member * NL + tile * QT, member * NL + tile * QT + QT)
+            mixed = take_diagonal(full[tile * PACK : tile * PACK + PACK])
+            mix_ref[rows, half(part)] = mixed.astype(BF16)
+
+    after_self_ref[...] = after_ref[...] + dot_plain(mix_ref[...], slab_matrix(slab_ref, WSO, 2)) + vec(ROW_SOBIAS)
 
     def second_norm(rows):
-        low, normed, rscale = norm_forward(res_ref[rows, :], vec(ROW_FGAIN), vec(ROW_FSHIFT))
+        low, normed, rscale = norm_forward(after_self_ref[rows, :], vec(ROW_FGAIN), vec(ROW_FSHIFT))
         low2_ref[rows, :] = low.astype(BF16)
         hat2_ref[rows, :] = normed
         rs2_ref[rows, :] = rscale
@@ -444,46 +477,41 @@
     over_rows(SELF_ROWS, 64, second_norm)
     dtop_ref[...] = jnp.zeros(dtop_ref.shape, F32)
 
-    def feed_block(block, carry):
-        columns = pl.ds(pl.multiple_of(block * D, D), D)
-        offset, height = WUP
-        side = block // 2
-        wup = jnp.concatenate(
+    def feed_front(block):
+        up = slab_part(slab_ref, WUP, *divmod(block, FF // PACK // HALVES))
+        offset, height = WDN
+        chunks = slice(block * PACK // height, (block + 1) * PACK // height)
+        down = jnp.concatenate(
             [
-                slab_ref[
-                    :,
-                    side,
-                    pl.ds(pl.multiple_of(offset + (block % 2 * 2 + piece) * height, height), height),
-                    :,
-                ].reshape(D, PACK)
-                for piece in range(2)
+                slab_ref[chunks, side, offset : offset + height, :].reshape(PACK, PACK)
+                for side in range(HALVES)
             ],
             1,
         )
-        offset, height = WDN
-        chunks = pl.ds(block * (D // height), D // height)
-        wdn = jnp.concatenate(
-            [
-                slab_ref[chunks, piece, offset : offset + height, :].reshape(D, PACK)
-                for piece in range(2)
-            ],
-            1,
-        )
-        hidden = dot_plain(low2_ref[...], wup) + vec_ref[pl.ds(ROW_UBIAS + block, 1), :]
+        row, column = divmod(block * PACK, D)
+        bias = vec_ref[ROW_UBIAS + row : ROW_UBIAS + row + 1, column : column + PACK]
+        hidden = dot_plain(low2_ref[...], up) + bias
+        return up, down, hidden, dot_last(cot_ref[...], down)
+
+    ahead = feed_front(0)
+    for block in range(FF // PACK):
+        up, down, hidden, dactive = ahead
+        if block + 1 < FF // PACK:
+            ahead = feed_front(block + 1)
         active, slope = gelu_pair(hidden)
         active = active.astype(BF16)
-        dhidden = (slope * dot_last(cot_ref[...], wdn)).astype(BF16)
-        small_ref[pl.ds(ROW_UBIAS + block, 1), :] += column_sum(dhidden.astype(F32))
-        res_ref[...] += dot_plain(active, wdn)
+        dhidden = slope * dactive
+        row, column = divmod(block * PACK, D)
+        row += ROW_UBIAS - CROSS_VECS
+        small_ref[row : row + 1, column : column + PACK] += column_sum(dhidden)
+        dhidden = dhidden.astype(BF16)
+        columns = slice(block * PACK, block * PACK + PACK)
         adn_ref[columns, :] += dot_first(active, cot_ref[...])
         aup_ref[:, columns] += dot_first(low2_ref[...], dhidden)
-        dtop_ref[...] += dot_last(dhidden, wup)
-        return carry
-
-    lax.fori_loop(0, FF // D, feed_block, 0)
+        active_ref[:, columns] = active
+        dtop_ref[...] += dot_last(dhidden, up)
 
     def after_feed(rows):
-        out_ref[rows, :] = (res_ref[rows, :] + vec(ROW_DBIAS)).astype(BF16)
         dtop = dtop_ref[rows, :]
         normed = hat2_ref[rows, :]
         cot = cot_ref[rows, :].astype(F32)
@@ -500,81 +528,122 @@
     aso_ref[...] += dot_first(mix_ref[...], dso_ref[...])
     dmix_ref[...] = dot_last(dso_ref[...], slab_matrix(slab_ref, WSO, 2)).astype(BF16)
 
-    def attend_group_back(member, carry):
-        start = pl.multiple_of(member * NL, NL)
-        group = pl.ds(start, NL)
-        tiles = [pl.ds(pl.multiple_of(start + tile * QT, QT), QT) for tile in range(TILES)]
-        for part in range(2):
-            keys = triple_ref[group, half(part + 2)]
-            values = triple_ref[group, half(part + 4)]
-            queries = [block_diagonal(triple_ref[rows, half(part)], mask_ref[...]) for rows in tiles]
-            grads = [block_diagonal(dmix_ref[rows, half(part)], mask_ref[...]) for rows in tiles]
-            dprobs = [dot_last(values, grad) for grad in grads]
-            probs = [probs_ref[(member * TILES + tile) * 2 + part] for tile in range(TILES)]
-            dscores = [score_grads(low.astype(F32), dp) for low, dp in zip(probs, dprobs)]
-            dvalues = dot_plain(jnp.concatenate(probs, 1), jnp.concatenate(grads, 0))
-            dtriple_ref[group, half(part + 4)] = dvalues.astype(BF16)
-            dkeys = dot_plain(jnp.concatenate(dscores, 1), jnp.concatenate(queries, 0))
-            dtriple_ref[group, half(part + 2)] = (dkeys * SCALE).astype(BF16)
-            for rows, dscore in zip(tiles, dscores):
-                dquery = take_diagonal(dot_first(dscore, keys))
-                dtriple_ref[rows, half(part)] = (dquery * SCALE).astype(BF16)
-        return carry
-
-    lax.fori_loop(0, SELF_GROUPS, attend_group_back, 0)
+    def unit_dprobs(member, part):
+        grads = block_rows(dmix_ref, member, part)
+        values = triple_ref[group_rows(member), half(part + 4)]
+        return grads, dot_last(grads, values)
+
+    ahead = unit_dprobs(*units[0])
+    for at, (member, part) in enumerate(units):
+        grads, dprobs = ahead
+        if at + 1 < len(units):
+            ahead = unit_dprobs(*units[at + 1])
+        group = group_rows(member)
+        probs = probs_ref[member * 2 + part]
+        dtriple_ref[group, half(part + 4)] = dot_first(probs, grads).astype(BF16)
+        dscores = []
+        for tile in range(TILES):
+            rows = slice(tile * PACK, tile * PACK + PACK)
+            block = probs[rows].astype(F32)
+            weighted = block * dprobs[rows]
+            delta = jnp.sum(weighted, 1, keepdims=True)
+            dscores.append((weighted - block * delta).astype(BF16))
+        dscores = jnp.concatenate(dscores, 0)
+        dkeys = dot_first(dscores, block_rows(triple_ref, member, part))
+        dtriple_ref[group, half(part + 2)] = (dkeys * SCALE).astype(BF16)
+        full = dot_plain(dscores, triple_ref[group, half(part + 2)])
+        for tile in range(TILES):
+            rows = slice(member * NL + tile * QT, member * NL + tile * QT + QT)
+            dquery = take_diagonal(full[tile * PACK : tile * PACK + PACK])
+            dtriple_ref[rows, half(part)] = (dquery * SCALE).astype(BF16)
     for block in range(3):
         columns = slice(D * block, D * block + D)
         aproj_ref[:, columns] += dot_first(low1_ref[...], dtriple_ref[:, columns])
     add_small(ROW_SQBIAS, column_sum(dtriple_ref[:, :D].astype(F32)))
     add_small(ROW_SVBIAS, column_sum(dtriple_ref[:, 2 * D :].astype(F32)))
     dtop_ref[...] = dot_last(dtriple_ref[...], slab_matrix(slab_ref, WPROJ, 6))
-    base = step % (G // SELF_GROUPS) * SELF_ROWS
 
     def after_self(rows):
         dmid = dtop_ref[rows, :]
         normed = hat1_ref[rows, :]
         dafter = res_ref[rows, :] + norm_backward(dmid, normed, rs1_ref[rows, :], vec(ROW_SGAIN))
-        dcross_ref[rows, :] = dafter.astype(BF16)
+        dlow = dafter.astype(BF16)
+        dso_ref[rows, :] = dlow
         glat_ref[pl.ds(pl.multiple_of(base + rows.start, 64), rows.size), :] += dafter
         add_small(ROW_SGAIN, column_sum(dmid * normed))
         add_small(ROW_SSHIFT, column_sum(dmid))
+        add_small(ROW_COBIAS, column_sum(dlow.astype(F32)))
 
     over_rows(SELF_ROWS, 64, after_self)
+    ao_ref[...] += dot_first(cross_mix_ref[...], dso_ref[...])
+    dcross_mix_ref[...] = dot_last(dso_ref[...], slab_matrix(slab_ref, WO, 2)).astype(BF16)
 
     @pl.when(step == last)
     def _():
-        store_slab(gslab_ref, WPROJ, aproj_ref[...])
-        store_slab(gslab_ref, WSO, aso_ref[...])
-        store_slab(gslab_ref, WUP, aup_ref[...])
-        store_slab(gslab_ref, WDN, adn_ref[...])
+        side = side_ref[0]
+        store_halves(side, keep_ref, send_ref, WPROJ, aproj_ref[...])
+        store_halves(side, keep_ref, send_ref, WSO, aso_ref[...])
+        store_halves(side, keep_ref, send_ref, WUP, aup_ref[...])
+        store_halves(side, keep_ref, send_ref, WDN, adn_ref[...])
+        store_halves(side, keep_ref, send_ref, WO, ao_ref[...])
+
+
+def row_dot(rows, matrix):
+    high = rows.astype(BF16)
+    low = (rows - high.astype(F32)).astype(BF16)
+    return dot_last(high, matrix) + dot_last(low, matrix)
+
+
+def row_sums(matrix):
+    high = matrix.astype(BF16)
+    low = (matrix - high.astype(F32)).astype(BF16)
+    ones = jnp.ones((8, matrix.shape[1]), BF16)
+    return (dot_last(ones, high) + dot_last(ones, low))[:1]
+
+
+VECTOR_PLACES = (
+    (ROW_QGAIN, 0),
+    (ROW_QSHIFT, 0),
+    (ROW_SOURCE, 0),
+    (ROW_SOURCE, CIN),
+    (ROW_QBIAS, 0),
+    (ROW_VBIAS, 0),
+    (ROW_COBIAS, 0),
+    (ROW_SGAIN, 0),
+    (ROW_SSHIFT, 0),
+    (ROW_SQBIAS, 0),
+    (ROW_SVBIAS, 0),
+    (ROW_SOBIAS, 0),
+    (ROW_FGAIN, 0),
+    (ROW_FSHIFT, 0),
+    (ROW_UBIAS, 0),
+    (ROW_DBIAS, 0),
+)
 
 
 def cross_backward_kernel(
     cuts_ref,
     plan_ref,
-    inputs_ref,
+    side_ref,
+    source_ref,
     kv_ref,
-    mix_ref,
     lse_ref,
-    dcross_ref,
+    dmix_ref,
     query_ref,
     glat_ref,
     slab_ref,
     vec_ref,
-    dinput_ref,
-    gslab_ref,
+    dkv_ref,
+    keep_ref,
+    send_ref,
     small_ref,
     mask_ref,
     seg_ref,
-    source_ref,
-    rs_ref,
-    dmix_ref,
     dkey_ref,
     dvalue_ref,
-    dkv_ref,
     dquery_ref,
     akv_ref,
-    ao_ref,
+    dsum_ref,
 ):
     step = pl.program_id(0)
     last = pl.num_programs(0) - 1
@@ -585,27 +654,14 @@
     def add_small(row, value):
         small_ref[row : row + 1, :] += value
 
+    def add_row(ref, value):
+        ref[...] += value
+
     @pl.when(step == 0)
     def _():
         fill_block_mask(mask_ref)
-        for ref in (small_ref, dquery_ref, akv_ref, ao_ref):
+        for ref in (small_ref, dquery_ref, akv_ref, dsum_ref):
             ref[...] = jnp.zeros(ref.shape, ref.dtype)
-
-    source_gain = vec_ref[ROW_SOURCE : ROW_SOURCE + 1, :CIN]
-    source_shift = vec_ref[ROW_SOURCE : ROW_SOURCE + 1, CIN:]
-
-    def source_rows(rows):
-        low, normed, rscale = norm_forward(
-            inputs_ref[rows, :].astype(F32), source_gain, source_shift
-        )
-        source_ref[rows, :] = low.astype(BF16)
-        dinput_ref[rows, :] = normed
-        rs_ref[rows, :] = rscale
-
-    over_rows(IN_STEP, 128, source_rows)
-    ao_ref[...] += dot_first(mix_ref[...], dcross_ref[...])
-    add_small(ROW_COBIAS, column_sum(dcross_ref[...].astype(F32)))
-    dmix_ref[...] = dot_last(dcross_ref[...], slab_matrix(slab_ref, WO, 2)).astype(BF16)
 
     fill_cross_segments(seg_ref, cuts_ref, step)
     dkey_ref[...] = jnp.zeros(dkey_ref.shape, F32)
@@ -645,32 +701,111 @@
     for part in range(2):
         columns = slice(D * part, D * part + D)
         akv_ref[:, columns] += dot_first(source_ref[...], dkv_ref[:, columns])
-    add_small(ROW_VBIAS, column_sum(dkv_ref[:, D:].astype(F32)))
-
-    def source_back(rows):
-        dsource = dot_last(dkv_ref[rows, :], slab_matrix(slab_ref, WKV, 4))
-        normed = dinput_ref[rows, :]
-        small_ref[ROW_SOURCE : ROW_SOURCE + 1, :CIN] += column_sum(dsource * normed)
-        small_ref[ROW_SOURCE : ROW_SOURCE + 1, CIN:] += column_sum(dsource)
-        dinput_ref[rows, :] = norm_backward(dsource, normed, rs_ref[rows, :], source_gain)
-
-    over_rows(IN_STEP, 256, source_back)
+    over_rows(IN_STEP, 256, lambda rows: add_row(dsum_ref, column_sum(dkv_ref[rows, :].astype(F32))))
 
     @pl.when(step == last)
     def _():
-        store_slab(gslab_ref, WKV, akv_ref[...])
-        store_slab(gslab_ref, WO, ao_ref[...])
+        side = side_ref[0]
+        store_halves(side, keep_ref, send_ref, WKV, akv_ref[...])
+        wkv = slab_matrix(slab_ref, WKV, 4)
+        sums = dsum_ref[...]
+        add_small(ROW_VBIAS, sums[:, D:])
+        shift_grad = row_dot(jnp.broadcast_to(sums, (8, 2 * D)), wkv)[:1]
+        product = wkv.astype(F32) * akv_ref[...]
+        both = row_sums(product)
+        gain = vec_ref[ROW_SOURCE : ROW_SOURCE + 1, :CIN]
+        shift = vec_ref[ROW_SOURCE : ROW_SOURCE + 1, CIN:]
+        small_ref[ROW_SOURCE : ROW_SOURCE + 1, :CIN] = (both - shift * shift_grad) / gain
+        small_ref[ROW_SOURCE : ROW_SOURCE + 1, CIN:] = shift_grad
         low, normed, rscale = norm_forward(
             slab_matrix(slab_ref, LATENT, 2).astype(F32), vec(ROW_QGAIN), vec(ROW_QSHIFT)
         )
         dquery = (dquery_ref[...] * SCALE).astype(BF16)
-        store_slab(gslab_ref, WQ, dot_first(low.astype(BF16), dquery))
+        store_halves(side, keep_ref, send_ref, WQ, dot_first(low.astype(BF16), dquery))
         add_small(ROW_QBIAS, column_sum(dquery.astype(F32)))
         dnorm = dot_last(dquery, slab_matrix(slab_ref, WQ, 2))
         add_small(ROW_QGAIN, column_sum(dnorm * normed))
         add_small(ROW_QSHIFT, column_sum(dnorm))
         total = glat_ref[...] + norm_backward(dnorm, normed, rscale, vec(ROW_QGAIN))
-        store_slab(gslab_ref, LATENT, total)
+        store_halves(side, keep_ref, send_ref, LATENT, total)
+
+
+def output_kernel(active_ref, after_self_ref, slab_ref, vec_ref, out_ref):
+    total = after_self_ref[...] + dot_plain(active_ref[...], slab_matrix(slab_ref, WDN, 2))
+    out_ref[...] = (total + vec_ref[ROW_DBIAS : ROW_DBIAS + 1, :]).astype(BF16)
+
+
+def source_kernel(inputs_ref, dkv_ref, slab_ref, vec_ref, dinput_ref):
+    gain = vec_ref[ROW_SOURCE : ROW_SOURCE + 1, :CIN]
+    shift = vec_ref[ROW_SOURCE : ROW_SOURCE + 1, CIN:]
+    wkv = slab_matrix(slab_ref, WKV, 4)
+
+    def source_back(rows):
+        dsource = dot_last(dkv_ref[rows, :], wkv)
+        _, normed, rscale = norm_forward(inputs_ref[rows, :].astype(F32), gain, shift)
+        dinput_ref[rows, :] = norm_backward(dsource, normed, rscale, gain)
+
+    over_rows(IN_STEP, 256, source_back)
+
+
+def pack_kernel(*refs):
+    cross, middle = refs[: len(CROSS_MATS)], refs[len(CROSS_MATS) : -2]
+    copies_ref, packed_ref = refs[-2:]
+    for targets, shards in (((copies_ref, True), cross), ((packed_ref, False), middle)):
+        target_ref, copied = targets
+        start = 0
+        for shard in shards:
+            rows, columns = shard.shape
+            for column in range(0, columns, PACK):
+                part = shard[:, column : column + PACK]
+                if copied:
+                    part = jnp.broadcast_to(part, (CHUNKS, rows, PACK))
+                    target_ref[:, start : start + rows, :] = part
+                else:
+                    target_ref[start : start + rows, :] = part
+                start += rows
+
+
+def combine_kernel(keep_ref, sent_ref, small_ref, small_sent_ref, out_ref):
+    total = keep_ref[...].astype(F32) + sent_ref[...].astype(F32)
+    out_ref[:, :CROSS_SLAB, :] = total.astype(BF16)
+    small = small_ref[...] + small_sent_ref[...]
+    small = jnp.concatenate([small[:, :PACK], small[:, PACK:]], 0)
+    high = small.astype(BF16)
+    low = (small - high.astype(F32)).astype(BF16)
+    rows = 2 * CROSS_VECS
+    for at, part in enumerate((high, low)):
+        start = CROSS_SLAB + at * rows
+        out_ref[:, start : start + rows, :] = jnp.broadcast_to(part, (CHUNKS, rows, PACK))
+
+
+def finish_kernel(parts_ref, middle_ref, small_ref, *outs):
+    mats, vectors = outs[: len(CROSS_MATS) + len(MIDDLE_MATS)], outs[-16:]
+    total = parts_ref[0].astype(F32)
+    for at in range(1, CHUNKS):
+        total = total + parts_ref[at].astype(F32)
+    middle = middle_ref[...].astype(F32)
+    for source, shards in ((total, mats[: len(CROSS_MATS)]), (middle, mats[len(CROSS_MATS) :])):
+        start = 0
+        for shard in shards:
+            rows, columns = shard.shape
+            for column in range(0, columns, PACK):
+                shard[:, column : column + PACK] = source[start : start + rows]
+                start += rows
+    rows = 2 * CROSS_VECS
+    small = total[CROSS_SLAB : CROSS_SLAB + rows] + total[CROSS_SLAB + rows :]
+    small = jnp.concatenate([small[:CROSS_VECS], small[CROSS_VECS:]], 1)
+    write_vectors(jnp.concatenate([small, jnp.sum(small_ref[...], 0)], 0), vectors)
+
+
+def write_vectors(rows, vectors):
+    for ref, (row, start) in zip(vectors, VECTOR_PLACES):
+        size = ref.shape[-1]
+        taken = [
+            rows[row + at : row + at + 1, start : start + min(size, D)]
+            for at in range(max(1, size // D))
+        ]
+        ref[...] = jnp.concatenate(taken, 1)
 
 
 def rows_spec(rows, columns):
@@ -715,30 +850,6 @@
     return jax.ShapeDtypeStruct((CHUNKS, HALVES, rows, PACK), BF16)
 
 
-def pack_shards(shards):
-    return jnp.concatenate(
-        [
-            shard[:, start : start + PACK]
-            for shard in shards
-            for start in range(0, shard.shape[1], PACK)
-        ],
-        0,
-    )
-
-
-def unpack_shards(packed, mats):
-    shards = []
-    start = 0
-    for rows, columns in mats:
-        height = rows // CHUNKS
-        pieces = []
-        for _ in range(columns // (HALVES * PACK)):
-            pieces.append(packed[start : start + height])
-            start += height
-        shards.append(jnp.concatenate(pieces, 1))
-    return shards
-
-
 def gather_whole(shards):
     parts = []
     for shard in shards:
@@ -771,42 +882,48 @@
 SWAP = ((0, 1), (1, 0))
 
 
-def gather_soon(shards):
-    packed = pack_shards(shards)
-    copies = jnp.broadcast_to(packed, (CHUNKS,) + packed.shape)
+def simple_call(kernel, out_shape):
+    return pl.pallas_call(
+        kernel,
+        out_shape=out_shape,
+        compiler_params=pltpu.CompilerParams(vmem_limit_bytes=VMEM_BYTES),
+    )
+
+
+def half_shape(rows):
+    return jax.ShapeDtypeStruct((CHUNKS, rows, PACK), BF16)
+
+
+def half_spec(rows):
+    return pl.BlockSpec(
+        (CHUNKS, rows, PACK), lambda step, *scalars: (0, 0, 0), pipeline_mode=pl.Buffered(1)
+    )
+
+
+def gather_soon(copies):
     mine = lax.all_to_all(copies, "wide", 0, 0)
     other = lax.ppermute(mine, "narrow", SWAP)
     first = lax.axis_index("narrow") == 0
     return jnp.stack([jnp.where(first, mine, other), jnp.where(first, other, mine)], 1)
 
 
-def gather_later(shards):
-    packed = pack_shards(shards)
+def gather_later(packed):
     full = lax.all_gather(packed, ("wide", "narrow"), axis=0)
     return full.reshape((CHUNKS, HALVES) + packed.shape)
 
 
-def sum_halves(slab):
-    first = lax.axis_index("narrow") == 0
-    sent = lax.ppermute(jnp.where(first, slab[:, 1], slab[:, 0]), "narrow", SWAP)
-    kept = jnp.where(first, slab[:, 0], slab[:, 1])
-    return (sent.astype(F32) + kept.astype(F32)).astype(BF16)
-
-
-def scatter_soon(slab, mats):
-    parts = lax.all_to_all(sum_halves(slab), "wide", 0, 0)
-    return unpack_shards(jnp.sum(parts.astype(F32), 0), mats)
-
-
-def sum_small_soon(rows):
-    pair = rows + lax.ppermute(rows, "narrow", SWAP)
-    copies = jnp.broadcast_to(pair, (CHUNKS,) + pair.shape)
-    return jnp.sum(lax.all_to_all(copies, "wide", 0, 0), 0)
-
-
-def scatter_later(slab, mats):
-    total = lax.psum_scatter(sum_halves(slab), "wide", scatter_dimension=0)
-    return unpack_shards(total.astype(F32), mats)
+def scatter_later(keep, send):
+    sent = lax.ppermute(send, "narrow", SWAP)
+    total = (keep.astype(F32) + sent.astype(F32)).astype(BF16)
+    return lax.psum_scatter(total, "wide", scatter_dimension=0)
+
+
+def scatter_soon(keep, send, small):
+    sent = lax.ppermute(send, "narrow", SWAP)
+    small_sent = lax.ppermute(small, "narrow", SWAP)
+    rows = CROSS_SLAB + 4 * CROSS_VECS
+    combined = simple_call(combine_kernel, half_shape(rows))(keep, sent, small, small_sent)
+    return lax.all_to_all(combined, "wide", 0, 0)
 
 
 def shape(rows, columns, dtype):
@@ -859,6 +976,8 @@
             source_shift,
             cross_qbias,
             cross_vbias,
+            jnp.zeros(((ROW_UBIAS - ROW_VBIAS - 1) * D,), BF16),
+            feed_ubias,
             cross_obias,
             self_gain,
             self_shift,
@@ -867,7 +986,6 @@
             self_obias,
             feed_gain,
             feed_shift,
-            feed_ubias,
             feed_dbias,
             jnp.zeros(((VEC_ROWS - ROW_DBIAS - 1) * D,), BF16),
         ]
@@ -885,39 +1003,40 @@
     )
     source_low = source_low.astype(BF16)
 
-    cross_shards = (latent_array, cross_query, cross_keyval, cross_output)
-    middle_shards = (self_project, self_output, feed_upward, feed_downward)
+    cross_shards = (latent_array, cross_query, cross_keyval)
+    middle_shards = (self_project, self_output, feed_upward, feed_downward, cross_output)
     packed = (wide, narrow) == (CHUNKS, HALVES)
     if packed:
-        cross_slab = gather_soon(cross_shards)
-        middle_slab = gather_later(middle_shards)
+        copies, middle_packed = simple_call(
+            pack_kernel, [half_shape(CROSS_SLAB), shape(MIDDLE_SLAB, PACK, BF16)]
+        )(*cross_shards, *middle_shards)
+        cross_slab = gather_soon(copies)
+        middle_slab = gather_later(middle_packed)
+        side = lax.axis_index("narrow").astype(jnp.int32).reshape(1)
     else:
         cross_slab = gather_whole(cross_shards)
         middle_slab = gather_whole(middle_shards)
+        side = jnp.zeros((1,), jnp.int32)
 
     vec_spec = whole_spec(VEC_ROWS, D)
     lse_rows = CROSS_GROUPS * TILES * 2
-    after, cross_mix, keyval, lse, query = kernel_call(
+    cross_mix, keyval, lse, query, latent_full = kernel_call(
         cross_forward_kernel,
         2,
         steps,
-        [
-            rows_spec(IN_STEP, CIN),
-            slab_spec(CROSS_SLAB),
-            vec_spec,
-        ],
-        [
-            rows_spec(LAT_STEP, D),
+        [rows_spec(IN_STEP, CIN), slab_spec(CROSS_SLAB), vec_spec],
+        [
             rows_spec(LAT_STEP, D),
             rows_spec(IN_STEP, 2 * D),
             rows_spec(lse_rows, PACK),
             whole_spec(G * NL, D),
+            whole_spec(G * NL, D),
         ],
         [
-            shape(lat_rows, D, F32),
             shape(lat_rows, D, BF16),
             shape(in_rows, 2 * D, BF16),
             shape(steps * lse_rows, PACK, F32),
+            shape(G * NL, D, BF16),
             shape(G * NL, D, BF16),
         ],
         [
@@ -927,37 +1046,43 @@
         60 * 10**9,
     )(cuts, plan, source_low, cross_slab, vectors)
 
-    latents_out, dcross, glat, middle_small, middle_grads = kernel_call(
+    active, after_self, dcross_mix, glat, middle_small, middle_keep, middle_send = kernel_call(
         middle_kernel,
-        1,
+        2,
         self_steps,
         [
             rows_spec(SELF_ROWS, D),
             rows_spec(SELF_ROWS, D),
+            whole_spec(G * NL, D),
             slab_spec(MIDDLE_SLAB),
             vec_spec,
         ],
         [
+            rows_spec(SELF_ROWS, FF),
             rows_spec(SELF_ROWS, D),
             rows_spec(SELF_ROWS, D),
             whole_spec(G * NL, D),
-            vec_spec,
-            slab_spec(MIDDLE_SLAB),
+            whole_spec(MIDDLE_VECS, D),
+            half_spec(MIDDLE_SLAB),
+            half_spec(MIDDLE_SLAB),
         ],
         [
-            shape(lat_rows, D, BF16),
+            shape(lat_rows, FF, BF16),
+            shape(lat_rows, D, F32),
             shape(lat_rows, D, BF16),
             shape(G * NL, D, F32),
-            shape(VEC_ROWS, D, F32),
-            slab_shape(MIDDLE_SLAB),
+            shape(MIDDLE_VECS, D, F32),
+            half_shape(MIDDLE_SLAB),
+            half_shape(MIDDLE_SLAB),
         ],
         [
             pltpu.VMEM((PACK, PACK), BF16),
+            pltpu.VMEM((SELF_ROWS, D), F32),
             pltpu.VMEM((SELF_ROWS, D), F32),
             pltpu.VMEM((SELF_ROWS, 1), F32),
             pltpu.VMEM((SELF_ROWS, D), BF16),
             pltpu.VMEM((SELF_ROWS, 3 * D), BF16),
-            pltpu.VMEM((SELF_GROUPS * TILES * 2, NL, PACK), BF16),
+            pltpu.VMEM((SELF_GROUPS * 2, TILES * PACK, NL), BF16),
             pltpu.VMEM((SELF_ROWS, D), BF16),
             pltpu.VMEM((SELF_ROWS, D), F32),
             pltpu.VMEM((SELF_ROWS, D), F32),
@@ -971,18 +1096,18 @@
             pltpu.VMEM((D, D), F32),
             pltpu.VMEM((D, FF), F32),
             pltpu.VMEM((FF, D), F32),
+            pltpu.VMEM((D, D), F32),
         ],
         250 * 10**9,
-    )(cuts, after, cotangent, middle_slab, vectors)
-
-    dinput, cross_grads, cross_small = kernel_call(
+    )(cuts, side, cross_mix, cotangent, latent_full, middle_slab, vectors)
+
+    dkeyval, cross_keep, cross_send, cross_small = kernel_call(
         cross_backward_kernel,
-        2,
+        3,
         steps,
         [
             rows_spec(IN_STEP, CIN),
             rows_spec(IN_STEP, 2 * D),
-            rows_spec(LAT_STEP, D),
             rows_spec(lse_rows, PACK),
             rows_spec(LAT_STEP, D),
             whole_spec(G * NL, D),
@@ -991,85 +1116,102 @@
             vec_spec,
         ],
         [
-            rows_spec(IN_STEP, CIN),
-            slab_spec(CROSS_SLAB),
+            rows_spec(IN_STEP, 2 * D),
+            half_spec(CROSS_SLAB),
+            half_spec(CROSS_SLAB),
+            whole_spec(CROSS_VECS, D),
+        ],
+        [
+            shape(in_rows, 2 * D, BF16),
+            half_shape(CROSS_SLAB),
+            half_shape(CROSS_SLAB),
+            shape(CROSS_VECS, D, F32),
+        ],
+        [
+            pltpu.VMEM((PACK, PACK), BF16),
+            pltpu.VMEM((IN_STEP, 128), jnp.int32),
+            pltpu.VMEM((IN_STEP, D), F32),
+            pltpu.VMEM((IN_STEP, D), F32),
+            pltpu.VMEM((G * NL, D), F32),
+            pltpu.VMEM((CIN, 2 * D), F32),
+            pltpu.VMEM((1, 2 * D), F32),
+        ],
+        100 * 10**9,
+    )(cuts, plan, side, source_low, keyval, lse, dcross_mix, query, glat, cross_slab, vectors)
+
+    late_vectors, _ = lax.optimization_barrier((vectors, cross_small))
+    latents_out = kernel_call(
+        output_kernel,
+        0,
+        self_steps,
+        [
+            rows_spec(SELF_ROWS, FF),
+            rows_spec(SELF_ROWS, D),
+            slab_spec(MIDDLE_SLAB),
             vec_spec,
         ],
-        [
-            shape(in_rows, CIN, F32),
-            slab_shape(CROSS_SLAB),
-            shape(VEC_ROWS, D, F32),
-        ],
-        [
-            pltpu.VMEM((PACK, PACK), BF16),
-            pltpu.VMEM((IN_STEP, 128), jnp.int32),
-            pltpu.VMEM((IN_STEP, CIN), BF16),
-            pltpu.VMEM((IN_STEP, 1), F32),
-            pltpu.VMEM((LAT_STEP, D), BF16),
-            pltpu.VMEM((IN_STEP, D), F32),
-            pltpu.VMEM((IN_STEP, D), F32),
-            pltpu.VMEM((IN_STEP, 2 * D), BF16),
-            pltpu.VMEM((G * NL, D), F32),
-            pltpu.VMEM((CIN, 2 * D), F32),
-            pltpu.VMEM((D, D), F32),
-        ],
-        120 * 10**9,
-    )(
-        cuts,
-        plan,
-        inputs,
-        keyval,
-        cross_mix,
-        lse,
-        dcross,
-        query,
-        glat,
-        cross_slab,
-        vectors,
-    )
+        rows_spec(SELF_ROWS, D),
+        shape(lat_rows, D, BF16),
+        [],
+        13 * 10**9,
+    )(active, after_self, middle_slab, late_vectors)
+
+    dinput = kernel_call(
+        source_kernel,
+        0,
+        steps,
+        [rows_spec(IN_STEP, CIN), rows_spec(IN_STEP, 2 * D), slab_spec(CROSS_SLAB), vec_spec],
+        rows_spec(IN_STEP, CIN),
+        shape(in_rows, CIN, F32),
+        [],
+        20 * 10**9,
+    )(inputs, dkeyval, cross_slab, vectors)
 
     axes = ("wide", "narrow")
-    middle_sum = lax.psum(middle_small, axes)[ROW_SGAIN:]
+    vector_sizes = [D, D, CIN, CIN] + [D] * 10 + [FF, D]
     if packed:
-        gproj, gso, gup, gdn = scatter_later(middle_grads, MIDDLE_MATS)
-        cross_sum = sum_small_soon(cross_small[:8])
-        glatent, gq, gkv, go = scatter_soon(cross_grads, CROSS_MATS)
+        middle_total = scatter_later(middle_keep, middle_send)
+        small_all = lax.all_gather(middle_small, axes, axis=0)
+        parts = scatter_soon(cross_keep, cross_send, cross_small)
+        mats = [
+            shape(rows // CHUNKS, columns // HALVES, F32)
+            for rows, columns in CROSS_MATS + MIDDLE_MATS
+        ]
+        results = simple_call(
+            finish_kernel, mats + [shape(1, size, F32) for size in vector_sizes]
+        )(parts, middle_total, small_all)
+        glatent, gq, gkv, gproj, gso, gup, gdn, go = results[:8]
+        sums = [row.reshape(-1) for row in results[8:]]
     else:
-        gproj, gso, gup, gdn = scatter_whole(middle_grads, MIDDLE_MATS)
-        cross_sum = lax.psum(cross_small, axes)
-        glatent, gq, gkv, go = scatter_whole(cross_grads, CROSS_MATS)
-    flat = jnp.concatenate([cross_sum[:ROW_SGAIN].reshape(-1), middle_sum.reshape(-1)])
-
-    def part(row, size, offset=0):
-        return flat[row * D + offset : row * D + offset + size]
+        cross_grads = jnp.stack([cross_keep, cross_send], 1)
+        middle_grads = jnp.stack([middle_keep, middle_send], 1)
+        glatent, gq, gkv = scatter_whole(cross_grads, CROSS_MATS)
+        gproj, gso, gup, gdn, go = scatter_whole(middle_grads, MIDDLE_MATS)
+        total = lax.psum(jnp.concatenate([cross_small, middle_small], 0), axes).reshape(-1)
+        sums = [
+            total[row * D + start : row * D + start + size]
+            for (row, start), size in zip(VECTOR_PLACES, vector_sizes)
+        ]
 
     return (
         latents_out,
         dinput,
         glatent,
-        part(ROW_QGAIN, D),
-        part(ROW_QSHIFT, D),
-        part(ROW_SOURCE, CIN),
-        part(ROW_SOURCE, CIN, CIN),
+        *sums[:4],
         gq,
-        part(ROW_QBIAS, D),
+        sums[4],
         gkv,
-        part(ROW_VBIAS, D),
+        sums[5],
         go,
-        part(ROW_COBIAS, D),
-        part(ROW_SGAIN, D),
-        part(ROW_SSHIFT, D),
+        *sums[6:9],
         gproj,
-        part(ROW_SQBIAS, D),
-        part(ROW_SVBIAS, D),
+        *sums[9:11],
         gso,
-        part(ROW_SOBIAS, D),
-        part(ROW_FGAIN, D),
-        part(ROW_FSHIFT, D),
+        *sums[11:14],
         gup,
-        part(ROW_UBIAS, FF),
+        sums[14],
         gdn,
-        part(ROW_DBIAS, D),
+        sums[15],
     )
 
 

time: 775 us -> 665 us (0.86)
  blocking collectives: 51.7 us -> 0 us
  waiting for transfers between devices: 33 us -> 10.8 us
  other arithmetic: 35.8 us -> 25.7 us
  local copies, waits for them, and re-layouts: 23.1 us -> 13.6 us
    psum x1 -> x0, blocking collectives: 51.7 us -> none  [local(): middle_sum = lax.psum(middle_small, axes)[ROW_SGAIN:]]
    all_to_all x1, waiting for transfers between devices: 16.3 us -> 1.8 us  [gather_soon(): mine = lax.all_to_all(copies, 'wide', 0, 0)]
    all_to_all x2 -> x1, starting transfers between devices: 24.7 us -> 18 us  [scatter_soon(): return lax.all_to_all(combined, 'wide', 0, 0)]
    pallas_call x2 -> x7, Pallas kernels: 485 us -> 482 us  [the longest x1 291 us: local(): kernel_call(middle_kernel, 2, self_steps, [rows_spec(SELF_ROWS, D), rows_...]
  transfers between devices with their start and end apart: 9 -> 9, of which waited for: 5 -> 3; matrix products, arithmetic and copies ran while one was open for 5% -> 6% of each run, Pallas kernels for 32% -> 41%
where the time goes in v3:
time: 665 us; the launch traced here: 660 us
  Pallas kernels  567 us (85%)
  starting transfers between devices  29 us (4%)
  other arithmetic  25.7 us (4%)
  between operations  14.3 us (2%)
  local copies, waits for them, and re-layouts  13.6 us (2%)
  waiting for transfers between devices  10.8 us (2%)
    pallas_call x1, Pallas kernels, local(): kernel_call(middle_kernel, 2, self_steps, [rows_spec(SELF_ROWS, D), rows_...  291 us
    pallas_call x1, Pallas kernels, local(): kernel_call(cross_backward_kernel, 3, steps, [rows_spec(IN_STEP, CIN), ro...  139 us
    pallas_call x1, Pallas kernels, local(): kernel_call(cross_forward_kernel, 2, steps, [rows_spec(IN_STEP, CIN), sla...  85.4 us
    pallas_call x1, Pallas kernels, local(): kernel_call(output_kernel, 0, self_steps, [rows_spec(SELF_ROWS, FF), rows...  24.6 us
    pallas_call x1, Pallas kernels, local(): kernel_call(source_kernel, 0, steps, [rows_spec(IN_STEP, CIN), rows_spec(...  20 us
    all_to_all x1, starting transfers between devices, scatter_soon(): return lax.all_to_all(combined, 'wide', 0, 0)  18 us
  transfers between devices with their start and end apart: 9, of which 3 were waited for; matrix products, arithmetic and copies ran while one was open for 6% of the time, Pallas kernels for 41%

profile of v3, /device:TPU:0, one launch (start us, length us, event | category | flops | bytes accessed | tf_op | source)
XLA Modules:
  0.0 660.5 jit_solution(17222627774804255887)
XLA Ops:
  7.2 2.1 shard_map.467
  9.3 8.3 %all-to-all-start = ((bf16[16,128,256]{2,1,0:T(8,128)(2,1)}), bf16[16,128,256]{2,1,0:T(8,128)(2,1)S(1)}, u32[]{:S(2)}, u32[]{:S(2)}) async-start(bf16[16,128,256]{2,1,0:T(8,128)(2,1)} %get-tuple-element.69), calls=%async_computation | async-start | bytes 2097152 | tf_op jit(solution)/shard_map/all_to_all | solution.py:904
  17.6 0.0 all-gather.5.cloned.1.call-start
  17.7 0.7 all-gather.5.cloned.1.call-update
  18.4 0.0 all-gather.7.cloned.1.call-start
  18.4 0.8 lt.60
  19.3 0.7 lt.64
  20.0 0.7 convert_element_type.49
  20.7 0.7 convert_element_type.50
  21.3 0.9 dynamic-update-slice
  22.2 0.9 dynamic-update-slice.1
  23.0 0.8 dynamic-update-slice.2
  23.9 0.8 dynamic-update-slice.3
  24.7 0.9 dynamic-update-slice.4
  25.6 0.9 dynamic-update-slice.5
  26.4 0.3 dynamic-update-slice.6
  26.7 0.2 convert_reduce_fusion.1
  26.9 0.8 constant_dynamic-update-slice_fusion
  27.8 0.2 convert_reduce_fusion.3
  28.0 0.1 convert_reduce_fusion.4
  28.1 4.9 convert_reduce_fusion
  33.0 3.8 fusion.2
  36.9 7.6 %fusion.5.source_ref = bf16[12288,256]{1,0:T(8,128)(2,1)} fusion(bf16[12288,256]{1,0:T(8,128)(2,1)S(1)} %copy-done, f32[256]{0:T(256)S(1)} %convert_element_type.50, f32[256]{0:T(256)S(1)} %convert_element_type.49, f32[12288]{0:T(1024)S(1)} %add_rsqrt_fusion, f32[12288]{0:T(1024)S(1)} %broadcast_multiply_fusion), kind=kLoop, calls=%fused_computation.7 | loop fusion | flops 18874368 | bytes 12683264 | tf_op jit(solution)/shard_map/convert_element_type | solution.py:1004
  44.5 1.8 all-to-all-done
  46.4 0.1 copy.64
  46.4 0.1 reduce_sum.98
  46.5 0.1 copy.63
  46.6 0.1 reshape.292
  46.7 0.2 dynamic-update-slice.8
  46.8 0.2 dynamic-update-slice.9
  47.1 0.2 dynamic-update-slice.10
  47.3 0.2 dynamic-update-slice.11
  47.5 0.2 dynamic-update-slice.12
  47.7 0.2 dynamic-update-slice.13
  48.0 0.2 dynamic-update-slice.14
  48.2 0.2 dynamic-update-slice.15
  48.4 0.2 dynamic-update-slice.16
  48.6 0.2 dynamic-update-slice.17
  48.8 0.6 reshape.310.vec_ref
  49.5 0.7 copy.67.cuts_ref
  50.2 0.1 convert_reduce_fusion.2
  50.3 0.2 select_reduce_fusion.1
  50.5 0.2 select_reduce_fusion
  50.7 0.7 pad_add_fusion.1.plan_ref
  51.3 0.1 select_bitcast_fusion.1
  51.5 1.6 pad_maximum_fusion.slab_ref
  53.0 85.4 %shard_map.468 = (bf16[6144,512]{1,0:T(8,128)(2,1)}, bf16[12288,1024]{1,0:T(8,128)(2,1)}, f32[384,256]{1,0:T(8,128)}, bf16[1024,512]{1,0:T(8,128)(2,1)}, bf16[1024,512]{1,0:T(8,128)(2,1)}) custom-call(s32[24,8]{1,0:T(8,128)} %copy.67.cuts_ref, s32[6,40]{1,0:T(8,128)} %pad_add_fusion.1.plan_ref, bf16[12288,256]{1,0:T(8,128)(2,1)} %fusion.5.source_ref, ...), custom_call_target="tpu_custom_call" | custom-call | flops 60000002048 | bytes 104857600 | tf_op jit(solution)/shard_map/pallas_call | solution.py:1023
  138.5 290.6 %shard_map.469 = (bf16[6144,2048]{1,0:T(8,128)(2,1)}, f32[6144,512]{1,0:T(8,128)}, bf16[6144,512]{1,0:T(8,128)(2,1)}, f32[1024,512]{1,0:T(8,128)}, f32[16,512]{1...) custom-call(s32[24,8]{1,0:T(8,128)} %copy.67.cuts_ref, s32[1]{0:T(128)} %bitcast.side_ref, ...), custom_call_target="tpu_custom_call" | custom-call | flops 249999998976 | bytes 104857600 | tf_op jit(solution)/shard_map/pallas_call | solution.py:1049
  429.0 0.7 collective-permute-start.3
  429.8 0.0 reduce-scatter.2.cloned.1.call-start
  429.8 5.8 collective-permute-done.3
  435.6 4.7 add_convert_fusion
  440.3 138.9 %shard_map.470 = (bf16[12288,1024]{1,0:T(8,128)(2,1)}, bf16[16,128,256]{2,1,0:T(8,128)(2,1)}, bf16[16,128,256]{2,1,0:T(8,128)(2,1)}, f32[8,512]{1,0:T(8,128)}) custom-call(s32[24,8]{1,0:T(8,128)} %copy.67.cuts_ref, s32[6,40]{1,0:T(8,128)} %pad_add_fusion.1.plan_ref, s32[1]{0:T(128)} %bitcast.side_ref, bf16[12288,256]{1,0:T(8,128)(2,1)} %fusion.5.source_ref, ...), custom_call_target="tpu_custom_call" | custom-call | flops 99999997952 | bytes 104857600 | tf_op jit(solution)/shard_map/pallas_call | solution.py:1104
  579.3 1.8 collective-permute-start.1
  581.0 0.1 collective-permute-start.2
  581.1 2.4 collective-permute-done.2.small_sent_ref
  583.5 0.6 copy-done.3
  584.1 0.4 copy-done.2
  584.5 2.8 shard_map.473
  587.4 18.0 %all-to-all-start.1 = ((bf16[16,160,256]{2,1,0:T(8,128)(2,1)}), bf16[16,160,256]{2,1,0:T(8,128)(2,1)S(1)}, u32[]{:S(2)}, u32[]{:S(2)}) async-start(bf16[16,160,256]{2,1,0:T(8,128)(2,1)} %shard_map.473), calls=%async_computation.1 | async-start | bytes 2621440 | tf_op jit(solution)/shard_map/all_to_all | solution.py:926
  605.4 24.6 %shard_map.471 = bf16[6144,512]{1,0:T(8,128)(2,1)} custom-call(bf16[6144,2048]{1,0:T(8,128)(2,1)} %get-tuple-element.73.active_ref, f32[6144,512]{1,0:T(8,128)} %get-tuple-element.74.after_self_ref, bf16[16,2,416,256]{3,2,1,0:T(8,128)(2,1)} %bitcast.27, f32[24,512]{1,0:T(8,128)} %reshape.310.vec_ref), custom_call_target="tpu_custom_call" | custom-call | flops 12999999488 | bytes 104857600 | tf_op jit(solution)/shard_map/pallas_call | solution.py:1143
  629.9 20.0 %shard_map.472 = f32[12288,256]{1,0:T(8,128)} custom-call(bf16[12288,256]{1,0:T(8,128)(2,1)} %inputs_ref.1, bf16[12288,1024]{1,0:T(8,128)(2,1)} %get-tuple-element.82.dkv_ref, bf16[16,2,128,256]{3,2,1,0:T(8,128)(2,1)} %pad_maximum_fusion.slab_ref, f32[24,512]{1,0:T(8,128)} %reshape.310.vec_ref), custom_call_target="tpu_custom_call" | custom-call | flops 20000000000 | bytes 104857600 | tf_op jit(solution)/shard_map/pallas_call | solution.py:1159
  650.0 1.0 copy-done.1
  651.0 2.7 shard_map.474
  (47 shorter events, 0.3 us)
Async XLA Ops:
  9.3 37.0 %all-to-all-start = ((bf16[16,128,256]{2,1,0:T(8,128)(2,1)}), bf16[16,128,256]{2,1,0:T(8,128)(2,1)S(1)}, u32[]{:S(2)}, u32[]{:S(2)}) async-start(bf16[16,128,256]{2,1,0:T(8,128)(2,1)} %get-tuple-element.69), calls=%async_computation | async-start | bytes 2097152 | tf_op jit(solution)/shard_map/all_to_all | solution.py:904
  17.6 120.8 %all-gather.5.cloned.1.call-start = ((), (), s32[]{:S(2)}) async-start(), calls=%async_computation.4 | async-start | bytes 7028736 | tf_op jit(solution)/shard_map/all_gather | solution.py:911
  18.4 631.6 %all-gather.7.cloned.1.call-start = ((), (), s32[]{:S(2)}) async-start(), calls=%async_computation.5 | async-start | bytes 1081344 | tf_op jit(solution)/shard_map/all_gather | solution.py:1174
  26.7 6.3 copy-start
  36.8 9.8 %copy-start.4 = (bf16[512]{0:T(512)(128)(2,1)S(1)}, bf16[512]{0:T(512)(128)(2,1)}, u32[]{:S(2)}) copy-start(bf16[512]{0:T(512)(128)(2,1)} %param.42) | copy-start | bytes 3076
  36.8 10.0 %copy-start.5 = (bf16[512]{0:T(512)(128)(2,1)S(1)}, bf16[512]{0:T(512)(128)(2,1)}, u32[]{:S(2)}) copy-start(bf16[512]{0:T(512)(128)(2,1)} %param.43) | copy-start | bytes 3076
  36.8 10.2 %copy-start.6 = (bf16[512]{0:T(512)(128)(2,1)S(1)}, bf16[512]{0:T(512)(128)(2,1)}, u32[]{:S(2)}) copy-start(bf16[512]{0:T(512)(128)(2,1)} %param.44) | copy-start | bytes 3076
  36.8 10.4 %copy-start.7 = (bf16[512]{0:T(512)(128)(2,1)S(1)}, bf16[512]{0:T(512)(128)(2,1)}, u32[]{:S(2)}) copy-start(bf16[512]{0:T(512)(128)(2,1)} %param.46) | copy-start | bytes 3076
  36.9 10.6 %copy-start.8 = (bf16[512]{0:T(512)(128)(2,1)S(1)}, bf16[512]{0:T(512)(128)(2,1)}, u32[]{:S(2)}) copy-start(bf16[512]{0:T(512)(128)(2,1)} %param.47) | copy-start | bytes 3076
  36.9 10.9 %copy-start.9 = (bf16[512]{0:T(512)(128)(2,1)S(1)}, bf16[512]{0:T(512)(128)(2,1)}, u32[]{:S(2)}) copy-start(bf16[512]{0:T(512)(128)(2,1)} %param.49) | copy-start | bytes 3076
  36.9 11.1 %copy-start.10 = (bf16[512]{0:T(512)(128)(2,1)S(1)}, bf16[512]{0:T(512)(128)(2,1)}, u32[]{:S(2)}) copy-start(bf16[512]{0:T(512)(128)(2,1)} %param.50) | copy-start | bytes 3076
  36.9 11.3 %copy-start.11 = (bf16[512]{0:T(512)(128)(2,1)S(1)}, bf16[512]{0:T(512)(128)(2,1)}, u32[]{:S(2)}) copy-start(bf16[512]{0:T(512)(128)(2,1)} %param.51) | copy-start | bytes 3076
  36.9 11.5 %copy-start.12 = (bf16[512]{0:T(512)(128)(2,1)S(1)}, bf16[512]{0:T(512)(128)(2,1)}, u32[]{:S(2)}) copy-start(bf16[512]{0:T(512)(128)(2,1)} %param.55) | copy-start | bytes 3076
  46.3 5.0 collective-permute-start
  429.0 6.6 collective-permute-start.3
  429.8 220.2 %reduce-scatter.2.cloned.1.call-start = ((), (), s32[]{:S(2)}) async-start(), calls=%async_computation.3 | async-start | bytes 3620864 | tf_op jit(solution)/shard_map/reduce_scatter | solution.py:918
  579.3 4.3 collective-permute-start.1
  581.0 2.5 collective-permute-start.2
  583.5 0.6 copy-start.3
  583.5 1.0 copy-start.2
  587.4 62.6 %all-to-all-start.1 = ((bf16[16,160,256]{2,1,0:T(8,128)(2,1)}), bf16[16,160,256]{2,1,0:T(8,128)(2,1)S(1)}, u32[]{:S(2)}, u32[]{:S(2)}) async-start(bf16[16,160,256]{2,1,0:T(8,128)(2,1)} %shard_map.473), calls=%async_computation.1 | async-start | bytes 2621440 | tf_op jit(solution)/shard_map/all_to_all | solution.py:926
  650.0 1.1 copy-start.1
Sparse Core Ops, SparseCore 0:
  21.3 75.3 all-gather.4
  429.9 57.6 all-gather.6
  489.9 83.9 reduce-scatter.1

commit v4 on v3

--- a/solution.py
+++ b/solution.py
@@ -158,15 +158,16 @@
     return result
 
 
-def in_widths(needed, body):
-    smaller = 0
-    for width in WIDTHS:
-
-        @pl.when((needed > smaller) & (needed <= width))
-        def _(width=width):
-            body(width)
-
-        smaller = width
+def in_widths(plan_ref, step, body):
+    first = CROSS_GROUPS * TILES
+
+    for at, width in enumerate(WIDTHS):
+
+        def batch_body(batch, carry, width=width):
+            body(batch, width)
+            return carry
+
+        lax.fori_loop(plan_ref[step, first + at], plan_ref[step, first + at + 1], batch_body, 0)
 
 
 def query_segments(query_cuts, tile):
@@ -256,10 +257,6 @@
         allowed = allowed_pairs(seg_ref[keys, :], query_segments(cuts, tile))
         units.append((slot, pl.ds(pl.multiple_of(slot * QT, QT), QT), keys, allowed))
     return units
-
-
-def batch_needed(plan_ref, step, batch):
-    return plan_ref[step, CROSS_GROUPS * TILES + batch]
 
 
 def plan_tiles(in_cuts, lat_cuts):
@@ -284,7 +281,9 @@
     batches = jnp.arange(count // UNITS, dtype=jnp.int32)[:, None]
     inside = rank[:, None, :] // UNITS == batches
     widest = jnp.max(jnp.where(inside, needed[:, None, :], 0), -1)
-    return jnp.concatenate([packed, widest], 1).astype(jnp.int32)
+    widths = jnp.array((0,) + WIDTHS, jnp.int32)
+    bounds = jnp.sum(widest[:, :, None] <= widths, 1, dtype=jnp.int32)
+    return jnp.concatenate([packed, bounds], 1).astype(jnp.int32)
 
 
 def cross_forward_kernel(
@@ -324,32 +323,28 @@
 
     fill_cross_segments(seg_ref, cuts_ref, step)
 
-    def batch_body(batch, carry):
-        def window(width):
-            units = cross_units(plan_ref, cuts_ref, seg_ref, step, batch, width)
-            scores = [
-                dot_last(
-                    kv_ref[keys, half(part)],
-                    block_diagonal(query_ref[rows, half(part)], mask_ref[...]),
-                )
-                for _, rows, keys, _ in units
-                for part in range(2)
-            ]
-            probs = []
-            for at, (slot, _, _, allowed) in enumerate(units):
-                for part in range(2):
-                    low, lse = softmax_rows(scores[2 * at + part], allowed)
-                    probs.append(low)
-                    lse_ref[pl.ds(slot * 2 + part, 1), :] = lse
-            for at, (_, rows, keys, _) in enumerate(units):
-                for part in range(2):
-                    full = dot_first(probs[2 * at + part], kv_ref[keys, half(part + 2)])
-                    mix_ref[rows, half(part)] = take_diagonal(full).astype(BF16)
-
-        in_widths(batch_needed(plan_ref, step, batch), window)
-        return carry
-
-    lax.fori_loop(0, CROSS_GROUPS * TILES // UNITS, batch_body, 0)
+    def window(batch, width):
+        units = cross_units(plan_ref, cuts_ref, seg_ref, step, batch, width)
+        scores = [
+            dot_last(
+                kv_ref[keys, half(part)],
+                block_diagonal(query_ref[rows, half(part)], mask_ref[...]),
+            )
+            for _, rows, keys, _ in units
+            for part in range(2)
+        ]
+        probs = []
+        for at, (slot, _, _, allowed) in enumerate(units):
+            for part in range(2):
+                low, lse = softmax_rows(scores[2 * at + part], allowed)
+                probs.append(low)
+                lse_ref[pl.ds(slot * 2 + part, 1), :] = lse
+        for at, (_, rows, keys, _) in enumerate(units):
+            for part in range(2):
+                full = dot_first(probs[2 * at + part], kv_ref[keys, half(part + 2)])
+                mix_ref[rows, half(part)] = take_diagonal(full).astype(BF16)
+
+    in_widths(plan_ref, step, window)
 
 
 def middle_kernel(
@@ -667,34 +662,30 @@
     dkey_ref[...] = jnp.zeros(dkey_ref.shape, F32)
     dvalue_ref[...] = jnp.zeros(dvalue_ref.shape, F32)
 
-    def batch_body(batch, carry):
-        def window(width):
-            units = cross_units(plan_ref, cuts_ref, seg_ref, step, batch, width)
-            work = []
-            for slot, rows, keys, allowed in units:
-                for part in range(2):
-                    queries = block_diagonal(query_ref[rows, half(part)], mask_ref[...])
-                    grads = block_diagonal(dmix_ref[rows, half(part)], mask_ref[...])
-                    scores = dot_last(kv_ref[keys, half(part)], queries)
-                    dprobs = dot_last(kv_ref[keys, half(part + 2)], grads)
-                    work.append((slot, rows, keys, allowed, part, queries, grads, scores, dprobs))
-            ready = []
-            for slot, rows, keys, allowed, part, queries, grads, scores, dprobs in work:
-                lse = lse_ref[pl.ds(slot * 2 + part, 1), :]
-                probs = jnp.exp2(jnp.where(allowed, scores * SCALE2 - lse, NEG_FILL))
-                dscores = score_grads(probs, dprobs)
-                ready.append((rows, keys, part, queries, grads, probs.astype(BF16), dscores))
-            for rows, keys, part, queries, grads, probs, dscores in ready:
-                dvalue_ref[keys, half(part)] += dot_plain(probs, grads)
-                dkey_ref[keys, half(part)] += dot_plain(dscores, queries)
-                dquery_ref[rows, half(part)] += take_diagonal(
-                    dot_first(dscores, kv_ref[keys, half(part)])
-                )
-
-        in_widths(batch_needed(plan_ref, step, batch), window)
-        return carry
-
-    lax.fori_loop(0, CROSS_GROUPS * TILES // UNITS, batch_body, 0)
+    def window(batch, width):
+        units = cross_units(plan_ref, cuts_ref, seg_ref, step, batch, width)
+        work = []
+        for slot, rows, keys, allowed in units:
+            for part in range(2):
+                queries = block_diagonal(query_ref[rows, half(part)], mask_ref[...])
+                grads = block_diagonal(dmix_ref[rows, half(part)], mask_ref[...])
+                scores = dot_last(kv_ref[keys, half(part)], queries)
+                dprobs = dot_last(kv_ref[keys, half(part + 2)], grads)
+                work.append((slot, rows, keys, allowed, part, queries, grads, scores, dprobs))
+        ready = []
+        for slot, rows, keys, allowed, part, queries, grads, scores, dprobs in work:
+            lse = lse_ref[pl.ds(slot * 2 + part, 1), :]
+            probs = jnp.exp2(jnp.where(allowed, scores * SCALE2 - lse, NEG_FILL))
+            dscores = score_grads(probs, dprobs)
+            ready.append((rows, keys, part, queries, grads, probs.astype(BF16), dscores))
+        for rows, keys, part, queries, grads, probs, dscores in ready:
+            dvalue_ref[keys, half(part)] += dot_plain(probs, grads)
+            dkey_ref[keys, half(part)] += dot_plain(dscores, queries)
+            dquery_ref[rows, half(part)] += take_diagonal(
+                dot_first(dscores, kv_ref[keys, half(part)])
+            )
+
+    in_widths(plan_ref, step, window)
     dkv_ref[:, :D] = (dkey_ref[...] * SCALE).astype(BF16)
     dkv_ref[:, D:] = dvalue_ref[...].astype(BF16)
 
@@ -1143,14 +1134,14 @@
     latents_out = kernel_call(
         output_kernel,
         0,
-        self_steps,
-        [
-            rows_spec(SELF_ROWS, FF),
-            rows_spec(SELF_ROWS, D),
+        steps,
+        [
+            rows_spec(LAT_STEP, FF),
+            rows_spec(LAT_STEP, D),
             slab_spec(MIDDLE_SLAB),
             vec_spec,
         ],
-        rows_spec(SELF_ROWS, D),
+        rows_spec(LAT_STEP, D),
         shape(lat_rows, D, BF16),
         [],
         13 * 10**9,

time: 665 us -> 657 us (0.988)
  starting transfers between devices: 29 us -> 19.1 us
    all_to_all x1, starting transfers between devices: 18 us -> 10 us  [scatter_soon(): return lax.all_to_all(combined, 'wide', 0, 0)]
  transfers between devices with their start and end apart: 9 -> 9, of which waited for: 3 -> 3; matrix products, arithmetic and copies ran while one was open for 6% -> 6% of each run, Pallas kernels for 41% -> 42%
where the time goes in v4:
time: 657 us; the launch traced here: 649 us
  Pallas kernels  565 us (86%)
  other arithmetic  25.8 us (4%)
  starting transfers between devices  19.1 us (3%)
  between operations  14.3 us (2%)
  local copies, waits for them, and re-layouts  13.6 us (2%)
  waiting for transfers between devices  11.1 us (2%)
    pallas_call x1, Pallas kernels, local(): kernel_call(middle_kernel, 2, self_steps, [rows_spec(SELF_ROWS, D), rows_...  291 us
    pallas_call x1, Pallas kernels, local(): kernel_call(cross_backward_kernel, 3, steps, [rows_spec(IN_STEP, CIN), ro...  141 us
    pallas_call x1, Pallas kernels, local(): kernel_call(cross_forward_kernel, 2, steps, [rows_spec(IN_STEP, CIN), sla...  84.4 us
    pallas_call x1, Pallas kernels, local(): kernel_call(output_kernel, 0, steps, [rows_spec(LAT_STEP, FF), rows_spec(...  21.9 us
    pallas_call x1, Pallas kernels, local(): kernel_call(source_kernel, 0, steps, [rows_spec(IN_STEP, CIN), rows_spec(...  20 us
  transfers between devices with their start and end apart: 9, of which 3 were waited for; matrix products, arithmetic and copies ran while one was open for 6% of the time, Pallas kernels for 42%

profile of v4, /device:TPU:0, one launch (start us, length us, event | category | flops | bytes accessed | tf_op | source)
XLA Modules:
  0.0 649.0 jit_solution(12288485249677169148)
XLA Ops:
  7.2 2.1 shard_map.476
  9.3 8.3 %all-to-all-start = ((bf16[16,128,256]{2,1,0:T(8,128)(2,1)}), bf16[16,128,256]{2,1,0:T(8,128)(2,1)S(1)}, u32[]{:S(2)}, u32[]{:S(2)}) async-start(bf16[16,128,256]{2,1,0:T(8,128)(2,1)} %get-tuple-element.69), calls=%async_computation | async-start | bytes 2097152 | tf_op jit(solution)/shard_map/all_to_all | solution.py:895
  17.6 0.0 all-gather.5.cloned.1.call-start
  17.7 0.7 all-gather.5.cloned.1.call-update
  18.5 0.8 lt.60
  19.3 0.7 lt.64
  20.0 0.7 convert_element_type.53
  20.7 0.7 convert_element_type.54
  21.3 0.9 dynamic-update-slice
  22.2 0.9 dynamic-update-slice.1
  23.0 0.8 dynamic-update-slice.2
  23.9 0.8 dynamic-update-slice.3
  24.7 0.9 dynamic-update-slice.4
  25.6 0.9 dynamic-update-slice.5
  26.4 0.3 dynamic-update-slice.6
  26.7 0.2 convert_reduce_fusion.1
  27.0 0.8 constant_dynamic-update-slice_fusion
  27.8 0.2 convert_reduce_fusion.3
  28.0 0.1 convert_reduce_fusion.5
  28.1 4.9 convert_reduce_fusion
  33.0 3.8 fusion.2
  37.0 7.6 %fusion.5.source_ref = bf16[12288,256]{1,0:T(8,128)(2,1)} fusion(bf16[12288,256]{1,0:T(8,128)(2,1)S(1)} %copy-done, f32[256]{0:T(256)S(1)} %convert_element_type.54, f32[256]{0:T(256)S(1)} %convert_element_type.53, f32[12288]{0:T(1024)S(1)} %add_rsqrt_fusion, f32[12288]{0:T(1024)S(1)} %broadcast_multiply_fusion), kind=kLoop, calls=%fused_computation.7 | loop fusion | flops 18874368 | bytes 12683264 | tf_op jit(solution)/shard_map/convert_element_type | solution.py:995
  44.6 1.8 all-to-all-done
  46.4 0.1 copy.65
  46.4 0.1 reduce_sum.107
  46.5 0.1 copy.64
  46.6 0.1 reshape.294
  46.7 0.2 dynamic-update-slice.8
  46.8 0.2 dynamic-update-slice.9
  47.1 0.2 dynamic-update-slice.10
  47.3 0.2 dynamic-update-slice.11
  47.5 0.2 dynamic-update-slice.12
  47.7 0.2 dynamic-update-slice.13
  48.0 0.2 dynamic-update-slice.14
  48.2 0.2 dynamic-update-slice.15
  48.4 0.2 dynamic-update-slice.16
  48.6 0.2 dynamic-update-slice.17
  48.8 0.6 reshape.312.vec_ref
  49.5 0.7 copy.68.cuts_ref
  50.2 0.1 convert_reduce_fusion.2
  50.3 0.2 select_reduce_fusion.1
  50.5 0.1 convert_reduce_fusion.4
  50.6 0.2 select_reduce_fusion
  50.8 0.7 pad_add_fusion.1.plan_ref
  51.4 0.1 select_bitcast_fusion.1
  51.6 1.6 pad_maximum_fusion.slab_ref
  53.1 84.4 %shard_map.477 = (bf16[6144,512]{1,0:T(8,128)(2,1)}, bf16[12288,1024]{1,0:T(8,128)(2,1)}, f32[384,256]{1,0:T(8,128)}, bf16[1024,512]{1,0:T(8,128)(2,1)}, bf16[1024,512]{1,0:T(8,128)(2,1)}) custom-call(s32[24,8]{1,0:T(8,128)} %copy.68.cuts_ref, s32[6,38]{1,0:T(8,128)} %pad_add_fusion.1.plan_ref, bf16[12288,256]{1,0:T(8,128)(2,1)} %fusion.5.source_ref, ...), custom_call_target="tpu_custom_call" | custom-call | flops 60000002048 | bytes 104857600 | tf_op jit(solution)/shard_map/pallas_call | solution.py:1014
  137.6 290.6 %shard_map.478 = (bf16[6144,2048]{1,0:T(8,128)(2,1)}, f32[6144,512]{1,0:T(8,128)}, bf16[6144,512]{1,0:T(8,128)(2,1)}, f32[1024,512]{1,0:T(8,128)}, f32[16,512]{1...) custom-call(s32[24,8]{1,0:T(8,128)} %copy.68.cuts_ref, s32[1]{0:T(128)} %bitcast.side_ref, ...), custom_call_target="tpu_custom_call" | custom-call | flops 249999998976 | bytes 104857600 | tf_op jit(solution)/shard_map/pallas_call | solution.py:1040
  428.1 0.1 collective-permute-start.3
  428.2 0.0 reduce-scatter.2.cloned.1.call-start
  428.3 6.2 collective-permute-done.3
  434.5 4.7 add_convert_fusion
  439.2 140.6 %shard_map.479 = (bf16[12288,1024]{1,0:T(8,128)(2,1)}, bf16[16,128,256]{2,1,0:T(8,128)(2,1)}, bf16[16,128,256]{2,1,0:T(8,128)(2,1)}, f32[8,512]{1,0:T(8,128)}) custom-call(s32[24,8]{1,0:T(8,128)} %copy.68.cuts_ref, s32[6,38]{1,0:T(8,128)} %pad_add_fusion.1.plan_ref, s32[1]{0:T(128)} %bitcast.side_ref, bf16[12288,256]{1,0:T(8,128)(2,1)} %fusion.5.source_ref, ...), custom_call_target="tpu_custom_call" | custom-call | flops 99999997952 | bytes 104857600 | tf_op jit(solution)/shard_map/pallas_call | solution.py:1095
  579.8 0.1 collective-permute-start.1
  579.8 0.5 collective-permute-start.2
  580.3 2.4 collective-permute-done.2.small_sent_ref
  582.7 0.6 copy-done.3
  583.3 0.4 copy-done.2
  583.7 2.9 shard_map.482
  586.6 10.0 %all-to-all-start.1 = ((bf16[16,160,256]{2,1,0:T(8,128)(2,1)}), bf16[16,160,256]{2,1,0:T(8,128)(2,1)S(1)}, u32[]{:S(2)}, u32[]{:S(2)}) async-start(bf16[16,160,256]{2,1,0:T(8,128)(2,1)} %shard_map.482), calls=%async_computation.1 | async-start | bytes 2621440 | tf_op jit(solution)/shard_map/all_to_all | solution.py:917
  596.6 21.9 %shard_map.480 = bf16[6144,512]{1,0:T(8,128)(2,1)} custom-call(bf16[6144,2048]{1,0:T(8,128)(2,1)} %get-tuple-element.73.active_ref, f32[6144,512]{1,0:T(8,128)} %get-tuple-element.74.after_self_ref, bf16[16,2,416,256]{3,2,1,0:T(8,128)(2,1)} %bitcast.27, f32[24,512]{1,0:T(8,128)} %reshape.312.vec_ref), custom_call_target="tpu_custom_call" | custom-call | flops 12999999488 | bytes 104857600 | tf_op jit(solution)/shard_map/pallas_call | solution.py:1134
  618.5 20.0 %shard_map.481 = f32[12288,256]{1,0:T(8,128)} custom-call(bf16[12288,256]{1,0:T(8,128)(2,1)} %inputs_ref.1, bf16[12288,1024]{1,0:T(8,128)(2,1)} %get-tuple-element.82.dkv_ref, bf16[16,2,128,256]{3,2,1,0:T(8,128)(2,1)} %pad_maximum_fusion.slab_ref, f32[24,512]{1,0:T(8,128)} %reshape.312.vec_ref), custom_call_target="tpu_custom_call" | custom-call | flops 20000000000 | bytes 104857600 | tf_op jit(solution)/shard_map/pallas_call | solution.py:1150
  638.5 1.0 copy-done.1
  639.6 2.7 shard_map.483
  (50 shorter events, 0.3 us)
Async XLA Ops:
  9.3 37.0 %all-to-all-start = ((bf16[16,128,256]{2,1,0:T(8,128)(2,1)}), bf16[16,128,256]{2,1,0:T(8,128)(2,1)S(1)}, u32[]{:S(2)}, u32[]{:S(2)}) async-start(bf16[16,128,256]{2,1,0:T(8,128)(2,1)} %get-tuple-element.69), calls=%async_computation | async-start | bytes 2097152 | tf_op jit(solution)/shard_map/all_to_all | solution.py:895
  17.6 119.9 %all-gather.5.cloned.1.call-start = ((), (), s32[]{:S(2)}) async-start(), calls=%async_computation.4 | async-start | bytes 7028736 | tf_op jit(solution)/shard_map/all_gather | solution.py:902
  18.4 620.1 %all-gather.7.cloned.1.call-start = ((), (), s32[]{:S(2)}) async-start(), calls=%async_computation.5 | async-start | bytes 1081344 | tf_op jit(solution)/shard_map/all_gather | solution.py:1165
  26.7 6.3 copy-start
  36.8 9.8 %copy-start.4 = (bf16[512]{0:T(512)(128)(2,1)S(1)}, bf16[512]{0:T(512)(128)(2,1)}, u32[]{:S(2)}) copy-start(bf16[512]{0:T(512)(128)(2,1)} %param.43) | copy-start | bytes 3076
  36.9 10.0 %copy-start.5 = (bf16[512]{0:T(512)(128)(2,1)S(1)}, bf16[512]{0:T(512)(128)(2,1)}, u32[]{:S(2)}) copy-start(bf16[512]{0:T(512)(128)(2,1)} %param.44) | copy-start | bytes 3076
  36.9 10.2 %copy-start.6 = (bf16[512]{0:T(512)(128)(2,1)S(1)}, bf16[512]{0:T(512)(128)(2,1)}, u32[]{:S(2)}) copy-start(bf16[512]{0:T(512)(128)(2,1)} %param.45) | copy-start | bytes 3076
  36.9 10.4 %copy-start.7 = (bf16[512]{0:T(512)(128)(2,1)S(1)}, bf16[512]{0:T(512)(128)(2,1)}, u32[]{:S(2)}) copy-start(bf16[512]{0:T(512)(128)(2,1)} %param.47) | copy-start | bytes 3076
  36.9 10.6 %copy-start.8 = (bf16[512]{0:T(512)(128)(2,1)S(1)}, bf16[512]{0:T(512)(128)(2,1)}, u32[]{:S(2)}) copy-start(bf16[512]{0:T(512)(128)(2,1)} %param.48) | copy-start | bytes 3076
  36.9 10.8 %copy-start.9 = (bf16[512]{0:T(512)(128)(2,1)S(1)}, bf16[512]{0:T(512)(128)(2,1)}, u32[]{:S(2)}) copy-start(bf16[512]{0:T(512)(128)(2,1)} %param.50) | copy-start | bytes 3076
  36.9 11.0 %copy-start.10 = (bf16[512]{0:T(512)(128)(2,1)S(1)}, bf16[512]{0:T(512)(128)(2,1)}, u32[]{:S(2)}) copy-start(bf16[512]{0:T(512)(128)(2,1)} %param.51) | copy-start | bytes 3076
  36.9 11.3 %copy-start.11 = (bf16[512]{0:T(512)(128)(2,1)S(1)}, bf16[512]{0:T(512)(128)(2,1)}, u32[]{:S(2)}) copy-start(bf16[512]{0:T(512)(128)(2,1)} %param.52) | copy-start | bytes 3076
  36.9 11.5 %copy-start.12 = (bf16[512]{0:T(512)(128)(2,1)S(1)}, bf16[512]{0:T(512)(128)(2,1)}, u32[]{:S(2)}) copy-start(bf16[512]{0:T(512)(128)(2,1)} %param.56) | copy-start | bytes 3076
  36.9 13.5 %copy-start.13 = (s32[6]{0:T(128)S(1)}, s32[6]{0:T(128)}, u32[]{:S(2)}) copy-start(s32[6]{0:T(128)} %constant.60.clone) | copy-start | bytes 76
  46.4 5.1 collective-permute-start
  428.1 6.3 collective-permute-start.3
  428.2 210.3 %reduce-scatter.2.cloned.1.call-start = ((), (), s32[]{:S(2)}) async-start(), calls=%async_computation.3 | async-start | bytes 3620864 | tf_op jit(solution)/shard_map/reduce_scatter | solution.py:909
  579.8 3.0 collective-permute-start.1
  579.8 2.9 collective-permute-start.2
  582.7 0.6 copy-start.3
  582.7 1.0 copy-start.2
  586.6 51.9 %all-to-all-start.1 = ((bf16[16,160,256]{2,1,0:T(8,128)(2,1)}), bf16[16,160,256]{2,1,0:T(8,128)(2,1)S(1)}, u32[]{:S(2)}, u32[]{:S(2)}) async-start(bf16[16,160,256]{2,1,0:T(8,128)(2,1)} %shard_map.482), calls=%async_computation.1 | async-start | bytes 2621440 | tf_op jit(solution)/shard_map/all_to_all | solution.py:917
  638.5 1.1 copy-start.1
Sparse Core Ops, SparseCore 0:
  21.3 75.4 all-gather.4
  428.4 54.4 all-gather.6
  485.2 83.5 reduce-scatter.1
